TPU v7x, 256 devices: a whole 4x4x8 slice. The times are simulated.
256 devices in a mesh: visit: 16 (over z, core), patch: 16 (over y, x).
Axes of the slice: x: 4, y: 4, z: 8, core: 2. Of those that a mesh axis runs over, the one named last changes fastest.
Arguments:
- images: bfloat16 [16, 4096, 4096], P('visit', 'patch'), may hold values from -6 to 6
- psf_taps: bfloat16 [16, 2, 13], P('visit'), may hold values from 0.019897461 to 0.19921875
- exposure_weights: float32 [16], P('visit'), may hold values from 0.5 to 8
- dest_patch: int32 [16, 32, 32], P('visit', 'patch'), may hold values from -1 to 15, as said below
- dest_cell: int32 [16, 32, 32], P('visit', 'patch'), may hold values from -1 to 63, as said below
- shift_class: int32 [16, 2, 32, 32], P('visit', None, 'patch'), may hold values from 0 to 7
Outputs:
- coadd: float32 [16, 64, 128, 128], P('patch', 'visit')
- weight_map: float32 [16, 64], P('patch', 'visit')
Inputs may be any that keep to these rules, and one draw needn't show every extreme that they name: `dest_patch`: within one exposure all tiles move to sky cells by one whole-cell offset of at most 2 cells along each direction, so distinct tiles land in distinct cells; the patch of cell row u and column w is (u // 8) * 4 + w // 8. Of the 64 tiles in one exposure's band of 256 rows, at most 16 fall in any one patch. `dest_cell`: cell index (u % 8) * 8 + w % 8; -1 exactly where dest_patch is -1.
All inputs are finite; a program needn't handle non-finite values.
Results may differ from a plain program's by a relative error of at most 0.0004.
The roundings to bfloat16 on the way count: a program that leaves them out, or rounds other values in their place, can miss the bound.
Values may be sent and summed in bfloat16 or wider, within the bound.
No kernel may reach another device: no remote copies, remote signals or barrier semaphores. Data moves between devices by JAX's collectives and lax.ppermute only.
A program may use at most 128 MiB of HBM per device.

v0:
```python
import jax
import jax.numpy as jnp
from jax import lax
from jax.sharding import PartitionSpec as P

TILE = 128
KTAPS = 13
SHIFTS = 8
CELLS = 64
CAP = 16


def padded_2(cells, sides, width):
    for axis, dim in sides:
        count = lax.axis_size(axis)
        ends = count - 1
        head = lax.slice_in_dim(cells, 0, width, axis=dim)
        tail = lax.slice_in_dim(cells, cells.shape[dim] - width, cells.shape[dim], axis=dim)
        cells = jnp.concatenate(
            [
                lax.ppermute(tail, axis, [(i, (i + 1) % count) for i in range(ends)]),
                cells,
                lax.ppermute(head, axis, [((i + 1) % count, i) for i in range(ends)]),
            ],
            axis=dim,
        )
    return cells


def passed_along(x, axis, by):
    size = lax.axis_size(axis)
    pairs = [(i, i + by) for i in range(size) if 0 <= i + by < size]
    return lax.ppermute(x, axis, pairs)


def lanczos_table(size, classes):
    out_pos = jnp.arange(size, dtype=jnp.float32)[None, :, None]
    src_pos = jnp.arange(size + 6, dtype=jnp.float32)[None, None, :] - 3.0
    frac = jnp.arange(classes, dtype=jnp.float32)[:, None, None] / classes
    dist = src_pos - out_pos - frac
    kernel = jnp.where(jnp.abs(dist) < 3.0, jnp.sinc(dist) * jnp.sinc(dist / 3.0), 0.0)
    kernel = kernel / jnp.sum(kernel, axis=2, keepdims=True)
    return kernel.astype(jnp.bfloat16)


def column_pass(rows, taps):
    count, height, cols = rows.shape
    reach = KTAPS // 2
    blocks = cols // TILE
    padded = jnp.pad(rows, ((0, 0), (0, 0), (reach, TILE - reach)))
    main = padded[:, :, :cols].reshape(count, height, blocks, TILE)
    tail = padded[:, :, TILE : TILE + cols].reshape(count, height, blocks, TILE)[..., : 2 * reach]
    windows = jnp.concatenate([main, tail], axis=3)
    offset = jnp.arange(TILE + 2 * reach)[:, None] - jnp.arange(TILE)[None, :]
    marks = (offset[None] == jnp.arange(KTAPS)[:, None, None]).astype(jnp.float32)
    toeplitz = jnp.einsum("eb,bji->eji", taps.astype(jnp.float32), marks).astype(jnp.bfloat16)
    result = jnp.einsum("enxj,eji->enxi", windows, toeplitz, preferred_element_type=jnp.float32)
    return result.reshape(count, height, cols).astype(jnp.bfloat16)


def row_pass(colpassed, taps, out_rows):
    offset = jnp.arange(out_rows + KTAPS - 1)[None, :] - jnp.arange(out_rows)[:, None]
    marks = (offset[None] == jnp.arange(KTAPS)[:, None, None]).astype(jnp.float32)
    toeplitz = jnp.einsum("eb,bor->eor", taps.astype(jnp.float32), marks).astype(jnp.bfloat16)
    return jnp.einsum("eor,erc->eoc", toeplitz, colpassed, preferred_element_type=jnp.float32)


def tile_windows(framed):
    count, height, cols = framed.shape
    band = height - 6
    padded = jnp.pad(framed, ((0, 0), (0, TILE - 6), (3, TILE - 3)))
    count_y = band // TILE
    count_x = cols // TILE
    width = cols + TILE
    rmain = padded[:, :band].reshape(count, count_y, TILE, width)
    rtail = padded[:, TILE : TILE + band].reshape(count, count_y, TILE, width)[:, :, :6]
    rowwin = jnp.concatenate([rmain, rtail], axis=2)
    cmain = rowwin[..., :cols].reshape(count, count_y, TILE + 6, count_x, TILE)
    ctail = rowwin[..., TILE : TILE + cols].reshape(count, count_y, TILE + 6, count_x, TILE)[
        ..., :6
    ]
    return jnp.concatenate([cmain, ctail], axis=4)


def pick_table(classes, table):
    marks = (classes[..., None] == jnp.arange(SHIFTS, dtype=classes.dtype)).astype(jnp.bfloat16)
    flat = table.reshape(SHIFTS, -1)
    chosen = jnp.dot(marks.reshape(-1, SHIFTS), flat, preferred_element_type=jnp.float32)
    return chosen.astype(jnp.bfloat16).reshape(classes.shape + table.shape[1:])


def local(images, psf_taps, exposure_weights, dest_patch, dest_cell, shift_class):
    count = images.shape[0]
    band = images.shape[1]
    cols = images.shape[2]
    owners = lax.axis_size("patch")
    table = lanczos_table(TILE, SHIFTS)
    reach = KTAPS // 2
    raw = padded_2(images, (("patch", 1),), reach)
    colpassed = column_pass(raw, psf_taps[:, 1])
    matched = row_pass(colpassed, psf_taps[:, 0], band).astype(jnp.bfloat16)
    framed = padded_2(matched, (("patch", 1),), 3)
    tiles = tile_windows(framed)
    along_cols = pick_table(shift_class[:, 1], table)
    half = jnp.einsum(
        "eyrxj,eyxij->eyxri", tiles, along_cols, preferred_element_type=jnp.float32
    ).astype(jnp.bfloat16)
    count_y = band // TILE
    count_x = cols // TILE
    per_expo = count_y * count_x
    patch_flat = dest_patch.reshape(count, per_expo)
    hits = (patch_flat[..., None] == jnp.arange(owners, dtype=jnp.int32)).astype(jnp.int32)
    rank = jnp.sum(jnp.cumsum(hits, axis=1) * hits, axis=2) - 1
    expo_index = jnp.arange(count, dtype=jnp.int32)[:, None]
    cell_values = dest_cell.reshape(count, per_expo).astype(jnp.float32) + 1.0
    along_rows = pick_table(shift_class[:, 0], table)
    warped = jnp.einsum(
        "eyxor,eyxri->eyxoi", along_rows, half, preferred_element_type=jnp.float32
    ).astype(jnp.bfloat16)
    content = warped.reshape((count * per_expo, TILE, TILE))
    extra = cell_values[..., None]
    width = extra.shape[-1]
    extra = extra.reshape(count * per_expo, width)
    item_shape = content.shape[1:]
    flat_content = content.reshape(count * per_expo, -1)
    cell_numbers = (jnp.arange(CELLS) + 1).astype(jnp.bfloat16)
    state = (jnp.zeros((CELLS, TILE * TILE), jnp.float32), jnp.zeros((CELLS,), jnp.float32))
    position = lax.axis_index("patch")
    span = min(4, owners - 1)
    for offset in range(-span, span + 1):
        slot = jnp.where(
            patch_flat == position + offset, expo_index * CAP + rank, count * CAP
        ).reshape(-1)
        slots = count * CAP
        picks = jnp.arange(slots, dtype=jnp.int32)[:, None] == slot[None, :]
        pack_placed = jnp.dot(
            picks.astype(jnp.bfloat16), flat_content, preferred_element_type=jnp.float32
        )
        pack_buffer = pack_placed.astype(jnp.bfloat16).reshape((slots,) + item_shape)
        pack_labels = jnp.dot(
            picks.astype(jnp.float32), extra, precision=lax.Precision.HIGHEST
        ).astype(jnp.bfloat16)
        buffer = pack_buffer
        labels = pack_labels
        buffer = buffer.reshape((1, count, CAP) + item_shape)
        labels = labels.reshape(1, count, CAP, width)
        if offset != 0:
            buffer, labels = passed_along((buffer, labels), "patch", offset)
        accumulate_total, accumulate_cover = state
        chosen = (cell_numbers[:, None] == labels[:, 0, :, 0]).astype(jnp.bfloat16)
        placed = jnp.dot(
            chosen, buffer[:, 0].reshape(-1, TILE * TILE), preferred_element_type=jnp.float32
        )
        accumulate_total = accumulate_total + exposure_weights[0] * placed
        accumulate_cover = accumulate_cover + exposure_weights[0] * jnp.sum(
            chosen.astype(jnp.float32), axis=1
        )
        state = (accumulate_total, accumulate_cover)
    total, cover = state
    total_sum, cover_sum = (
        lax.psum_scatter(
            total.reshape(1, CELLS, TILE, TILE), "visit", scatter_dimension=1, tiled=True
        ),
        lax.psum_scatter(cover.reshape(1, CELLS), "visit", scatter_dimension=1, tiled=True),
    )
    coadd = total_sum / jnp.maximum(cover_sum, 1.0)[:, :, None, None]
    return (coadd, cover_sum)


def solution(mesh):
    placed = (
        P("visit", "patch", None),
        P("visit", None, None),
        P("visit"),
        P("visit", "patch", None),
        P("visit", "patch", None),
        P("visit", None, "patch", None),
    )
    return jax.shard_map(
        local,
        mesh=mesh,
        in_specs=placed,
        out_specs=(P("patch", "visit", None, None), P("patch", "visit")),
        check_vma=False,
    )
```

profile of v0, /device:TPU:8, one launch (start us, length us, event | category | flops | bytes accessed | tf_op | source)
XLA Modules:
  0.0 290.9 jit_solution(4712974838691603217)
XLA Ops:
  8.1 3.4 %collective-permute-start.1 = (bf16[1,6,4096]{2,1,0:T(8,128)(2,1)S(1)}, bf16[1,6,4096]{2,1,0:T(8,128)(2,1)S(1)}, u32[]{:S(2)}, u32[]{:S(2)}) collective-permute-start(bf16[1,6,4096]{2,1,0:T(8,128)(2,1)S(1)} %get-tuple-element.22), channel_id=1, source_target_pairs={{0,1},{1,2},{2,3},{3,4},{4,5},{5,6},{6,7},{7,8},{8,9},{9,10},{10,1... | collective-permute-start | bytes 147464 | tf_op jit(solution)/shard_map/ppermute | solution.py:21
  11.5 4.6 %collective-permute-start.2 = (bf16[1,6,4096]{2,1,0:T(8,128)(2,1)S(1)}, bf16[1,6,4096]{2,1,0:T(8,128)(2,1)S(1)}, u32[]{:S(2)}, u32[]{:S(2)}) collective-permute-start(bf16[1,6,4096]{2,1,0:T(8,128)(2,1)S(1)} %get-tuple-element.23), channel_id=1, source_target_pairs={{1,0},{2,1},{3,2},{4,3},{5,4},{6,5},{7,6},{8,7},{9,8},{10,9},{11,1... | collective-permute-start | bytes 147464 | tf_op jit(solution)/shard_map/ppermute | solution.py:23
  27.5 3.0 %fusion.162 = f32[8,128]{1,0:T(8,128)S(1)} fusion(f32[8]{0:T(128)S(1)} %iota_multiply_fusion, f32[128,134]{1,0:T(8,128)S(1)} %iota_subtract_fusion.1), kind=kLoop, calls=%fused_computation.194 | loop fusion | flops 9878528 | bytes 72736 | tf_op jit(solution)/shard_map/reduce_sum | solution.py:42
  38.1 3.3 %fusion.36 = bf16[1,268,4224]{2,1,0:T(8,128)(2,1)S(1)} fusion(bf16[1,6,4096]{2,1,0:T(8,128)(2,1)S(1)} %collective-permute-done.2, bf16[1,256,4096]{2,1,0:T(8,128)(2,1)} %param.7, bf16[1,6,4096]{2,1,0:T(8,128)(2,1)S(1)} %collective-permute-done.1), kind=kLoop, calls=%fused_computation.64 | loop fusion | flops 13584384 | bytes 4459520 | tf_op jit(solution)/shard_map/concatenate | solution.py:19
  49.1 2.8 collective-permute-start.3
  51.9 5.2 %collective-permute-start.4 = (bf16[1,3,4096]{2,1,0:T(4,128)(2,1)S(1)}, bf16[1,3,4096]{2,1,0:T(4,128)(2,1)S(1)}, u32[]{:S(2)}, u32[]{:S(2)}) collective-permute-start(bf16[1,3,4096]{2,1,0:T(4,128)(2,1)S(1)} %get-tuple-element.21), channel_id=1, source_target_pairs={{1,0},{2,1},{3,2},{4,3},{5,4},{6,5},{7,6},{8,7},{9,8},{10,9},{11,1... | collective-permute-start | bytes 73736 | tf_op jit(solution)/shard_map/ppermute | solution.py:23
  57.1 13.2 %reshape.545 = bf16[2,32,128,134]{3,2,1,0:T(8,128)(2,1)} reshape(bf16[64,17152]{1,0:T(8,128)(2,1)S(1)} %convolution_convert_fusion.1) | data formatting | bytes 4390912 | tf_op jit(solution)/shard_map/reshape.24
  70.3 14.5 %reshape.556 = bf16[2,32,128,134]{3,2,1,0:T(8,128)(2,1)} reshape(bf16[64,17152]{1,0:T(8,128)(2,1)} %convolution_convert_fusion) | data formatting | bytes 4390912 | tf_op jit(solution)/shard_map/reshape.22
  85.4 8.9 %fusion.24 = bf16[1,384,4224]{2,1,0:T(8,128)(2,1)S(1)} fusion(bf16[1,3,4096]{2,1,0:T(4,128)(2,1)S(1)} %collective-permute-done.4, bf16[1,256,4096]{2,1,0:T(8,128)(2,1)S(1)} %copy-done.2, bf16[1,3,4096]{2,1,0:T(4,128)(2,1)S(1)} %collective-permute-done.3), kind=kLoop, calls=%fused_computation.52 | loop fusion | flops 27574272 | bytes 5390336 | tf_op jit(solution)/shard_map/concatenate | solution.py:19
  96.4 3.4 %reshape.553 = bf16[1,2,134,32,128]{4,3,2,1,0:T(8,128)(2,1)} reshape(bf16[1,2,134,4096]{3,2,1,0:T(8,128)(2,1)} %get-tuple-element.16) | data formatting | bytes 4390912 | tf_op jit(solution)/shard_map/reshape | solution.py:78
  99.8 3.9 %copy.15 = bf16[1,2,134,32,128]{4,2,3,1,0:T(8,128)(2,1)} copy(bf16[1,2,134,32,128]{4,3,2,1,0:T(8,128)(2,1)} %reshape.553) | data formatting | bytes 4390912 | tf_op jit(solution)/shard_map/reshape | solution.py:78
  106.2 3.9 %copy.25 = bf16[1,2,134,32,6]{4,2,3,1,0:T(8,128)(2,1)} copy(bf16[1,2,134,32,6]{4,3,2,1,0:T(8,128)(2,1)} %bitcast.285) | data formatting | bytes 205824
  110.0 7.2 %fusion.57 = bf16[2,32,128,128]{3,2,1,0:T(8,128)(2,1)S(1)} fusion(bf16[2,32,128,134]{3,2,1,0:T(8,128)(2,1)} %reshape.545, bf16[2,32,128,134]{3,2,1,0:T(8,128)(2,1)} %reshape.556, bf16[1,2,134,32,6]{4,2,3,1,0:T(8,128)(2,1)} %copy.25, bf16[1,2,134,32,128]{4,2,3,1,0:T(8,128)(2,1)} %copy.15), kind=kOutput, calls=%fused_computation.90 | convolution fusion | flops 581952512 | bytes 8786432 | tf_op jit(solution)/shard_map/eyxor,eyxri->eyxoi/dot_general | solution.py:117
  136.1 3.7 %fusion.63 = f32[64,16384]{1,0:T(8,128)} fusion(bf16[8,8,128,128]{3,2,1,0:T(8,128)(2,1)S(1)} %bitcast.276, s32[64]{0:T(128)S(1)} %get-tuple-element.30, bf16[64]{0:T(256)(128)(2,1)S(1)} %add_convert_fusion, bf16[16]{0:T(256)(128)(2,1)S(1)} %fusion.99), kind=kOutput, calls=%fused_computation.97 | convolution fusion | flops 67373056 | bytes 6291872 | tf_op jit(solution)/shard_map/dot_general | solution.py:151
  146.5 5.9 %collective-permute-start.16 = (bf16[1,1,16,1]{2,3,1,0:T(2,128)(2,1)S(1)}, bf16[1,1,16,1]{2,3,1,0:T(2,128)(2,1)S(1)}, u32[]{:S(2)}, u32[]{:S(2)}) collective-permute-start(bf16[1,1,16,1]{2,3,1,0:T(2,128)(2,1)S(1)} %fusion.105), channel_id=1, source_target_pairs={{0,3},{1,4},{2,5},{3,6},{4,7},{5,8},{6,9},{7,10},{8,11},{9,12},{10... | collective-permute-start | bytes 104 | tf_op jit(solution)/shard_map/ppermute | solution.py:33
  155.2 3.8 %collective-permute-start.14 = (bf16[1,1,16,1]{2,3,1,0:T(2,128)(2,1)S(1)}, bf16[1,1,16,1]{2,3,1,0:T(2,128)(2,1)S(1)}, u32[]{:S(2)}, u32[]{:S(2)}) collective-permute-start(bf16[1,1,16,1]{2,3,1,0:T(2,128)(2,1)S(1)} %fusion.103), channel_id=1, source_target_pairs={{0,2},{1,3},{2,4},{3,5},{4,6},{5,7},{6,8},{7,9},{8,10},{9,11},{10,... | collective-permute-start | bytes 104 | tf_op jit(solution)/shard_map/ppermute | solution.py:33
  159.2 4.2 %collective-permute-start.18 = (bf16[1,1,16,1]{2,3,1,0:T(2,128)(2,1)S(1)}, bf16[1,1,16,1]{2,3,1,0:T(2,128)(2,1)S(1)}, u32[]{:S(2)}, u32[]{:S(2)}) collective-permute-start(bf16[1,1,16,1]{2,3,1,0:T(2,128)(2,1)S(1)} %fusion.107), channel_id=1, source_target_pairs={{0,4},{1,5},{2,6},{3,7},{4,8},{5,9},{6,10},{7,11},{8,12},{9,13},{1... | collective-permute-start | bytes 104 | tf_op jit(solution)/shard_map/ppermute | solution.py:33
  164.4 9.7 %collective-permute-start.17 = (bf16[1,1,16,128,128]{4,3,2,1,0:T(8,128)(2,1)S(1)}, bf16[1,1,16,128,128]{4,3,2,1,0:T(8,128)(2,1)S(1)}, u32[]{:S(2)}, u32[]{:S(2)}) collective-permute-start(bf16[1,1,16,128,128]{4,3,2,1,0:T(8,128)(2,1)S(1)} %bitcast.300), channel_id=1, source_target_pairs={{0,3},{1,4},{2,5},{3,6},{4,7},{5,8},{6,9},{7,10},{8,11},{9,12},{10... | collective-permute-start | bytes 1572872 | tf_op jit(solution)/shard_map/ppermute | solution.py:33
  174.1 3.1 %collective-permute-start.15 = (bf16[1,1,16,128,128]{4,3,2,1,0:T(8,128)(2,1)S(1)}, bf16[1,1,16,128,128]{4,3,2,1,0:T(8,128)(2,1)S(1)}, u32[]{:S(2)}, u32[]{:S(2)}) collective-permute-start(bf16[1,1,16,128,128]{4,3,2,1,0:T(8,128)(2,1)S(1)} %bitcast.299), channel_id=1, source_target_pairs={{0,2},{1,3},{2,4},{3,5},{4,6},{5,7},{6,8},{7,9},{8,10},{9,11},{10,... | collective-permute-start | bytes 1572872 | tf_op jit(solution)/shard_map/ppermute | solution.py:33
  178.9 6.3 %collective-permute-start.12 = (bf16[1,1,16,1]{2,3,1,0:T(2,128)(2,1)S(1)}, bf16[1,1,16,1]{2,3,1,0:T(2,128)(2,1)S(1)}, u32[]{:S(2)}, u32[]{:S(2)}) collective-permute-start(bf16[1,1,16,1]{2,3,1,0:T(2,128)(2,1)S(1)} %fusion.101), channel_id=1, source_target_pairs={{0,1},{1,2},{2,3},{3,4},{4,5},{5,6},{6,7},{7,8},{8,9},{9,10},{10,1... | collective-permute-start | bytes 104 | tf_op jit(solution)/shard_map/ppermute | solution.py:33
  185.1 9.0 %collective-permute-done.17 = bf16[1,1,16,128,128]{4,3,2,1,0:T(8,128)(2,1)S(1)} collective-permute-done((bf16[1,1,16,128,128]{4,3,2,1,0:T(8,128)(2,1)S(1)}, bf16[1,1,16,128,128]{4,3,2,1,0:T(8,128)(2,1)S(1)}, u32[]{:S(2)}, u32[]{:S(2)}) %collective-permute-start.17) | collective-permute-done | bytes 524320 | tf_op jit(solution)/shard_map/ppermute | solution.py:33
  199.9 12.8 %collective-permute-done.19 = bf16[1,1,16,128,128]{4,3,2,1,0:T(8,128)(2,1)S(1)} collective-permute-done((bf16[1,1,16,128,128]{4,3,2,1,0:T(8,128)(2,1)S(1)}, bf16[1,1,16,128,128]{4,3,2,1,0:T(8,128)(2,1)S(1)}, u32[]{:S(2)}, u32[]{:S(2)}) %collective-permute-start.19) | collective-permute-done | bytes 524320 | tf_op jit(solution)/shard_map/ppermute | solution.py:33
  220.0 26.1 %all-reduce.2 = f32[1,64]{1,0:T(1,128)S(1)} all-reduce(f32[1,64]{1,0:T(1,128)S(1)} %multiply_bitcast_fusion), channel_id=3, replica_groups=mesh['visit'=16,'patch'=16] {'visit'}, use_global_device_ids=true, to_apply=%region_13.15.clone | all-reduce | flops 64 | bytes 512
  246.6 35.4 %reduce-scatter.3.cloned.1.call-done = f32[1,4,128,128]{3,2,1,0:T(8,128)} async-done(((f32[1,64,128,128]{3,2,1,0:T(8,128)}), f32[1,4,128,128]{3,2,1,0:T(8,128)}) %reduce-scatter.3.cloned.1.call-update) | async-done | bytes 262160 | tf_op jit(solution)/shard_map/reduce_scatter | solution.py:161
  (131 shorter events, 77.6 us)
Async XLA Ops:
  7.2 19.0 %copy-start.9 = (bf16[1,2,13]{2,1,0:T(2,128)(2,1)S(1)}, bf16[1,2,13]{2,1,0:T(2,128)(2,1)}, u32[]{:S(2)}) copy-start(bf16[1,2,13]{2,1,0:T(2,128)(2,1)} %param.8) | copy-start | bytes 160
  7.2 274.9 %reduce-scatter.3.cloned.1.call-start = ((), (), s32[]{:S(2)}) async-start(), calls=%async_computation.1 | async-start | bytes 4456448 | tf_op jit(solution)/shard_map/reduce_scatter | solution.py:161
  8.1 29.9 %collective-permute-start.1 = (bf16[1,6,4096]{2,1,0:T(8,128)(2,1)S(1)}, bf16[1,6,4096]{2,1,0:T(8,128)(2,1)S(1)}, u32[]{:S(2)}, u32[]{:S(2)}) collective-permute-start(bf16[1,6,4096]{2,1,0:T(8,128)(2,1)S(1)} %get-tuple-element.22), channel_id=1, source_target_pairs={{0,1},{1,2},{2,3},{3,4},{4,5},{5,6},{6,7},{7,8},{8,9},{9,10},{10,1... | collective-permute-start | bytes 147464 | tf_op jit(solution)/shard_map/ppermute | solution.py:21
  11.5 26.5 %collective-permute-start.2 = (bf16[1,6,4096]{2,1,0:T(8,128)(2,1)S(1)}, bf16[1,6,4096]{2,1,0:T(8,128)(2,1)S(1)}, u32[]{:S(2)}, u32[]{:S(2)}) collective-permute-start(bf16[1,6,4096]{2,1,0:T(8,128)(2,1)S(1)} %get-tuple-element.23), channel_id=1, source_target_pairs={{1,0},{2,1},{3,2},{4,3},{5,4},{6,5},{7,6},{8,7},{9,8},{10,9},{11,1... | collective-permute-start | bytes 147464 | tf_op jit(solution)/shard_map/ppermute | solution.py:23
  18.1 123.1 %collective-permute-start.10 = (bf16[1,1,16,1]{2,3,1,0:T(2,128)(2,1)S(1)}, bf16[1,1,16,1]{2,3,1,0:T(2,128)(2,1)S(1)}, u32[]{:S(2)}, u32[]{:S(2)}) collective-permute-start(bf16[1,1,16,1]{2,3,1,0:T(2,128)(2,1)S(1)} %fusion.98), channel_id=1, source_target_pairs={{1,0},{2,1},{3,2},{4,3},{5,4},{6,5},{7,6},{8,7},{9,8},{10,9},{11,1... | collective-permute-start | bytes 104 | tf_op jit(solution)/shard_map/ppermute | solution.py:33
  20.7 125.8 %collective-permute-start.8 = (bf16[1,1,16,1]{2,3,1,0:T(2,128)(2,1)S(1)}, bf16[1,1,16,1]{2,3,1,0:T(2,128)(2,1)S(1)}, u32[]{:S(2)}, u32[]{:S(2)}) collective-permute-start(bf16[1,1,16,1]{2,3,1,0:T(2,128)(2,1)S(1)} %fusion.96), channel_id=1, source_target_pairs={{2,0},{3,1},{4,2},{5,3},{6,4},{7,5},{8,6},{9,7},{10,8},{11,9},{12,... | collective-permute-start | bytes 104 | tf_op jit(solution)/shard_map/ppermute | solution.py:33
  23.5 131.6 %collective-permute-start.6 = (bf16[1,1,16,1]{2,3,1,0:T(2,128)(2,1)S(1)}, bf16[1,1,16,1]{2,3,1,0:T(2,128)(2,1)S(1)}, u32[]{:S(2)}, u32[]{:S(2)}) collective-permute-start(bf16[1,1,16,1]{2,3,1,0:T(2,128)(2,1)S(1)} %fusion.94), channel_id=1, source_target_pairs={{3,0},{4,1},{5,2},{6,3},{7,4},{8,5},{9,6},{10,7},{11,8},{12,9},{13... | collective-permute-start | bytes 104 | tf_op jit(solution)/shard_map/ppermute | solution.py:33
  49.1 36.3 %collective-permute-start.3 = (bf16[1,3,4096]{2,1,0:T(4,128)(2,1)S(1)}, bf16[1,3,4096]{2,1,0:T(4,128)(2,1)S(1)}, u32[]{:S(2)}, u32[]{:S(2)}) collective-permute-start(bf16[1,3,4096]{2,1,0:T(4,128)(2,1)S(1)} %get-tuple-element.20), channel_id=1, source_target_pairs={{0,1},{1,2},{2,3},{3,4},{4,5},{5,6},{6,7},{7,8},{8,9},{9,10},{10,1... | collective-permute-start | bytes 73736 | tf_op jit(solution)/shard_map/ppermute | solution.py:21
  51.9 33.5 %collective-permute-start.4 = (bf16[1,3,4096]{2,1,0:T(4,128)(2,1)S(1)}, bf16[1,3,4096]{2,1,0:T(4,128)(2,1)S(1)}, u32[]{:S(2)}, u32[]{:S(2)}) collective-permute-start(bf16[1,3,4096]{2,1,0:T(4,128)(2,1)S(1)} %get-tuple-element.21), channel_id=1, source_target_pairs={{1,0},{2,1},{3,2},{4,3},{5,4},{6,5},{7,6},{8,7},{9,8},{10,9},{11,1... | collective-permute-start | bytes 73736 | tf_op jit(solution)/shard_map/ppermute | solution.py:23
  70.3 15.1 %copy-start.2 = (bf16[1,256,4096]{2,1,0:T(8,128)(2,1)S(1)}, bf16[1,256,4096]{2,1,0:T(8,128)(2,1)}, u32[]{:S(2)}) copy-start(bf16[1,256,4096]{2,1,0:T(8,128)(2,1)} %copy-done.1) | copy-start | bytes 6291460
  126.7 17.0 %collective-permute-start.11 = (bf16[1,1,16,128,128]{4,3,2,1,0:T(8,128)(2,1)}, bf16[1,1,16,128,128]{4,3,2,1,0:T(8,128)(2,1)S(1)}, u32[]{:S(2)}, u32[]{:S(2)}) collective-permute-start(bf16[1,1,16,128,128]{4,3,2,1,0:T(8,128)(2,1)} %bitcast.81), channel_id=1, source_target_pairs={{1,0},{2,1},{3,2},{4,3},{5,4},{6,5},{7,6},{8,7},{9,8},{10,9},{11,1... | collective-permute-start | bytes 1572872 | tf_op jit(solution)/shard_map/ppermute | solution.py:33
  129.7 22.6 %collective-permute-start.9 = (bf16[1,1,16,128,128]{4,3,2,1,0:T(8,128)(2,1)}, bf16[1,1,16,128,128]{4,3,2,1,0:T(8,128)(2,1)S(1)}, u32[]{:S(2)}, u32[]{:S(2)}) collective-permute-start(bf16[1,1,16,128,128]{4,3,2,1,0:T(8,128)(2,1)} %bitcast.75), channel_id=1, source_target_pairs={{2,0},{3,1},{4,2},{5,3},{6,4},{7,5},{8,6},{9,7},{10,8},{11,9},{12,... | collective-permute-start | bytes 1572872 | tf_op jit(solution)/shard_map/ppermute | solution.py:33
  141.2 23.1 %collective-permute-start = (bf16[1,1,16,1]{2,3,1,0:T(2,128)(2,1)S(1)}, bf16[1,1,16,1]{2,3,1,0:T(2,128)(2,1)S(1)}, u32[]{:S(2)}, u32[]{:S(2)}) collective-permute-start(bf16[1,1,16,1]{2,3,1,0:T(2,128)(2,1)S(1)} %fusion.92), channel_id=1, source_target_pairs={{4,0},{5,1},{6,2},{7,3},{8,4},{9,5},{10,6},{11,7},{12,8},{13,9},{1... | collective-permute-start | bytes 104 | tf_op jit(solution)/shard_map/ppermute | solution.py:33
  143.7 15.6 %collective-permute-start.7 = (bf16[1,1,16,128,128]{4,3,2,1,0:T(8,128)(2,1)S(1)}, bf16[1,1,16,128,128]{4,3,2,1,0:T(8,128)(2,1)S(1)}, u32[]{:S(2)}, u32[]{:S(2)}) collective-permute-start(bf16[1,1,16,128,128]{4,3,2,1,0:T(8,128)(2,1)S(1)} %bitcast.302), channel_id=1, source_target_pairs={{3,0},{4,1},{5,2},{6,3},{7,4},{8,5},{9,6},{10,7},{11,8},{12,9},{13... | collective-permute-start | bytes 1572872 | tf_op jit(solution)/shard_map/ppermute | solution.py:33
  146.5 32.4 %collective-permute-start.16 = (bf16[1,1,16,1]{2,3,1,0:T(2,128)(2,1)S(1)}, bf16[1,1,16,1]{2,3,1,0:T(2,128)(2,1)S(1)}, u32[]{:S(2)}, u32[]{:S(2)}) collective-permute-start(bf16[1,1,16,1]{2,3,1,0:T(2,128)(2,1)S(1)} %fusion.105), channel_id=1, source_target_pairs={{0,3},{1,4},{2,5},{3,6},{4,7},{5,8},{6,9},{7,10},{8,11},{9,12},{10... | collective-permute-start | bytes 104 | tf_op jit(solution)/shard_map/ppermute | solution.py:33
  152.4 21.7 %collective-permute-start.5 = (bf16[1,1,16,128,128]{4,3,2,1,0:T(8,128)(2,1)S(1)}, bf16[1,1,16,128,128]{4,3,2,1,0:T(8,128)(2,1)S(1)}, u32[]{:S(2)}, u32[]{:S(2)}) collective-permute-start(bf16[1,1,16,128,128]{4,3,2,1,0:T(8,128)(2,1)S(1)} %bitcast.301), channel_id=1, source_target_pairs={{4,0},{5,1},{6,2},{7,3},{8,4},{9,5},{10,6},{11,7},{12,8},{13,9},{1... | collective-permute-start | bytes 1572872 | tf_op jit(solution)/shard_map/ppermute | solution.py:33
  155.2 41.7 %collective-permute-start.14 = (bf16[1,1,16,1]{2,3,1,0:T(2,128)(2,1)S(1)}, bf16[1,1,16,1]{2,3,1,0:T(2,128)(2,1)S(1)}, u32[]{:S(2)}, u32[]{:S(2)}) collective-permute-start(bf16[1,1,16,1]{2,3,1,0:T(2,128)(2,1)S(1)} %fusion.103), channel_id=1, source_target_pairs={{0,2},{1,3},{2,4},{3,5},{4,6},{5,7},{6,8},{7,9},{8,10},{9,11},{10,... | collective-permute-start | bytes 104 | tf_op jit(solution)/shard_map/ppermute | solution.py:33
  159.2 40.6 %collective-permute-start.18 = (bf16[1,1,16,1]{2,3,1,0:T(2,128)(2,1)S(1)}, bf16[1,1,16,1]{2,3,1,0:T(2,128)(2,1)S(1)}, u32[]{:S(2)}, u32[]{:S(2)}) collective-permute-start(bf16[1,1,16,1]{2,3,1,0:T(2,128)(2,1)S(1)} %fusion.107), channel_id=1, source_target_pairs={{0,4},{1,5},{2,6},{3,7},{4,8},{5,9},{6,10},{7,11},{8,12},{9,13},{1... | collective-permute-start | bytes 104 | tf_op jit(solution)/shard_map/ppermute | solution.py:33
  164.4 29.8 %collective-permute-start.17 = (bf16[1,1,16,128,128]{4,3,2,1,0:T(8,128)(2,1)S(1)}, bf16[1,1,16,128,128]{4,3,2,1,0:T(8,128)(2,1)S(1)}, u32[]{:S(2)}, u32[]{:S(2)}) collective-permute-start(bf16[1,1,16,128,128]{4,3,2,1,0:T(8,128)(2,1)S(1)} %bitcast.300), channel_id=1, source_target_pairs={{0,3},{1,4},{2,5},{3,6},{4,7},{5,8},{6,9},{7,10},{8,11},{9,12},{10... | collective-permute-start | bytes 1572872 | tf_op jit(solution)/shard_map/ppermute | solution.py:33
  174.1 25.0 %collective-permute-start.15 = (bf16[1,1,16,128,128]{4,3,2,1,0:T(8,128)(2,1)S(1)}, bf16[1,1,16,128,128]{4,3,2,1,0:T(8,128)(2,1)S(1)}, u32[]{:S(2)}, u32[]{:S(2)}) collective-permute-start(bf16[1,1,16,128,128]{4,3,2,1,0:T(8,128)(2,1)S(1)} %bitcast.299), channel_id=1, source_target_pairs={{0,2},{1,3},{2,4},{3,5},{4,6},{5,7},{6,8},{7,9},{8,10},{9,11},{10,... | collective-permute-start | bytes 1572872 | tf_op jit(solution)/shard_map/ppermute | solution.py:33
  177.2 16.9 %copy-start.3 = (bf16[2,8,128,128]{3,2,1,0:T(8,128)(2,1)S(1)}, bf16[2,8,128,128]{3,2,1,0:T(8,128)(2,1)}, u32[]{:S(2)}) copy-start(bf16[2,8,128,128]{3,2,1,0:T(8,128)(2,1)} %copy.44) | copy-start | bytes 1572868
  178.9 34.6 %collective-permute-start.12 = (bf16[1,1,16,1]{2,3,1,0:T(2,128)(2,1)S(1)}, bf16[1,1,16,1]{2,3,1,0:T(2,128)(2,1)S(1)}, u32[]{:S(2)}, u32[]{:S(2)}) collective-permute-start(bf16[1,1,16,1]{2,3,1,0:T(2,128)(2,1)S(1)} %fusion.101), channel_id=1, source_target_pairs={{0,1},{1,2},{2,3},{3,4},{4,5},{5,6},{6,7},{7,8},{8,9},{9,10},{10,1... | collective-permute-start | bytes 104 | tf_op jit(solution)/shard_map/ppermute | solution.py:33
  194.1 18.5 %collective-permute-start.19 = (bf16[1,1,16,128,128]{4,3,2,1,0:T(8,128)(2,1)S(1)}, bf16[1,1,16,128,128]{4,3,2,1,0:T(8,128)(2,1)S(1)}, u32[]{:S(2)}, u32[]{:S(2)}) collective-permute-start(bf16[1,1,16,128,128]{4,3,2,1,0:T(8,128)(2,1)S(1)} %bitcast.298), channel_id=1, source_target_pairs={{0,4},{1,5},{2,6},{3,7},{4,8},{5,9},{6,10},{7,11},{8,12},{9,13},{1... | collective-permute-start | bytes 1572872 | tf_op jit(solution)/shard_map/ppermute | solution.py:33
  196.9 16.6 %collective-permute-start.13 = (bf16[1,1,16,128,128]{4,3,2,1,0:T(8,128)(2,1)S(1)}, bf16[1,1,16,128,128]{4,3,2,1,0:T(8,128)(2,1)S(1)}, u32[]{:S(2)}, u32[]{:S(2)}) collective-permute-start(bf16[1,1,16,128,128]{4,3,2,1,0:T(8,128)(2,1)S(1)} %bitcast.297), channel_id=1, source_target_pairs={{0,1},{1,2},{2,3},{3,4},{4,5},{5,6},{6,7},{7,8},{8,9},{9,10},{10,1... | collective-permute-start | bytes 1572872 | tf_op jit(solution)/shard_map/ppermute | solution.py:33
  (8 other events, 54.4 us)
Sparse Core Ops, SparseCore 0:
  218.1 63.9 reduce-scatter.2
where the time goes:
time: 294 us; the launch traced here: 291 us
  starting transfers between devices  69.8 us (24%)
  local copies, waits for them, and re-layouts  59.8 us (20%)
  waiting for transfers between devices  58 us (20%)
  matrix products  37 us (13%)
  blocking collectives  26.1 us (9%)
  other arithmetic  23.9 us (8%)
  between operations  16.3 us (6%)
    ppermute x16, starting transfers between devices, passed_along(): return lax.ppermute(x, axis, pairs)  53.9 us
    reduce_scatter x1, waiting for transfers between devices, local(): lax.psum_scatter(total.reshape(1, CELLS, TILE, TILE), 'visit', scatter_di...  35.4 us
    another operation x2, local copies, waits for them, and re-layouts  27.6 us
    unnamed x1, blocking collectives  26.1 us
    ppermute x16, waiting for transfers between devices, passed_along(): return lax.ppermute(x, axis, pairs)  22.6 us
    unnamed x37, local copies, waits for them, and re-layouts  18 us
    concatenate x2, other arithmetic, padded_2(): jnp.concatenate([lax.ppermute(tail, axis, [(i, (i + 1) % count) for i in...  12.2 us
    dot_general x9, matrix products, local(): jnp.dot(chosen, buffer[:, 0].reshape(-1, TILE * TILE), preferred_element_...  12.1 us
  transfers between devices with their start and end apart: 21, of which 5 were waited for; matrix products, arithmetic and copies ran while one was open for 38% of the time, Pallas kernels for 0%

commit v1 on v0

v1 whole, which is shorter than its diff:
```python
import jax
import jax.numpy as jnp
import numpy as np
from jax import lax
from jax.experimental import pallas as pl
from jax.experimental.pallas import tpu as pltpu
from jax.sharding import Mesh, PartitionSpec as P

TILE = 128
KTAPS = 13
SHIFTS = 8
HALO = 16
BAND = 256
COLS = 4096
STACK = BAND + 2 * HALO
BLOCKS = COLS // TILE + 1
FRAME = 144
LEAD = 119
HALF_TILES = 8
PIECE = HALF_TILES * TILE + 32
CELLROW = 4 * TILE + 16
VMEM = 50 * 1024 * 1024
f32 = jnp.float32
bf16 = jnp.bfloat16


def lanczos_tables():
    out_pos = np.arange(TILE)[None, :, None]
    src_pos = np.arange(TILE + 6)[None, None, :] - 3.0
    frac = np.arange(SHIFTS)[:, None, None] / SHIFTS
    dist = src_pos - out_pos - frac
    kernel = np.where(np.abs(dist) < 3.0, np.sinc(dist) * np.sinc(dist / 3.0), 0.0)
    kernel = kernel / np.sum(kernel, axis=2, keepdims=True)
    along_rows = np.zeros((SHIFTS + 1, TILE, FRAME), np.float32)
    along_rows[:SHIFTS, :, : TILE + 6] = kernel
    along_cols = np.zeros((SHIFTS, 2 * TILE, TILE), np.float32)
    along_cols[:, LEAD : LEAD + TILE + 6] = kernel.transpose(0, 2, 1)
    return along_rows.astype(bf16), along_cols.astype(bf16)


def banded(taps_ref, which, shape, diff):
    total = jnp.zeros(shape, f32)
    for k in range(KTAPS):
        total = jnp.where(diff == k, taps_ref[which, k], total)
    return total


def filter_kernel(pos_ref, taps_ref, top_ref, img_ref, bot_ref, out_ref, raw_ref):
    patch = pos_ref[0]
    raw_ref[:, :TILE] = jnp.zeros((STACK, TILE), bf16)
    raw_ref[:, TILE + COLS :] = jnp.zeros((STACK, TILE), bf16)
    raw_ref[:HALO, TILE : TILE + COLS] = top_ref[...]
    raw_ref[HALO : HALO + BAND, TILE : TILE + COLS] = img_ref[...]
    raw_ref[HALO + BAND :, TILE : TILE + COLS] = bot_ref[...]
    shape = (2 * TILE, TILE)
    diff = lax.broadcasted_iota(jnp.int32, shape, 0) - lax.broadcasted_iota(jnp.int32, shape, 1)
    over_cols = banded(taps_ref, 1, shape, diff).astype(bf16)
    shape = (FRAME, FRAME + 16)
    row = lax.broadcasted_iota(jnp.int32, shape, 0)
    base = banded(taps_ref, 0, shape, lax.broadcasted_iota(jnp.int32, shape, 1) - row - 7)
    over_rows = []
    for r in range(2):
        first = jnp.where(patch == 0, 3, 0) if r == 0 else 0
        last = jnp.where(patch == 15, 130, 133) if r == 1 else 133
        over_rows.append(jnp.where((row >= first) & (row <= last), base, 0.0).astype(bf16))

    def step(i, carry):
        start = pl.multiple_of(i * (3 * TILE), TILE)
        passed = [
            jnp.dot(
                raw_ref[:, pl.ds(pl.multiple_of(start + b * TILE, TILE), 2 * TILE)],
                over_cols,
                preferred_element_type=f32,
            ).astype(bf16)
            for b in range(3)
        ]
        passed = jnp.concatenate(passed, axis=1)
        for r in range(2):
            out_ref[r, :, pl.ds(start, 3 * TILE)] = jnp.dot(
                over_rows[r],
                passed[r * TILE : r * TILE + FRAME + 16],
                preferred_element_type=f32,
            ).astype(bf16)
        return carry

    lax.fori_loop(0, BLOCKS // 3, step, 0)
    lane = lax.broadcasted_iota(jnp.int32, (FRAME, TILE), 1)
    for r in range(2):
        edge = out_ref[r, :, :TILE].astype(f32)
        out_ref[r, :, :TILE] = jnp.where(lane >= 122, edge, 0.0).astype(bf16)
        edge = out_ref[r, :, COLS:].astype(f32)
        out_ref[r, :, COLS:] = jnp.where(lane < 122, edge, 0.0).astype(bf16)


def filtered(pos, taps, top, img, bot):
    smem = pl.BlockSpec(memory_space=pltpu.SMEM)
    vmem = pl.BlockSpec(memory_space=pltpu.VMEM)
    return pl.pallas_call(
        filter_kernel,
        out_shape=jax.ShapeDtypeStruct((2, FRAME, BLOCKS * TILE), bf16),
        in_specs=[smem, smem, vmem, vmem, vmem],
        out_specs=vmem,
        scratch_shapes=[pltpu.VMEM((STACK, COLS + 2 * TILE), bf16)],
        compiler_params=pltpu.CompilerParams(vmem_limit_bytes=VMEM),
        name="filter_band",
    )(pos, taps, top, img, bot)


def warp_kernel(hop, pos_ref, shift_ref, class_ref, flag_ref, weight_ref, rows_ref, cols_ref, in_ref, own_ref, sib_ref):
    core = pos_ref[1]
    dest = (pos_ref[2] + hop) % 4
    down = shift_ref[0]
    right = shift_ref[1]
    line = lax.broadcasted_iota(jnp.int32, (32, TILE), 0)
    weight = jnp.full((32, TILE), weight_ref[0], f32)
    high = weight.astype(bf16).astype(f32)
    mid = (weight - high).astype(bf16).astype(f32)
    low = weight - high - mid
    parts = jnp.where(line < 8, high, jnp.where(line < 16, mid, low))
    for side, out_ref in ((0, own_ref), (1, sib_ref)):
        half = core if side == 0 else 1 - core
        marks = jnp.zeros((32, TILE), f32)
        for r in range(2):
            for w in range(4):
                slot = r * 4 + w
                col = dest * 8 + half * 4 + w - right
                inside = (col >= 0) & (col < 32)
                col = jnp.clip(col, 0, 31)
                there = jnp.where(inside, flag_ref[r, col], 0)
                tile = in_ref[r, :, pl.ds(pl.multiple_of(col * TILE, TILE), 2 * TILE)]
                along = jnp.dot(tile, cols_ref[class_ref[1, r, col]], preferred_element_type=f32)
                picked = jnp.where(there > 0, class_ref[0, r, col], SHIFTS)
                out_ref[slot * TILE : (slot + 1) * TILE, :] = jnp.dot(
                    rows_ref[picked], along.astype(bf16), preferred_element_type=f32
                ).astype(bf16)
                marks = jnp.where((line & 7) == slot, there.astype(f32), marks)
        notes = jnp.where(line < 24, marks * parts, down.astype(f32))
        out_ref[HALF_TILES * TILE :, :] = notes.astype(bf16)


def warped(hop, pos, shift, classes, flags, weight, rows, cols, matched):
    smem = pl.BlockSpec(memory_space=pltpu.SMEM)
    vmem = pl.BlockSpec(memory_space=pltpu.VMEM)
    piece = jax.ShapeDtypeStruct((PIECE, TILE), bf16)
    return pl.pallas_call(
        lambda *refs: warp_kernel(hop, *refs),
        out_shape=(piece, piece),
        in_specs=[smem] * 5 + [vmem] * 3,
        out_specs=(vmem, vmem),
        compiler_params=pltpu.CompilerParams(vmem_limit_bytes=VMEM),
        name=f"warp_to_{hop}",
    )(pos, shift, classes, flags, weight, rows, cols, matched)


def place_kernel(pos_ref, *refs):
    pieces = refs[:8]
    main_ref, above_ref, below_ref, rows_ref = refs[8:]
    x = pos_ref[2]
    rows_ref[...] = jnp.zeros(rows_ref.shape, f32)
    for n, piece in enumerate(pieces):
        band = (x + 4 - n % 4) % 4
        notes = piece[HALF_TILES * TILE :, :].astype(f32)
        weights = notes[0:8] + notes[8:16] + notes[16:24]
        down = jnp.max(notes[24:32]).astype(jnp.int32)
        for r in range(2):
            at = 2 * band + r + down + 2
            for w in range(4):
                slot = r * 4 + w
                line = weights[slot : slot + 1]
                tile = piece[slot * TILE : (slot + 1) * TILE, :].astype(f32)
                rows_ref[at, w * TILE : (w + 1) * TILE, :] += line * tile
            rows_ref[at, 4 * TILE : 4 * TILE + 4, :] += weights[r * 4 : r * 4 + 4]
    above_ref[...] = rows_ref[0:2]
    main_ref[...] = rows_ref[2:10]
    below_ref[...] = rows_ref[10:12]


def placed_rows(pos, pieces):
    smem = pl.BlockSpec(memory_space=pltpu.SMEM)
    vmem = pl.BlockSpec(memory_space=pltpu.VMEM)

    def rows(n):
        return jax.ShapeDtypeStruct((n, CELLROW, TILE), f32)

    return pl.pallas_call(
        place_kernel,
        out_shape=(rows(8), rows(2), rows(2)),
        in_specs=[smem] + [vmem] * 8,
        out_specs=(vmem,) * 3,
        scratch_shapes=[pltpu.VMEM((12, CELLROW, TILE), f32)],
        compiler_params=pltpu.CompilerParams(vmem_limit_bytes=VMEM),
        name="place_rows",
    )(pos, *pieces)


def local(images, psf_taps, exposure_weights, dest_patch, dest_cell, shift_class):
    z, core, y, x = (lax.axis_index(a) for a in ("z", "core", "y", "x"))
    patch = y * 4 + x
    img = images[0]
    line = [(i, i + 1) for i in range(15)]
    top = lax.ppermute(img[BAND - HALO :], ("y", "x"), line)
    bot = lax.ppermute(img[:HALO], ("y", "x"), [(j, i) for i, j in line])
    pos = jnp.stack([patch, core, x]).astype(jnp.int32)
    owner = dest_patch[0]
    cell = dest_cell[0]
    flags = (owner >= 0).astype(jnp.int32)
    across = (owner & 3) * 8 + (cell & 7) - jnp.arange(32, dtype=jnp.int32)[None, :]
    along = (owner >> 2) * 8 + (cell >> 3) - jnp.arange(2, dtype=jnp.int32)[:, None] - 2 * patch
    shift = jnp.stack([jnp.max(jnp.where(flags > 0, s, -3)) for s in (along, across)])
    shift = jnp.where(shift > -3, shift, 0).astype(jnp.int32)
    rows, cols = lanczos_tables()
    matched = filtered(pos, psf_taps[0].astype(f32), top, img, bot)
    own = [None] * 4
    sib = [None] * 4
    for hop in (2, 1, 3, 0):
        stay, leave = warped(
            hop, pos, shift, shift_class[0], flags, exposure_weights, jnp.asarray(rows), jnp.asarray(cols), matched
        )
        if hop:
            own[hop] = lax.ppermute(stay, "x", [(i, (i + hop) % 4) for i in range(4)])
        else:
            own[hop] = stay
        sib[hop] = lax.ppermute(
            leave, ("core", "x"), [(c * 4 + i, (1 - c) * 4 + (i + hop) % 4) for c in range(2) for i in range(4)]
        )
    main, above, below = placed_rows(pos, own + sib)
    from_above = lax.ppermute(below, "y", [(i, i + 1) for i in range(3)])
    from_below = lax.ppermute(above, "y", [(i + 1, i) for i in range(3)])
    main = main.at[0:2].add(from_above).at[6:8].add(from_below)

    def block(i):
        return lax.dynamic_index_in_dim(main, (i + 16) % 8, 0, keepdims=False)

    up = block(z + 4)
    dn = block(z - 3)
    for s in range(4):
        up = lax.ppermute(up, "z", [(i, (i + 1) % 8) for i in range(8)])
        if s < 3:
            up = up + block(z + 3 - s)
            dn = lax.ppermute(dn, "z", [((i + 1) % 8, i) for i in range(8)])
            if s < 2:
                dn = dn + block(z - 2 + s)
    total = up + dn + block(z)
    cover = total[4 * TILE : 4 * TILE + 4, 0]
    coadd = total[: 4 * TILE].reshape(1, 4, TILE, TILE) / jnp.maximum(cover, 1.0)[None, :, None, None]
    return coadd, cover[None]


def solution(mesh):
    split = Mesh(mesh.devices.reshape(8, 2, 4, 4), ("z", "core", "y", "x"))
    visit = ("z", "core")
    patch = ("y", "x")
    placed = (
        P(visit, patch, None),
        P(visit, None, None),
        P(visit),
        P(visit, patch, None),
        P(visit, patch, None),
        P(visit, None, patch, None),
    )
    return jax.shard_map(
        local,
        mesh=split,
        in_specs=placed,
        out_specs=(P(patch, visit, None, None), P(patch, visit)),
        check_vma=False,
    )
```

time: 294 us -> 131 us (0.45)
  local copies, waits for them, and re-layouts: 59.8 us -> 5.36 us
  matrix products: 37 us -> 0 us
  starting transfers between devices: 69.8 us -> 35.4 us
  blocking collectives: 26.1 us -> 0 us
  Pallas kernels: 0 us -> 25.4 us
  between operations: 16.3 us -> 1.53 us
  other arithmetic: 23.9 us -> 13.6 us
  waiting for transfers between devices: 58 us -> 48.8 us
    dot_general x33 -> x0, matrix products: 37 us -> none  [the longest x9 12.1 us: local(): jnp.dot(chosen, buffer[:, 0].reshape(-1, TILE * TILE), preferred_element_...]
    reduce_scatter x1 -> x0, waiting for transfers between devices: 35.4 us -> none  [local(): lax.psum_scatter(total.reshape(1, CELLS, TILE, TILE), 'visit', scatter_di...]
    ppermute x20 -> x18, starting transfers between devices: 69.8 us -> 35.4 us  [the longest x3 10.6 us: local(): dn = lax.ppermute(dn, 'z', [((i + 1) % 8, i) for i in range(8)])]
    another operation x2 -> x0, local copies, waits for them, and re-layouts: 27.6 us -> none
    ppermute x20 -> x18, waiting for transfers between devices: 22.6 us -> 48.8 us  [the longest x4 25.3 us: local(): up = lax.ppermute(up, 'z', [(i, (i + 1) % 8) for i in range(8)])]
    unnamed x1 -> x0, blocking collectives: 26.1 us -> none
    pallas_call x0 -> x6, Pallas kernels: none -> 25.4 us  [the longest x4 15 us: warped(): pl.pallas_call(lambda *refs: warp_kernel(hop, *refs), out_shape=(piece, p...]
    unnamed x37 -> x10, local copies, waits for them, and re-layouts: 18 us -> 3.28 us
  transfers between devices with their start and end apart: 21 -> 18, of which waited for: 5 -> 9; matrix products, arithmetic and copies ran while one was open for 38% -> 5% of each run, Pallas kernels for 0% -> 9%
where the time goes in v1:
time: 131 us; the launch traced here: 130 us
  waiting for transfers between devices  48.8 us (37%)
  starting transfers between devices  35.4 us (27%)
  Pallas kernels  25.4 us (19%)
  other arithmetic  13.6 us (10%)
  local copies, waits for them, and re-layouts  5.36 us (4%)
  between operations  1.53 us (1%)
    ppermute x4, waiting for transfers between devices, local(): up = lax.ppermute(up, 'z', [(i, (i + 1) % 8) for i in range(8)])  25.3 us
    pallas_call x4, Pallas kernels, warped(): pl.pallas_call(lambda *refs: warp_kernel(hop, *refs), out_shape=(piece, p...  15 us
    ppermute x3, starting transfers between devices, local(): dn = lax.ppermute(dn, 'z', [((i + 1) % 8, i) for i in range(8)])  10.6 us
    ppermute x1, waiting for transfers between devices, local(): from_above = lax.ppermute(below, 'y', [(i, i + 1) for i in range(3)])  10.5 us
    pallas_call x1, Pallas kernels, filtered(): pl.pallas_call(filter_kernel, out_shape=jax.ShapeDtypeStruct((2, FRAME, B...  7.37 us
    ppermute x4, waiting for transfers between devices, local(): lax.ppermute(leave, ('core', 'x'), [(c * 4 + i, (1 - c) * 4 + (i + hop) %...  6.53 us
    ppermute x4, starting transfers between devices, local(): lax.ppermute(leave, ('core', 'x'), [(c * 4 + i, (1 - c) * 4 + (i + hop) %...  4.83 us
    ppermute x3, waiting for transfers between devices, local(): own[hop] = lax.ppermute(stay, 'x', [(i, (i + hop) % 4) for i in range(4)])  4.57 us
  transfers between devices with their start and end apart: 18, of which 9 were waited for; matrix products, arithmetic and copies ran while one was open for 5% of the time, Pallas kernels for 9%

profile of v1, /device:TPU:8, one launch (start us, length us, event | category | flops | bytes accessed | tf_op | source)
XLA Modules:
  0.0 130.1 jit_solution(11724338745798977226)
XLA Ops:
  1.6 3.4 %collective-permute-start = (bf16[16,4096]{1,0:T(8,128)(2,1)S(1)}, bf16[16,4096]{1,0:T(8,128)(2,1)S(1)}, u32[]{:S(2)}, u32[]{:S(2)}) collective-permute-start(bf16[16,4096]{1,0:T(8,128)(2,1)S(1)} %get-tuple-element.59), channel_id=1, source_target_pairs={{0,1},{1,2},{2,3},{3,4},{4,5},{5,6},{6,7},{7,8},{8,9},{9,10},{10,1... | collective-permute-start | bytes 393224 | tf_op jit(solution)/shard_map/ppermute | solution.py:201
  5.0 4.6 %collective-permute-start.1 = (bf16[16,4096]{1,0:T(8,128)(2,1)S(1)}, bf16[16,4096]{1,0:T(8,128)(2,1)S(1)}, u32[]{:S(2)}, u32[]{:S(2)}) collective-permute-start(bf16[16,4096]{1,0:T(8,128)(2,1)S(1)} %get-tuple-element.58), channel_id=1, source_target_pairs={{1,0},{2,1},{3,2},{4,3},{5,4},{6,5},{7,6},{8,7},{9,8},{10,9},{11,1... | collective-permute-start | bytes 393224 | tf_op jit(solution)/shard_map/ppermute | solution.py:202
  16.0 7.4 %filter_band.1.refs_7_ = bf16[2,144,4224]{2,1,0:T(8,128)(2,1)} custom-call(s32[3]{0:T(128)S(1)} %pad_add_fusion.pos_ref.refs_0_, f32[2,13]{1,0:T(2,128)S(1)} %bitcast_convert_fusion.taps_ref, bf16[16,4096]{1,0:T(8,128)(2,1)S(1)} %collective-permute-done.top_ref, bf16[256,4096]{1,0:T(8,128)(2,1)S(1)} %bitcast.52, ...), custom_call_target="tpu_custom_call" | custom-call | tf_op jit(solution)/shard_map/filter_band/pallas_call | solution.py:98
  25.1 3.7 %warp_to_1.1 = (bf16[1056,128]{1,0:T(8,128)(2,1)S(1)}, bf16[1056,128]{1,0:T(8,128)(2,1)S(1)}) custom-call(s32[3]{0:T(128)S(1)} %pad_add_fusion.pos_ref.refs_0_, s32[2]{0:T(128)S(1)} %compare_select_fusion.refs_1_, s32[2,2,32]{2,1,0:T(2,128)S(1)} %bitcast.53, s32[2,32]{1,0:T(2,128)S(1)} %fusion.1.refs_3_, f32[1]{0:T(128)S(6)} %copy.13.refs_4_, ...), custom_call_target="tpu_custom_call" | custom-call | tf_op jit(solution)/shard_map/warp_to_1/pallas_call | solution.py:145
  28.9 3.7 %warp_to_2.1 = (bf16[1056,128]{1,0:T(8,128)(2,1)S(1)}, bf16[1056,128]{1,0:T(8,128)(2,1)S(1)}) custom-call(s32[3]{0:T(128)S(1)} %pad_add_fusion.pos_ref.refs_0_, s32[2]{0:T(128)S(1)} %compare_select_fusion.refs_1_, s32[2,2,32]{2,1,0:T(2,128)S(1)} %bitcast.54, s32[2,32]{1,0:T(2,128)S(1)} %fusion.1.refs_3_, f32[1]{0:T(128)S(6)} %copy.13.refs_4_, ...), custom_call_target="tpu_custom_call" | custom-call | tf_op jit(solution)/shard_map/warp_to_2/pallas_call | solution.py:145
  32.7 3.9 %collective-permute-start.3 = (bf16[1056,128]{1,0:T(8,128)(2,1)S(1)}, bf16[1056,128]{1,0:T(8,128)(2,1)S(1)}, u32[]{:S(2)}, u32[]{:S(2)}) collective-permute-start(bf16[1056,128]{1,0:T(8,128)(2,1)S(1)} %get-tuple-element.39), channel_id=1, source_target_pairs={{0,2},{1,3},{2,0},{3,1},{4,6},{5,7},{6,4},{7,5},{8,10},{9,11},{10,... | collective-permute-start | bytes 811016 | tf_op jit(solution)/shard_map/ppermute | solution.py:220
  36.5 3.7 %warp_to_3.1 = (bf16[1056,128]{1,0:T(8,128)(2,1)S(1)}, bf16[1056,128]{1,0:T(8,128)(2,1)S(1)}) custom-call(s32[3]{0:T(128)S(1)} %pad_add_fusion.pos_ref.refs_0_, s32[2]{0:T(128)S(1)} %compare_select_fusion.refs_1_, s32[2,2,32]{2,1,0:T(2,128)S(1)} %bitcast.55, s32[2,32]{1,0:T(2,128)S(1)} %fusion.1.refs_3_, f32[1]{0:T(128)S(6)} %copy.13.refs_4_, ...), custom_call_target="tpu_custom_call" | custom-call | tf_op jit(solution)/shard_map/warp_to_3/pallas_call | solution.py:145
  40.3 3.7 %warp_to_0.1 = (bf16[1056,128]{1,0:T(8,128)(2,1)S(1)}, bf16[1056,128]{1,0:T(8,128)(2,1)S(1)}) custom-call(s32[3]{0:T(128)S(1)} %pad_add_fusion.pos_ref.refs_0_, s32[2]{0:T(128)S(1)} %compare_select_fusion.refs_1_, s32[2,2,32]{2,1,0:T(2,128)S(1)} %bitcast.56, s32[2,32]{1,0:T(2,128)S(1)} %fusion.1.refs_3_, f32[1]{0:T(128)S(6)} %copy.13.refs_4_, ...), custom_call_target="tpu_custom_call" | custom-call | tf_op jit(solution)/shard_map/warp_to_0/pallas_call | solution.py:145
  45.9 2.7 %collective-permute-start.8 = (bf16[1056,128]{1,0:T(8,128)(2,1)S(1)}, bf16[1056,128]{1,0:T(8,128)(2,1)S(1)}, u32[]{:S(2)}, u32[]{:S(2)}) collective-permute-start(bf16[1056,128]{1,0:T(8,128)(2,1)S(1)} %get-tuple-element.44), channel_id=1, source_target_pairs={{0,19},{1,16},{2,17},{3,18},{16,3},{17,0},{18,1},{19,2},{4,23},{5,... | collective-permute-start | bytes 811016 | tf_op jit(solution)/shard_map/ppermute | solution.py:223
  49.0 4.6 %collective-permute-done.4.refs_3_ = bf16[1056,128]{1,0:T(8,128)(2,1)S(1)} collective-permute-done((bf16[1056,128]{1,0:T(8,128)(2,1)S(1)}, bf16[1056,128]{1,0:T(8,128)(2,1)S(1)}, u32[]{:S(2)}, u32[]{:S(2)}) %collective-permute-start.4) | collective-permute-done | bytes 270368 | tf_op jit(solution)/shard_map/ppermute | solution.py:220
  53.6 4.3 %collective-permute-done.7.refs_6_ = bf16[1056,128]{1,0:T(8,128)(2,1)S(1)} collective-permute-done((bf16[1056,128]{1,0:T(8,128)(2,1)S(1)}, bf16[1056,128]{1,0:T(8,128)(2,1)S(1)}, u32[]{:S(2)}, u32[]{:S(2)}) %collective-permute-start.7) | collective-permute-done | bytes 270368 | tf_op jit(solution)/shard_map/ppermute | solution.py:223
  57.8 2.2 %collective-permute-done.8.refs_7_ = bf16[1056,128]{1,0:T(8,128)(2,1)S(1)} collective-permute-done((bf16[1056,128]{1,0:T(8,128)(2,1)S(1)}, bf16[1056,128]{1,0:T(8,128)(2,1)S(1)}, u32[]{:S(2)}, u32[]{:S(2)}) %collective-permute-start.8) | collective-permute-done | bytes 270368 | tf_op jit(solution)/shard_map/ppermute | solution.py:223
  60.1 3.0 %place_rows.1 = (f32[8,528,128]{2,1,0:T(8,128)}, f32[2,528,128]{2,1,0:T(8,128)S(1)}, f32[2,528,128]{2,1,0:T(8,128)S(1)}) custom-call(s32[3]{0:T(128)S(1)} %pad_add_fusion.pos_ref.refs_0_, bf16[1056,128]{1,0:T(8,128)(2,1)S(1)} %get-tuple-element.37.refs_0_, bf16[1056,128]{1,0:T(8,128)(2,1)S(1)} %collective-permute-done.2.refs_1_, ...), custom_call_target="tpu_custom_call" | custom-call | tf_op jit(solution)/shard_map/place_rows/pallas_call | solution.py:185
  63.1 3.5 %collective-permute-start.9 = (f32[2,528,128]{2,1,0:T(8,128)S(1)}, f32[2,528,128]{2,1,0:T(8,128)S(1)}, u32[]{:S(2)}, u32[]{:S(2)}) collective-permute-start(f32[2,528,128]{2,1,0:T(8,128)S(1)} %get-tuple-element.46), channel_id=1, source_target_pairs={{0,4},{4,8},{8,12},{1,5},{5,9},{9,13},{2,6},{6,10},{10,14},{3,7},{... | collective-permute-start | bytes 1622024 | tf_op jit(solution)/shard_map/ppermute | solution.py:227
  66.6 2.4 %collective-permute-start.10 = (f32[2,528,128]{2,1,0:T(8,128)S(1)}, f32[2,528,128]{2,1,0:T(8,128)S(1)}, u32[]{:S(2)}, u32[]{:S(2)}) collective-permute-start(f32[2,528,128]{2,1,0:T(8,128)S(1)} %get-tuple-element.47), channel_id=1, source_target_pairs={{4,0},{8,4},{12,8},{5,1},{9,5},{13,9},{6,2},{10,6},{14,10},{7,3},{... | collective-permute-start | bytes 1622024 | tf_op jit(solution)/shard_map/ppermute | solution.py:228
  69.0 10.5 %collective-permute-done.9 = f32[2,528,128]{2,1,0:T(8,128)S(1)} collective-permute-done((f32[2,528,128]{2,1,0:T(8,128)S(1)}, f32[2,528,128]{2,1,0:T(8,128)S(1)}, u32[]{:S(2)}, u32[]{:S(2)}) %collective-permute-start.9) | collective-permute-done | bytes 540704 | tf_op jit(solution)/shard_map/ppermute | solution.py:227
  81.4 2.0 %collective-permute-done.10 = f32[2,528,128]{2,1,0:T(8,128)S(1)} collective-permute-done((f32[2,528,128]{2,1,0:T(8,128)S(1)}, f32[2,528,128]{2,1,0:T(8,128)S(1)}, u32[]{:S(2)}, u32[]{:S(2)}) %collective-permute-start.10) | collective-permute-done | bytes 540704 | tf_op jit(solution)/shard_map/ppermute | solution.py:228
  88.3 4.1 %collective-permute-start.15 = (f32[528,128]{1,0:T(8,128)S(1)}, f32[528,128]{1,0:T(8,128)S(1)}, u32[]{:S(2)}, u32[]{:S(2)}) collective-permute-start(f32[528,128]{1,0:T(8,128)S(1)} %get-tuple-element.56), channel_id=1, source_target_pairs={{32,0},{64,32},{96,64},{128,96},{160,128},{192,160},{224,192},{0,2... | collective-permute-start | bytes 811016 | tf_op jit(solution)/shard_map/ppermute | solution.py:240
  92.4 6.7 %collective-permute-done.11 = f32[528,128]{1,0:T(8,128)S(1)} collective-permute-done((f32[528,128]{1,0:T(8,128)S(1)}, f32[528,128]{1,0:T(8,128)S(1)}, u32[]{:S(2)}, u32[]{:S(2)}) %collective-permute-start.11) | collective-permute-done | bytes 270368 | tf_op jit(solution)/shard_map/ppermute | solution.py:237
  100.1 9.1 %collective-permute-done.12 = f32[528,128]{1,0:T(8,128)S(1)} collective-permute-done((f32[528,128]{1,0:T(8,128)S(1)}, f32[528,128]{1,0:T(8,128)S(1)}, u32[]{:S(2)}, u32[]{:S(2)}) %collective-permute-start.12) | collective-permute-done | bytes 270368 | tf_op jit(solution)/shard_map/ppermute | solution.py:237
  110.5 3.2 %collective-permute-start.16 = (f32[528,128]{1,0:T(8,128)S(1)}, f32[528,128]{1,0:T(8,128)S(1)}, u32[]{:S(2)}, u32[]{:S(2)}) collective-permute-start(f32[528,128]{1,0:T(8,128)S(1)} %get-tuple-element.54), channel_id=1, source_target_pairs={{32,0},{64,32},{96,64},{128,96},{160,128},{192,160},{224,192},{0,2... | collective-permute-start | bytes 811016 | tf_op jit(solution)/shard_map/ppermute | solution.py:240
  113.7 5.1 %collective-permute-done.13 = f32[528,128]{1,0:T(8,128)S(1)} collective-permute-done((f32[528,128]{1,0:T(8,128)S(1)}, f32[528,128]{1,0:T(8,128)S(1)}, u32[]{:S(2)}, u32[]{:S(2)}) %collective-permute-start.13) | collective-permute-done | bytes 270368 | tf_op jit(solution)/shard_map/ppermute | solution.py:237
  120.0 3.2 %collective-permute-start.17 = (f32[528,128]{1,0:T(8,128)S(1)}, f32[528,128]{1,0:T(8,128)S(1)}, u32[]{:S(2)}, u32[]{:S(2)}) collective-permute-start(f32[528,128]{1,0:T(8,128)S(1)} %get-tuple-element.52), channel_id=1, source_target_pairs={{32,0},{64,32},{96,64},{128,96},{160,128},{192,160},{224,192},{0,2... | collective-permute-start | bytes 811016 | tf_op jit(solution)/shard_map/ppermute | solution.py:240
  123.2 4.4 %collective-permute-done.14 = f32[528,128]{1,0:T(8,128)S(1)} collective-permute-done((f32[528,128]{1,0:T(8,128)S(1)}, f32[528,128]{1,0:T(8,128)S(1)}, u32[]{:S(2)}, u32[]{:S(2)}) %collective-permute-start.14) | collective-permute-done | bytes 270368 | tf_op jit(solution)/shard_map/ppermute | solution.py:237
  (44 shorter events, 23.5 us)
Async XLA Ops:
  1.6 12.8 %collective-permute-start = (bf16[16,4096]{1,0:T(8,128)(2,1)S(1)}, bf16[16,4096]{1,0:T(8,128)(2,1)S(1)}, u32[]{:S(2)}, u32[]{:S(2)}) collective-permute-start(bf16[16,4096]{1,0:T(8,128)(2,1)S(1)} %get-tuple-element.59), channel_id=1, source_target_pairs={{0,1},{1,2},{2,3},{3,4},{4,5},{5,6},{6,7},{7,8},{8,9},{9,10},{10,1... | collective-permute-start | bytes 393224 | tf_op jit(solution)/shard_map/ppermute | solution.py:201
  5.0 9.4 %collective-permute-start.1 = (bf16[16,4096]{1,0:T(8,128)(2,1)S(1)}, bf16[16,4096]{1,0:T(8,128)(2,1)S(1)}, u32[]{:S(2)}, u32[]{:S(2)}) collective-permute-start(bf16[16,4096]{1,0:T(8,128)(2,1)S(1)} %get-tuple-element.58), channel_id=1, source_target_pairs={{1,0},{2,1},{3,2},{4,3},{5,4},{6,5},{7,6},{8,7},{9,8},{10,9},{11,1... | collective-permute-start | bytes 393224 | tf_op jit(solution)/shard_map/ppermute | solution.py:202
  14.4 1.6 %copy-start.3 = (bf16[1,256,4096]{2,1,0:T(8,128)(2,1)S(1)}, bf16[1,256,4096]{2,1,0:T(8,128)(2,1)}, u32[]{:S(2)}) copy-start(bf16[1,256,4096]{2,1,0:T(8,128)(2,1)} %param.12) | copy-start | bytes 6291460
  16.0 7.4 %copy-start.1 = (bf16[9,128,144]{2,1,0:T(8,128)(2,1)S(1)}, bf16[9,128,144]{2,1,0:T(8,128)(2,1)}, u32[]{:S(2)}) copy-start(bf16[9,128,144]{2,1,0:T(8,128)(2,1)} %constant.179.clone.refs_5_) | copy-start | bytes 995332
  16.0 7.4 %copy-start.2 = (bf16[8,256,128]{2,1,0:T(8,128)(2,1)S(1)}, bf16[8,256,128]{2,1,0:T(8,128)(2,1)}, u32[]{:S(2)}) copy-start(bf16[8,256,128]{2,1,0:T(8,128)(2,1)} %constant.180.clone.refs_6_) | copy-start | bytes 1572868
  16.0 7.4 %copy-start.4 = (s32[1,2,2,32]{3,2,1,0:T(2,128)S(1)}, s32[1,2,2,32]{3,2,1,0:T(2,128)}, u32[]{:S(2)}) copy-start(s32[1,2,2,32]{3,2,1,0:T(2,128)} %param.17) | copy-start | bytes 1540
  23.4 1.7 %copy-start = (bf16[2,144,4224]{2,1,0:T(8,128)(2,1)S(1)}, bf16[2,144,4224]{2,1,0:T(8,128)(2,1)}, u32[]{:S(2)}) copy-start(bf16[2,144,4224]{2,1,0:T(8,128)(2,1)} %filter_band.1.refs_7_) | copy-start | bytes 7299076
  28.8 17.1 %collective-permute-start.2 = (bf16[1056,128]{1,0:T(8,128)(2,1)S(1)}, bf16[1056,128]{1,0:T(8,128)(2,1)S(1)}, u32[]{:S(2)}, u32[]{:S(2)}) collective-permute-start(bf16[1056,128]{1,0:T(8,128)(2,1)S(1)} %get-tuple-element.38), channel_id=1, source_target_pairs={{0,1},{1,2},{2,3},{3,0},{4,5},{5,6},{6,7},{7,4},{8,9},{9,10},{10,1... | collective-permute-start | bytes 811016 | tf_op jit(solution)/shard_map/ppermute | solution.py:220
  32.7 15.9 %collective-permute-start.3 = (bf16[1056,128]{1,0:T(8,128)(2,1)S(1)}, bf16[1056,128]{1,0:T(8,128)(2,1)S(1)}, u32[]{:S(2)}, u32[]{:S(2)}) collective-permute-start(bf16[1056,128]{1,0:T(8,128)(2,1)S(1)} %get-tuple-element.39), channel_id=1, source_target_pairs={{0,2},{1,3},{2,0},{3,1},{4,6},{5,7},{6,4},{7,5},{8,10},{9,11},{10,... | collective-permute-start | bytes 811016 | tf_op jit(solution)/shard_map/ppermute | solution.py:220
  44.0 9.5 %collective-permute-start.4 = (bf16[1056,128]{1,0:T(8,128)(2,1)S(1)}, bf16[1056,128]{1,0:T(8,128)(2,1)S(1)}, u32[]{:S(2)}, u32[]{:S(2)}) collective-permute-start(bf16[1056,128]{1,0:T(8,128)(2,1)S(1)} %get-tuple-element.40), channel_id=1, source_target_pairs={{0,3},{1,0},{2,1},{3,2},{4,7},{5,4},{6,5},{7,6},{8,11},{9,8},{10,9... | collective-permute-start | bytes 811016 | tf_op jit(solution)/shard_map/ppermute | solution.py:220
  44.1 9.4 %collective-permute-start.6 = (bf16[1056,128]{1,0:T(8,128)(2,1)S(1)}, bf16[1056,128]{1,0:T(8,128)(2,1)S(1)}, u32[]{:S(2)}, u32[]{:S(2)}) collective-permute-start(bf16[1056,128]{1,0:T(8,128)(2,1)S(1)} %get-tuple-element.42), channel_id=1, source_target_pairs={{0,17},{1,18},{2,19},{3,16},{16,1},{17,2},{18,3},{19,0},{4,21},{5,... | collective-permute-start | bytes 811016 | tf_op jit(solution)/shard_map/ppermute | solution.py:223
  44.2 13.6 %collective-permute-start.7 = (bf16[1056,128]{1,0:T(8,128)(2,1)S(1)}, bf16[1056,128]{1,0:T(8,128)(2,1)S(1)}, u32[]{:S(2)}, u32[]{:S(2)}) collective-permute-start(bf16[1056,128]{1,0:T(8,128)(2,1)S(1)} %get-tuple-element.43), channel_id=1, source_target_pairs={{0,18},{1,19},{2,16},{3,17},{16,2},{17,3},{18,0},{19,1},{4,22},{5,... | collective-permute-start | bytes 811016 | tf_op jit(solution)/shard_map/ppermute | solution.py:223
  45.9 14.2 %collective-permute-start.8 = (bf16[1056,128]{1,0:T(8,128)(2,1)S(1)}, bf16[1056,128]{1,0:T(8,128)(2,1)S(1)}, u32[]{:S(2)}, u32[]{:S(2)}) collective-permute-start(bf16[1056,128]{1,0:T(8,128)(2,1)S(1)} %get-tuple-element.44), channel_id=1, source_target_pairs={{0,19},{1,16},{2,17},{3,18},{16,3},{17,0},{18,1},{19,2},{4,23},{5,... | collective-permute-start | bytes 811016 | tf_op jit(solution)/shard_map/ppermute | solution.py:223
  48.6 11.5 %collective-permute-start.5 = (bf16[1056,128]{1,0:T(8,128)(2,1)S(1)}, bf16[1056,128]{1,0:T(8,128)(2,1)S(1)}, u32[]{:S(2)}, u32[]{:S(2)}) collective-permute-start(bf16[1056,128]{1,0:T(8,128)(2,1)S(1)} %get-tuple-element.41), channel_id=1, source_target_pairs={{0,16},{1,17},{2,18},{3,19},{16,0},{17,1},{18,2},{19,3},{4,20},{5,... | collective-permute-start | bytes 811016 | tf_op jit(solution)/shard_map/ppermute | solution.py:223
  63.1 16.4 %collective-permute-start.9 = (f32[2,528,128]{2,1,0:T(8,128)S(1)}, f32[2,528,128]{2,1,0:T(8,128)S(1)}, u32[]{:S(2)}, u32[]{:S(2)}) collective-permute-start(f32[2,528,128]{2,1,0:T(8,128)S(1)} %get-tuple-element.46), channel_id=1, source_target_pairs={{0,4},{4,8},{8,12},{1,5},{5,9},{9,13},{2,6},{6,10},{10,14},{3,7},{... | collective-permute-start | bytes 1622024 | tf_op jit(solution)/shard_map/ppermute | solution.py:227
  66.6 16.8 %collective-permute-start.10 = (f32[2,528,128]{2,1,0:T(8,128)S(1)}, f32[2,528,128]{2,1,0:T(8,128)S(1)}, u32[]{:S(2)}, u32[]{:S(2)}) collective-permute-start(f32[2,528,128]{2,1,0:T(8,128)S(1)} %get-tuple-element.47), channel_id=1, source_target_pairs={{4,0},{8,4},{12,8},{5,1},{9,5},{13,9},{6,2},{10,6},{14,10},{7,3},{... | collective-permute-start | bytes 1622024 | tf_op jit(solution)/shard_map/ppermute | solution.py:228
  86.3 12.7 %collective-permute-start.11 = (f32[528,128]{1,0:T(8,128)S(1)}, f32[528,128]{1,0:T(8,128)S(1)}, u32[]{:S(2)}, u32[]{:S(2)}) collective-permute-start(f32[528,128]{1,0:T(8,128)S(1)} %get-tuple-element.57), channel_id=1, source_target_pairs={{0,32},{32,64},{64,96},{96,128},{128,160},{160,192},{192,224},{224... | collective-permute-start | bytes 811016 | tf_op jit(solution)/shard_map/ppermute | solution.py:237
  88.3 11.9 %collective-permute-start.15 = (f32[528,128]{1,0:T(8,128)S(1)}, f32[528,128]{1,0:T(8,128)S(1)}, u32[]{:S(2)}, u32[]{:S(2)}) collective-permute-start(f32[528,128]{1,0:T(8,128)S(1)} %get-tuple-element.56), channel_id=1, source_target_pairs={{32,0},{64,32},{96,64},{128,96},{160,128},{192,160},{224,192},{0,2... | collective-permute-start | bytes 811016 | tf_op jit(solution)/shard_map/ppermute | solution.py:240
  100.0 9.3 %collective-permute-start.12 = (f32[528,128]{1,0:T(8,128)S(1)}, f32[528,128]{1,0:T(8,128)S(1)}, u32[]{:S(2)}, u32[]{:S(2)}) collective-permute-start(f32[528,128]{1,0:T(8,128)S(1)} %bitcast_add_fusion.5), channel_id=1, source_target_pairs={{0,32},{32,64},{64,96},{96,128},{128,160},{160,192},{192,224},{224... | collective-permute-start | bytes 811016 | tf_op jit(solution)/shard_map/ppermute | solution.py:237
  110.4 8.4 %collective-permute-start.13 = (f32[528,128]{1,0:T(8,128)S(1)}, f32[528,128]{1,0:T(8,128)S(1)}, u32[]{:S(2)}, u32[]{:S(2)}) collective-permute-start(f32[528,128]{1,0:T(8,128)S(1)} %get-tuple-element.55), channel_id=1, source_target_pairs={{0,32},{32,64},{64,96},{96,128},{128,160},{160,192},{192,224},{224... | collective-permute-start | bytes 811016 | tf_op jit(solution)/shard_map/ppermute | solution.py:237
  110.5 8.3 %collective-permute-start.16 = (f32[528,128]{1,0:T(8,128)S(1)}, f32[528,128]{1,0:T(8,128)S(1)}, u32[]{:S(2)}, u32[]{:S(2)}) collective-permute-start(f32[528,128]{1,0:T(8,128)S(1)} %get-tuple-element.54), channel_id=1, source_target_pairs={{32,0},{64,32},{96,64},{128,96},{160,128},{192,160},{224,192},{0,2... | collective-permute-start | bytes 811016 | tf_op jit(solution)/shard_map/ppermute | solution.py:240
  119.9 7.7 %collective-permute-start.14 = (f32[528,128]{1,0:T(8,128)S(1)}, f32[528,128]{1,0:T(8,128)S(1)}, u32[]{:S(2)}, u32[]{:S(2)}) collective-permute-start(f32[528,128]{1,0:T(8,128)S(1)} %get-tuple-element.53), channel_id=1, source_target_pairs={{0,32},{32,64},{64,96},{96,128},{128,160},{160,192},{192,224},{224... | collective-permute-start | bytes 811016 | tf_op jit(solution)/shard_map/ppermute | solution.py:237
  120.0 7.7 %collective-permute-start.17 = (f32[528,128]{1,0:T(8,128)S(1)}, f32[528,128]{1,0:T(8,128)S(1)}, u32[]{:S(2)}, u32[]{:S(2)}) collective-permute-start(f32[528,128]{1,0:T(8,128)S(1)} %get-tuple-element.52), channel_id=1, source_target_pairs={{32,0},{64,32},{96,64},{128,96},{160,128},{192,160},{224,192},{0,2... | collective-permute-start | bytes 811016 | tf_op jit(solution)/shard_map/ppermute | solution.py:240

commit v2 on v1

v2 whole, which is shorter than its diff:
```python
import math

import jax
import jax.numpy as jnp
import numpy as np
from jax import lax
from jax.experimental import pallas as pl
from jax.experimental.pallas import tpu as pltpu
from jax.sharding import Mesh, PartitionSpec as P

TILE = 128
KTAPS = 13
SHIFTS = 8
HALO = 16
BAND = 256
COLS = 4096
BLOCKS = COLS // TILE + 1
EDGE = 122
FRAME = 144
WINDOW = FRAME + 16
LEAD = 119
HALF_TILES = 8
PIECE = HALF_TILES * TILE + 32
CELLROW = 4 * TILE + 16
TOP_CODE = 32000.0
f32 = jnp.float32
bf16 = jnp.bfloat16
i16 = jnp.int16
i32 = jnp.int32
SMEM = pl.BlockSpec(memory_space=pltpu.SMEM)
VMEM = pl.BlockSpec(memory_space=pltpu.VMEM)


def call(kernel, name, out_shape, in_specs, out_specs, scratch=(), mib=8):
    return pl.pallas_call(
        kernel,
        out_shape=out_shape,
        in_specs=in_specs,
        out_specs=out_specs,
        scratch_shapes=scratch,
        compiler_params=pltpu.CompilerParams(vmem_limit_bytes=mib * 2**20),
        name=name,
    )


def lanczos_tables():
    out_pos = np.arange(TILE)[None, :, None]
    src_pos = np.arange(TILE + 6)[None, None, :] - 3.0
    frac = np.arange(SHIFTS)[:, None, None] / SHIFTS
    dist = src_pos - out_pos - frac
    kernel = np.where(np.abs(dist) < 3.0, np.sinc(dist) * np.sinc(dist / 3.0), 0.0)
    kernel = kernel / np.sum(kernel, axis=2, keepdims=True)
    along_rows = np.zeros((SHIFTS + 1, TILE, FRAME), np.float32)
    along_rows[:SHIFTS, :, : TILE + 6] = kernel
    along_cols = np.zeros((SHIFTS, 2 * TILE, TILE), np.float32)
    along_cols[:, LEAD : LEAD + TILE + 6] = kernel.transpose(0, 2, 1)
    return along_rows.astype(bf16), along_cols.astype(bf16)


def banded(taps, shape, base):
    diff = lax.broadcasted_iota(i32, shape, 0) - lax.broadcasted_iota(i32, shape, 1) + base
    total = jnp.zeros(shape, f32)
    for k in range(KTAPS):
        total = jnp.where(diff == k, taps[:, k : k + 1], total)
    return total


def columns_kernel(taps_ref, patch_ref, cell_ref, img_ref, out_ref, info_ref):
    over_cols = banded(taps_ref[0].astype(f32)[1:2], (2 * TILE, TILE), 0)
    lane = lax.broadcasted_iota(i32, (TILE, TILE), 1)
    first = jnp.where(lane >= EDGE, over_cols[TILE:], 0.0).astype(bf16)
    last = jnp.where(lane < EDGE, over_cols[:TILE], 0.0).astype(bf16)
    over_cols = over_cols.astype(bf16)
    for b in range(BLOCKS):
        if b == 0:
            window, weights = img_ref[0, :, :TILE], first
        elif b == BLOCKS - 1:
            window, weights = img_ref[0, :, COLS - TILE :], last
        else:
            window, weights = img_ref[0, :, (b - 1) * TILE : (b + 1) * TILE], over_cols
        out_ref[:, b * TILE : (b + 1) * TILE] = jnp.dot(window, weights, preferred_element_type=f32).astype(bf16)
    owner = patch_ref[0]
    cell = cell_ref[0]
    row0 = 2 * (lax.axis_index("y") * 4 + lax.axis_index("x"))
    down = (owner >> 2) * 8 + (cell >> 3) - lax.broadcasted_iota(i32, owner.shape, 0) - row0
    right = (owner & 3) * 8 + (cell & 7) - lax.broadcasted_iota(i32, owner.shape, 1)
    for n, offset in enumerate((down, right)):
        most = jnp.max(jnp.where(owner >= 0, offset.astype(f32), -8.0)).astype(i32)
        info_ref[n] = jnp.where(most > -8, most, 0)


def rows_kernel(taps_ref, top_ref, bot_ref, passed_ref, out_ref, window_ref, edge_ref):
    patch = lax.axis_index("y") * 4 + lax.axis_index("x")
    taps = taps_ref[0].astype(f32)
    over_cols = banded(taps[1:2], (2 * TILE, TILE), 0).astype(bf16)
    halo = 2 * HALO
    for b in range(BLOCKS):
        for side in range(2):
            k = b - 1 + side
            at = (slice(b * halo, b * halo + HALO), slice(side * TILE, (side + 1) * TILE))
            at_bot = (slice(b * halo + HALO, (b + 1) * halo), at[1])
            if 0 <= k < BLOCKS - 1:
                window_ref[at] = top_ref[:, k * TILE : (k + 1) * TILE]
                window_ref[at_bot] = bot_ref[:, k * TILE : (k + 1) * TILE]
            else:
                window_ref[at] = jnp.zeros((HALO, TILE), bf16)
                window_ref[at_bot] = jnp.zeros((HALO, TILE), bf16)
    lane = lax.broadcasted_iota(i32, (halo, TILE), 1)
    for part in range(3):
        each = BLOCKS // 3
        got = jnp.dot(
            window_ref[part * each * halo : (part + 1) * each * halo], over_cols, preferred_element_type=f32
        )
        for n in range(each):
            b = part * each + n
            rows = got[n * halo : (n + 1) * halo]
            if b == 0:
                rows = jnp.where(lane >= EDGE, rows, 0.0)
            if b == BLOCKS - 1:
                rows = jnp.where(lane < EDGE, rows, 0.0)
            edge_ref[:, b * TILE : (b + 1) * TILE] = rows.astype(bf16)
    shape = (FRAME, WINDOW)
    row = lax.broadcasted_iota(i32, shape, 0)
    base = jnp.zeros(shape, f32)
    step = lax.broadcasted_iota(i32, shape, 1) - row - 7
    for k in range(KTAPS):
        base = jnp.where(step == k, taps[0:1, k : k + 1], base)
    low = jnp.where(patch == 0, 3, 0)
    high = jnp.where(patch == 15, 130, 133)
    over_rows = (
        jnp.where((row >= low) & (row <= 133), base, 0.0).astype(bf16),
        jnp.where(row <= high, base, 0.0).astype(bf16),
    )
    for n in range(BLOCKS // 3):
        at = slice(n * 3 * TILE, (n + 1) * 3 * TILE)
        upper = jnp.concatenate([edge_ref[:HALO, at], passed_ref[:FRAME, at]], axis=0)
        lower = jnp.concatenate([passed_ref[BAND - FRAME :, at], edge_ref[HALO:, at]], axis=0)
        for r, window in enumerate((upper, lower)):
            out_ref[r, :, at] = jnp.dot(over_rows[r], window, preferred_element_type=f32).astype(bf16)


def warp_kernel(hop, info_ref, patch_ref, class_ref, weight_ref, rows_ref, cols_ref, in_ref, own_ref, sib_ref, half_ref):
    core = lax.axis_index("core")
    dest = (lax.axis_index("x") + hop) & 3
    line = lax.broadcasted_iota(i32, (32, TILE), 0)
    weight = jnp.full((32, TILE), weight_ref[0], f32)
    high = weight.astype(bf16).astype(f32)
    mid = (weight - high).astype(bf16).astype(f32)
    low = weight - high - mid
    parts = jnp.where(line < 8, high, jnp.where(line < 16, mid, low))
    down = info_ref[0].astype(f32)
    plan = []
    for side, out_ref in enumerate((own_ref, sib_ref)):
        half = core if side == 0 else 1 - core
        marks = jnp.zeros((32, TILE), f32)
        for slot in range(HALF_TILES):
            r, w = divmod(slot, 4)
            col = dest * 8 + half * 4 + w - info_ref[1]
            inside = (col >= 0) & (col < 32)
            col = jnp.clip(col, 0, 31)
            there = inside & (patch_ref[0, r, col] >= 0)
            plan.append((out_ref, slot, r, col, jnp.where(there, class_ref[0, 0, r, col], SHIFTS)))
            marks = jnp.where((line & 7) == slot, jnp.where(there, 1.0, 0.0), marks)
        out_ref[HALF_TILES * TILE :, :] = jnp.where(line < 24, marks * parts, down).astype(bf16)
    for n, (out_ref, slot, r, col, picked) in enumerate(plan):
        tile = in_ref[r, :, pl.ds(pl.multiple_of(col * TILE, TILE), 2 * TILE)]
        half_ref[n] = jnp.dot(tile, cols_ref[class_ref[0, 1, r, col]], preferred_element_type=f32).astype(bf16)
    for n, (out_ref, slot, r, col, picked) in enumerate(plan):
        out_ref[slot * TILE : (slot + 1) * TILE, :] = jnp.dot(
            rows_ref[picked], half_ref[n], preferred_element_type=f32
        ).astype(bf16)


def encode(cells, weights, out_ref, start):
    line = lax.broadcasted_iota(i32, (16, TILE), 0)
    notes = jnp.zeros((16, TILE), f32)
    for w in range(4):
        cell = cells[w]
        most = jnp.max(jnp.max(jnp.abs(cell), axis=0, keepdims=True), axis=1, keepdims=True)
        level = jnp.ceil(jnp.log(jnp.maximum(most, 1e-33)) * (128.0 / math.log(2.0)))
        code = jnp.floor(cell * (TOP_CODE * jnp.exp(level * (-math.log(2.0) / 128.0))) + 0.5)
        out_ref[start + w * TILE : start + (w + 1) * TILE, :] = code.astype(i32).astype(i16)
        whole = jnp.floor(weights[w : w + 1] * 128.0)
        rest = jnp.floor((weights[w : w + 1] * 128.0 - whole) * 32767.0 + 0.5)
        notes = jnp.where(line == w, level, notes)
        notes = jnp.where(line == 4 + w, whole, notes)
        notes = jnp.where(line == 8 + w, rest, notes)
    out_ref[start + 4 * TILE : start + CELLROW, :] = notes.astype(i32).astype(i16)


def decode(in_ref, start):
    notes = in_ref[start + 4 * TILE : start + CELLROW, :].astype(i32).astype(f32)
    cells = []
    for w in range(4):
        scale = jnp.exp(notes[w : w + 1] * (math.log(2.0) / 128.0)) * (1.0 / TOP_CODE)
        code = in_ref[start + w * TILE : start + (w + 1) * TILE, :].astype(i32).astype(f32)
        cells.append(code * scale)
    return cells, (notes[4:8] + notes[8:12] * (1.0 / 32767.0)) * (1.0 / 128.0)


def held(ref, at):
    cells = [ref[at, w * TILE : (w + 1) * TILE, :] for w in range(4)]
    return cells, ref[at, 4 * TILE : 4 * TILE + 4, :]


def added(*parts):
    cells = [sum(p[0][w] for p in parts[1:]) + parts[0][0][w] for w in range(4)]
    return cells, sum(p[1] for p in parts[1:]) + parts[0][1]


def place_kernel(*refs):
    pieces = refs[:8]
    main_ref, above_ref, below_ref, rows_ref = refs[8:]
    x = lax.axis_index("x")
    rows_ref[...] = jnp.zeros(rows_ref.shape, f32)
    for n, piece in enumerate(pieces):
        band = (x + 4 - n % 4) & 3
        notes = piece[HALF_TILES * TILE :, :].astype(f32)
        weights = notes[0:8] + notes[8:16] + notes[16:24]
        down = jnp.max(notes[24:32]).astype(i32)
        for r in range(2):
            at = 2 * band + r + down + 2
            for w in range(4):
                slot = r * 4 + w
                tile = piece[slot * TILE : (slot + 1) * TILE, :].astype(f32)
                rows_ref[at, w * TILE : (w + 1) * TILE, :] += weights[slot : slot + 1] * tile
            rows_ref[at, 4 * TILE : 4 * TILE + 4, :] += weights[r * 4 : r * 4 + 4]
    for r in range(2):
        encode(*held(rows_ref, r), above_ref, r * CELLROW)
        encode(*held(rows_ref, 10 + r), below_ref, r * CELLROW)
    main_ref[...] = rows_ref[2:10]


def merge_kernel(in_ref, above_ref, below_ref, main_ref, up_ref, dn_ref, far_ref):
    main_ref[...] = in_ref[...]
    for r in range(2):
        for ref, at in ((above_ref, r), (below_ref, 6 + r)):
            cells, weights = added(held(in_ref, at), decode(ref, r * CELLROW))
            for w in range(4):
                main_ref[at, w * TILE : (w + 1) * TILE, :] = cells[w]
            main_ref[at, 4 * TILE : 4 * TILE + 4, :] = weights
    z = lax.axis_index("z")
    encode(*held(main_ref, (z + 3) & 7), up_ref, 0)
    encode(*held(main_ref, (z + 5) & 7), dn_ref, 0)
    encode(*held(main_ref, (z + 4) & 7), far_ref, 0)


def step_kernel(ahead, main_ref, in_ref, out_ref):
    at = (lax.axis_index("z") + 8 + ahead) & 7
    encode(*added(held(main_ref, at), decode(in_ref, 0)), out_ref, 0)


def finish_kernel(main_ref, up_ref, dn_ref, far_ref, coadd_ref, cover_ref):
    z = lax.axis_index("z")
    cells, weights = added(held(main_ref, z), decode(up_ref, 0), decode(dn_ref, 0), decode(far_ref, 0))
    lane = lax.broadcasted_iota(i32, (1, TILE), 1)
    cover = jnp.zeros((1, TILE), f32)
    for w in range(4):
        coadd_ref[0, w] = cells[w] / jnp.maximum(weights[w : w + 1], 1.0)
        cover = jnp.where(lane == w, weights[w : w + 1], cover)
    cover_ref[...] = cover[:, :4]


def local(images, psf_taps, exposure_weights, dest_patch, dest_cell, shift_class):
    shape = jax.ShapeDtypeStruct
    line = [(i, i + 1) for i in range(15)]
    top = lax.ppermute(images[0, BAND - HALO :], ("y", "x"), line)
    bot = lax.ppermute(images[0, :HALO], ("y", "x"), [(j, i) for i, j in line])
    rows, cols = (jnp.asarray(t) for t in lanczos_tables())
    passed, info = call(
        columns_kernel,
        "columns",
        (shape((BAND, BLOCKS * TILE), bf16), shape((2,), i32)),
        [VMEM] * 4,
        (VMEM, SMEM),
    )(psf_taps, dest_patch, dest_cell, images)
    matched = call(
        rows_kernel,
        "rows",
        shape((2, FRAME, BLOCKS * TILE), bf16),
        [VMEM] * 4,
        VMEM,
        [pltpu.VMEM((BLOCKS * 2 * HALO, 2 * TILE), bf16), pltpu.VMEM((2 * HALO, BLOCKS * TILE), bf16)],
    )(psf_taps, top, bot, passed)
    piece = shape((PIECE, TILE), bf16)
    own = [None] * 4
    sib = [None] * 4
    for hop in (2, 1, 3, 0):
        stay, leave = call(
            lambda *refs, hop=hop: warp_kernel(hop, *refs),
            f"warp_{hop}",
            (piece, piece),
            [SMEM] * 4 + [VMEM] * 3,
            (VMEM, VMEM),
            [pltpu.VMEM((2 * HALF_TILES, FRAME, TILE), bf16)],
        )(info, dest_patch, shift_class, exposure_weights, rows, cols, matched)
        if hop:
            own[hop] = lax.ppermute(stay, "x", [(i, (i + hop) % 4) for i in range(4)])
        else:
            own[hop] = stay
        sib[hop] = lax.ppermute(
            leave, ("core", "x"), [(c * 4 + i, (1 - c) * 4 + (i + hop) % 4) for c in range(2) for i in range(4)]
        )
    held_rows = shape((8, CELLROW, TILE), f32)
    spill = shape((2 * CELLROW, TILE), i16)
    coded = shape((CELLROW, TILE), i16)
    main, above, below = call(
        place_kernel, "place", (held_rows, spill, spill), [VMEM] * 8, (VMEM,) * 3, [pltpu.VMEM((12, CELLROW, TILE), f32)]
    )(*own, *sib)
    from_above = lax.ppermute(below, "y", [(i, i + 1) for i in range(3)])
    from_below = lax.ppermute(above, "y", [(i + 1, i) for i in range(3)])
    main, up, dn, far = call(
        merge_kernel, "merge", (held_rows, coded, coded, coded), [VMEM] * 3, (VMEM,) * 4
    )(main, from_above, from_below)
    far = lax.ppermute(far, "z", [(i, (i + 4) % 8) for i in range(8)])
    for s in (2, 1, 0):
        up = lax.ppermute(up, "z", [(i, (i + 1) % 8) for i in range(8)])
        dn = lax.ppermute(dn, "z", [((i + 1) % 8, i) for i in range(8)])
        if s:
            up = call(lambda *refs, s=s: step_kernel(s, *refs), f"up_{s}", coded, [VMEM] * 2, VMEM)(main, up)
            dn = call(lambda *refs, s=s: step_kernel(-s, *refs), f"down_{s}", coded, [VMEM] * 2, VMEM)(main, dn)
    return call(
        finish_kernel, "finish", (shape((1, 4, TILE, TILE), f32), shape((1, 4), f32)), [VMEM] * 4, (VMEM, VMEM)
    )(main, up, dn, far)


def solution(mesh):
    split = Mesh(mesh.devices.reshape(8, 2, 4, 4), ("z", "core", "y", "x"))
    visit = ("z", "core")
    patch = ("y", "x")
    placed = (
        P(visit, patch, None),
        P(visit, None, None),
        P(visit),
        P(visit, patch, None),
        P(visit, patch, None),
        P(visit, None, patch, None),
    )
    return jax.shard_map(
        local,
        mesh=split,
        in_specs=placed,
        out_specs=(P(patch, visit, None, None), P(patch, visit)),
        check_vma=False,
    )
```

time: 131 us -> 96.8 us (0.74)
  other arithmetic: 13.6 us -> 0 us
  Pallas kernels: 25.4 us -> 12.3 us
  waiting for transfers between devices: 48.8 us -> 38.3 us
  starting transfers between devices: 35.4 us -> 39.8 us
    ppermute x4 -> x3, waiting for transfers between devices: 25.3 us -> 3.27 us  [local(): up = lax.ppermute(up, 'z', [(i, (i + 1) % 8) for i in range(8)])]
    pallas_call x6 -> x13, Pallas kernels: 25.4 us -> 12.3 us  [the longest x4 5.42 us: local(): call(lambda *refs, hop=hop: warp_kernel(hop, *refs), f'warp_{hop}', (piec...]
    ppermute x4, waiting for transfers between devices: 6.53 us -> 19.1 us  [local(): lax.ppermute(leave, ('core', 'x'), [(c * 4 + i, (1 - c) * 4 + (i + hop) %...]
    ppermute x1, waiting for transfers between devices: 10.5 us -> 4.34 us  [local(): from_above = lax.ppermute(below, 'y', [(i, i + 1) for i in range(3)])]
    add x4 -> x0, other arithmetic: 4.2 us -> none  [the longest x2 2.21 us: local(): dn = dn + block(z - 2 + s)]
    ppermute x3, waiting for transfers between devices: 0.01 us -> 4 us  [local(): dn = lax.ppermute(dn, 'z', [((i + 1) % 8, i) for i in range(8)])]
    scatter-add x2 -> x0, other arithmetic: 3.81 us -> none  [local(): main = main.at[0:2].add(from_above).at[6:8].add(from_below)]
    ppermute x2 -> x3, starting transfers between devices: 7.95 us -> 11 us  [the longest x1 4.56 us: local(): far = lax.ppermute(far, 'z', [(i, (i + 4) % 8) for i in range(8)])]
  transfers between devices with their start and end apart: 18 -> 18, of which waited for: 9 -> 10; matrix products, arithmetic and copies ran while one was open for 5% -> 0% of each run, Pallas kernels for 9% -> 7%
where the time goes in v2:
time: 96.8 us; the launch traced here: 96.5 us
  starting transfers between devices  39.8 us (41%)
  waiting for transfers between devices  38.3 us (40%)
  Pallas kernels  12.3 us (13%)
  local copies, waits for them, and re-layouts  4.6 us (5%)
  between operations  1.49 us (2%)
    ppermute x4, waiting for transfers between devices, local(): lax.ppermute(leave, ('core', 'x'), [(c * 4 + i, (1 - c) * 4 + (i + hop) %...  19.1 us
    ppermute x3, starting transfers between devices, local(): dn = lax.ppermute(dn, 'z', [((i + 1) % 8, i) for i in range(8)])  12 us
    ppermute x3, starting transfers between devices, local(): own[hop] = lax.ppermute(stay, 'x', [(i, (i + hop) % 4) for i in range(4)])  5.53 us
    pallas_call x4, Pallas kernels, local(): call(lambda *refs, hop=hop: warp_kernel(hop, *refs), f'warp_{hop}', (piec...  5.42 us
    ppermute x1, starting transfers between devices, local(): far = lax.ppermute(far, 'z', [(i, (i + 4) % 8) for i in range(8)])  4.56 us
    ppermute x1, starting transfers between devices, local(): bot = lax.ppermute(images[0, :HALO], ('y', 'x'), [(j, i) for i, j in line])  4.55 us
    ppermute x1, waiting for transfers between devices, local(): from_above = lax.ppermute(below, 'y', [(i, i + 1) for i in range(3)])  4.34 us
    ppermute x3, waiting for transfers between devices, local(): dn = lax.ppermute(dn, 'z', [((i + 1) % 8, i) for i in range(8)])  4 us
  transfers between devices with their start and end apart: 18, of which 10 were waited for; matrix products, arithmetic and copies ran while one was open for 0% of the time, Pallas kernels for 7%

profile of v2, /device:TPU:8, one launch (start us, length us, event | category | flops | bytes accessed | tf_op | source)
XLA Modules:
  0.0 96.5 jit_solution(2670617725083588428)
XLA Ops:
  1.6 4.6 %collective-permute-start.1 = (bf16[16,4096]{1,0:T(8,128)(2,1)S(1)}, bf16[16,4096]{1,0:T(8,128)(2,1)S(1)}, u32[]{:S(2)}, u32[]{:S(2)}) collective-permute-start(bf16[16,4096]{1,0:T(8,128)(2,1)S(1)} %get-tuple-element.36), channel_id=1, source_target_pairs={{1,0},{2,1},{3,2},{4,3},{5,4},{6,5},{7,6},{8,7},{9,8},{10,9},{11,1... | collective-permute-start | bytes 393224 | tf_op jit(solution)/shard_map/ppermute | solution.py:268
  6.2 1.9 %collective-permute-start = (bf16[16,4096]{1,0:T(8,128)(2,1)S(1)}, bf16[16,4096]{1,0:T(8,128)(2,1)S(1)}, u32[]{:S(2)}, u32[]{:S(2)}) collective-permute-start(bf16[16,4096]{1,0:T(8,128)(2,1)S(1)} %get-tuple-element.37), channel_id=1, source_target_pairs={{0,1},{1,2},{2,3},{3,4},{4,5},{5,6},{6,7},{7,8},{8,9},{9,10},{10,1... | collective-permute-start | bytes 393224 | tf_op jit(solution)/shard_map/ppermute | solution.py:267
  8.8 1.6 %copy-done.2 = bf16[1,256,4096]{2,1,0:T(8,128)(2,1)S(1)} copy-done((bf16[1,256,4096]{2,1,0:T(8,128)(2,1)S(1)}, bf16[1,256,4096]{2,1,0:T(8,128)(2,1)}, u32[]{:S(2)}) %copy-start.2) | copy-done | bytes 2097176
  12.4 1.9 %columns.1 = (bf16[256,4224]{1,0:T(8,128)(2,1)S(1)}, s32[2]{0:T(128)S(1)}) custom-call(bf16[1,2,13]{2,1,0:T(2,128)(2,1)S(1)} %copy-done.6, s32[1,2,32]{2,1,0:T(2,128)S(1)} %copy-done.4, s32[1,2,32]{2,1,0:T(2,128)S(1)} %copy-done.7, bf16[1,256,4096]{2,1,0:T(8,128)(2,1)S(1)} %copy-done.2), custom_call_target="tpu_custom_call" | custom-call | tf_op jit(solution)/shard_map/columns/pallas_call | solution.py:270
  15.2 1.4 %rows.1.refs_6_ = bf16[2,144,4224]{2,1,0:T(8,128)(2,1)S(1)} custom-call(bf16[1,2,13]{2,1,0:T(2,128)(2,1)S(1)} %copy-done.6, bf16[16,4096]{1,0:T(8,128)(2,1)S(1)} %collective-permute-done.top_ref, bf16[16,4096]{1,0:T(8,128)(2,1)S(1)} %collective-permute-done.1.bot_ref, bf16[256,4224]{1,0:T(8,128)(2,1)S(1)} %get-tuple-element.20.passed_ref), custom_call_target="tpu_custom_call" | custom-call | tf_op jit(solution)/shard_map/rows/pallas_call | solution.py:277
  18.0 3.5 %collective-permute-start.4 = (bf16[1056,128]{1,0:T(8,128)(2,1)S(1)}, bf16[1056,128]{1,0:T(8,128)(2,1)S(1)}, u32[]{:S(2)}, u32[]{:S(2)}) collective-permute-start(bf16[1056,128]{1,0:T(8,128)(2,1)S(1)} %get-tuple-element.24), channel_id=1, source_target_pairs={{0,3},{1,0},{2,1},{3,2},{4,7},{5,4},{6,5},{7,6},{8,11},{9,8},{10,9... | collective-permute-start | bytes 811016 | tf_op jit(solution)/shard_map/ppermute | solution.py:298
  22.8 1.4 %warp_1.1 = (bf16[1056,128]{1,0:T(8,128)(2,1)S(1)}, bf16[1056,128]{1,0:T(8,128)(2,1)S(1)}) custom-call(s32[2]{0:T(128)S(1)} %get-tuple-element.19.refs_0_, s32[1,2,32]{2,1,0:T(2,128)S(1)} %copy-done.5, s32[1,2,2,32]{3,2,1,0:T(2,128)S(1)} %copy-done.3, f32[1]{0:T(128)S(6)} %copy.10.refs_3_, bf16[9,128,144]{2,1,0:T(8,128)(2,1)S(1)} %copy-done, ...), custom_call_target="tpu_custom_call" | custom-call | tf_op jit(solution)/shard_map/warp_1/pallas_call | solution.py:289
  25.7 3.0 %collective-permute-start.7 = (bf16[1056,128]{1,0:T(8,128)(2,1)S(1)}, bf16[1056,128]{1,0:T(8,128)(2,1)S(1)}, u32[]{:S(2)}, u32[]{:S(2)}) collective-permute-start(bf16[1056,128]{1,0:T(8,128)(2,1)S(1)} %get-tuple-element.27), channel_id=1, source_target_pairs={{0,18},{1,19},{2,16},{3,17},{16,2},{17,3},{18,0},{19,1},{4,22},{5,... | collective-permute-start | bytes 811016 | tf_op jit(solution)/shard_map/ppermute | solution.py:301
  28.7 1.9 %collective-permute-start.2 = (bf16[1056,128]{1,0:T(8,128)(2,1)S(1)}, bf16[1056,128]{1,0:T(8,128)(2,1)S(1)}, u32[]{:S(2)}, u32[]{:S(2)}) collective-permute-start(bf16[1056,128]{1,0:T(8,128)(2,1)S(1)} %get-tuple-element.22), channel_id=1, source_target_pairs={{0,1},{1,2},{2,3},{3,0},{4,5},{5,6},{6,7},{7,4},{8,9},{9,10},{10,1... | collective-permute-start | bytes 811016 | tf_op jit(solution)/shard_map/ppermute | solution.py:298
  30.6 13.4 %collective-permute-done.8.refs_7_ = bf16[1056,128]{1,0:T(8,128)(2,1)S(1)} collective-permute-done((bf16[1056,128]{1,0:T(8,128)(2,1)S(1)}, bf16[1056,128]{1,0:T(8,128)(2,1)S(1)}, u32[]{:S(2)}, u32[]{:S(2)}) %collective-permute-start.8) | collective-permute-done | bytes 270368 | tf_op jit(solution)/shard_map/ppermute | solution.py:301
  44.0 3.3 %collective-permute-done.2.refs_1_ = bf16[1056,128]{1,0:T(8,128)(2,1)S(1)} collective-permute-done((bf16[1056,128]{1,0:T(8,128)(2,1)S(1)}, bf16[1056,128]{1,0:T(8,128)(2,1)S(1)}, u32[]{:S(2)}, u32[]{:S(2)}) %collective-permute-start.2) | collective-permute-done | bytes 270368 | tf_op jit(solution)/shard_map/ppermute | solution.py:298
  47.3 5.7 %collective-permute-done.6.refs_5_ = bf16[1056,128]{1,0:T(8,128)(2,1)S(1)} collective-permute-done((bf16[1056,128]{1,0:T(8,128)(2,1)S(1)}, bf16[1056,128]{1,0:T(8,128)(2,1)S(1)}, u32[]{:S(2)}, u32[]{:S(2)}) %collective-permute-start.6) | collective-permute-done | bytes 270368 | tf_op jit(solution)/shard_map/ppermute | solution.py:301
  54.4 3.7 %collective-permute-start.9 = (s16[1056,128]{1,0:T(8,128)(2,1)S(1)}, s16[1056,128]{1,0:T(8,128)(2,1)S(1)}, u32[]{:S(2)}, u32[]{:S(2)}) collective-permute-start(s16[1056,128]{1,0:T(8,128)(2,1)S(1)} %get-tuple-element.30), channel_id=1, source_target_pairs={{0,4},{4,8},{8,12},{1,5},{5,9},{9,13},{2,6},{6,10},{10,14},{3,7},{... | collective-permute-start | bytes 811016 | tf_op jit(solution)/shard_map/ppermute | solution.py:310
  58.1 2.4 %collective-permute-start.10 = (s16[1056,128]{1,0:T(8,128)(2,1)S(1)}, s16[1056,128]{1,0:T(8,128)(2,1)S(1)}, u32[]{:S(2)}, u32[]{:S(2)}) collective-permute-start(s16[1056,128]{1,0:T(8,128)(2,1)S(1)} %get-tuple-element.31), channel_id=1, source_target_pairs={{4,0},{8,4},{12,8},{5,1},{9,5},{13,9},{6,2},{10,6},{14,10},{7,3},{... | collective-permute-start | bytes 811016 | tf_op jit(solution)/shard_map/ppermute | solution.py:311
  60.5 4.3 %collective-permute-done.9.above_ref = s16[1056,128]{1,0:T(8,128)(2,1)S(1)} collective-permute-done((s16[1056,128]{1,0:T(8,128)(2,1)S(1)}, s16[1056,128]{1,0:T(8,128)(2,1)S(1)}, u32[]{:S(2)}, u32[]{:S(2)}) %collective-permute-start.9) | collective-permute-done | bytes 270368 | tf_op jit(solution)/shard_map/ppermute | solution.py:310
  64.8 3.4 %collective-permute-done.10.below_ref = s16[1056,128]{1,0:T(8,128)(2,1)S(1)} collective-permute-done((s16[1056,128]{1,0:T(8,128)(2,1)S(1)}, s16[1056,128]{1,0:T(8,128)(2,1)S(1)}, u32[]{:S(2)}, u32[]{:S(2)}) %collective-permute-start.10) | collective-permute-done | bytes 270368 | tf_op jit(solution)/shard_map/ppermute | solution.py:311
  68.8 2.0 %collective-permute-start.11 = (s16[528,128]{1,0:T(8,128)(2,1)S(1)}, s16[528,128]{1,0:T(8,128)(2,1)S(1)}, u32[]{:S(2)}, u32[]{:S(2)}) collective-permute-start(s16[528,128]{1,0:T(8,128)(2,1)S(1)} %get-tuple-element.33), channel_id=1, source_target_pairs={{0,32},{32,64},{64,96},{96,128},{128,160},{160,192},{192,224},{224... | collective-permute-start | bytes 405512 | tf_op jit(solution)/shard_map/ppermute | solution.py:317
  70.8 4.2 %collective-permute-start.14 = (s16[528,128]{1,0:T(8,128)(2,1)S(1)}, s16[528,128]{1,0:T(8,128)(2,1)S(1)}, u32[]{:S(2)}, u32[]{:S(2)}) collective-permute-start(s16[528,128]{1,0:T(8,128)(2,1)S(1)} %get-tuple-element.34), channel_id=1, source_target_pairs={{32,0},{64,32},{96,64},{128,96},{160,128},{192,160},{224,192},{0,2... | collective-permute-start | bytes 405512 | tf_op jit(solution)/shard_map/ppermute | solution.py:318
  74.9 2.9 %collective-permute-done.11.refs_1_ = s16[528,128]{1,0:T(8,128)(2,1)S(1)} collective-permute-done((s16[528,128]{1,0:T(8,128)(2,1)S(1)}, s16[528,128]{1,0:T(8,128)(2,1)S(1)}, u32[]{:S(2)}, u32[]{:S(2)}) %collective-permute-start.11) | collective-permute-done | bytes 135200 | tf_op jit(solution)/shard_map/ppermute | solution.py:317
  78.4 3.3 %collective-permute-start.15 = (s16[528,128]{1,0:T(8,128)(2,1)S(1)}, s16[528,128]{1,0:T(8,128)(2,1)S(1)}, u32[]{:S(2)}, u32[]{:S(2)}) collective-permute-start(s16[528,128]{1,0:T(8,128)(2,1)S(1)} %down_2.1), channel_id=1, source_target_pairs={{32,0},{64,32},{96,64},{128,96},{160,128},{192,160},{224,192},{0,2... | collective-permute-start | bytes 405512 | tf_op jit(solution)/shard_map/ppermute | solution.py:318
  81.6 4.6 %collective-permute-start.17 = (s16[528,128]{1,0:T(8,128)(2,1)S(1)}, s16[528,128]{1,0:T(8,128)(2,1)S(1)}, u32[]{:S(2)}, u32[]{:S(2)}) collective-permute-start(s16[528,128]{1,0:T(8,128)(2,1)S(1)} %get-tuple-element.35), channel_id=1, source_target_pairs={{0,128},{32,160},{64,192},{96,224},{128,0},{160,32},{192,64},{224,... | collective-permute-start | bytes 405512 | tf_op jit(solution)/shard_map/ppermute | solution.py:315
  86.5 1.8 %collective-permute-done.15.refs_1_ = s16[528,128]{1,0:T(8,128)(2,1)S(1)} collective-permute-done((s16[528,128]{1,0:T(8,128)(2,1)S(1)}, s16[528,128]{1,0:T(8,128)(2,1)S(1)}, u32[]{:S(2)}, u32[]{:S(2)}) %collective-permute-start.15) | collective-permute-done | bytes 135200 | tf_op jit(solution)/shard_map/ppermute | solution.py:318
  88.5 4.5 %collective-permute-start.16 = (s16[528,128]{1,0:T(8,128)(2,1)S(1)}, s16[528,128]{1,0:T(8,128)(2,1)S(1)}, u32[]{:S(2)}, u32[]{:S(2)}) collective-permute-start(s16[528,128]{1,0:T(8,128)(2,1)S(1)} %down_1.1), channel_id=1, source_target_pairs={{32,0},{64,32},{96,64},{128,96},{160,128},{192,160},{224,192},{0,2... | collective-permute-start | bytes 405512 | tf_op jit(solution)/shard_map/ppermute | solution.py:318
  93.5 2.2 %collective-permute-done.16.dn_ref = s16[528,128]{1,0:T(8,128)(2,1)S(1)} collective-permute-done((s16[528,128]{1,0:T(8,128)(2,1)S(1)}, s16[528,128]{1,0:T(8,128)(2,1)S(1)}, u32[]{:S(2)}, u32[]{:S(2)}) %collective-permute-start.16) | collective-permute-done | bytes 135200 | tf_op jit(solution)/shard_map/ppermute | solution.py:318
  (42 shorter events, 12.2 us)
Async XLA Ops:
  1.6 12.7 %collective-permute-start.1 = (bf16[16,4096]{1,0:T(8,128)(2,1)S(1)}, bf16[16,4096]{1,0:T(8,128)(2,1)S(1)}, u32[]{:S(2)}, u32[]{:S(2)}) collective-permute-start(bf16[16,4096]{1,0:T(8,128)(2,1)S(1)} %get-tuple-element.36), channel_id=1, source_target_pairs={{1,0},{2,1},{3,2},{4,3},{5,4},{6,5},{7,6},{8,7},{9,8},{10,9},{11,1... | collective-permute-start | bytes 393224 | tf_op jit(solution)/shard_map/ppermute | solution.py:268
  6.2 9.0 %collective-permute-start = (bf16[16,4096]{1,0:T(8,128)(2,1)S(1)}, bf16[16,4096]{1,0:T(8,128)(2,1)S(1)}, u32[]{:S(2)}, u32[]{:S(2)}) collective-permute-start(bf16[16,4096]{1,0:T(8,128)(2,1)S(1)} %get-tuple-element.37), channel_id=1, source_target_pairs={{0,1},{1,2},{2,3},{3,4},{4,5},{5,6},{6,7},{7,8},{8,9},{9,10},{10,1... | collective-permute-start | bytes 393224 | tf_op jit(solution)/shard_map/ppermute | solution.py:267
  8.8 1.6 %copy-start.2 = (bf16[1,256,4096]{2,1,0:T(8,128)(2,1)S(1)}, bf16[1,256,4096]{2,1,0:T(8,128)(2,1)}, u32[]{:S(2)}) copy-start(bf16[1,256,4096]{2,1,0:T(8,128)(2,1)} %img_ref.1) | copy-start | bytes 6291460
  10.4 0.7 copy-start.4
  15.2 1.4 %copy-start = (bf16[9,128,144]{2,1,0:T(8,128)(2,1)S(1)}, bf16[9,128,144]{2,1,0:T(8,128)(2,1)}, u32[]{:S(2)}) copy-start(bf16[9,128,144]{2,1,0:T(8,128)(2,1)} %constant.4.clone.refs_4_) | copy-start | bytes 995332
  15.2 1.4 %copy-start.1 = (bf16[8,256,128]{2,1,0:T(8,128)(2,1)S(1)}, bf16[8,256,128]{2,1,0:T(8,128)(2,1)}, u32[]{:S(2)}) copy-start(bf16[8,256,128]{2,1,0:T(8,128)(2,1)} %constant.5.clone.refs_5_) | copy-start | bytes 1572868
  15.2 1.4 %copy-start.3 = (s32[1,2,2,32]{3,2,1,0:T(2,128)S(1)}, s32[1,2,2,32]{3,2,1,0:T(2,128)}, u32[]{:S(2)}) copy-start(s32[1,2,2,32]{3,2,1,0:T(2,128)} %refs_2_.7) | copy-start | bytes 1540
  15.2 1.4 %copy-start.5 = (s32[1,2,32]{2,1,0:T(2,128)S(1)}, s32[1,2,32]{2,1,0:T(2,128)}, u32[]{:S(2)}) copy-start(s32[1,2,32]{2,1,0:T(2,128)} %refs_1_.7) | copy-start | bytes 772
  18.0 12.7 %collective-permute-start.4 = (bf16[1056,128]{1,0:T(8,128)(2,1)S(1)}, bf16[1056,128]{1,0:T(8,128)(2,1)S(1)}, u32[]{:S(2)}, u32[]{:S(2)}) collective-permute-start(bf16[1056,128]{1,0:T(8,128)(2,1)S(1)} %get-tuple-element.24), channel_id=1, source_target_pairs={{0,3},{1,0},{2,1},{3,2},{4,7},{5,4},{6,5},{7,6},{8,11},{9,8},{10,9... | collective-permute-start | bytes 811016 | tf_op jit(solution)/shard_map/ppermute | solution.py:298
  21.5 22.6 %collective-permute-start.8 = (bf16[1056,128]{1,0:T(8,128)(2,1)S(1)}, bf16[1056,128]{1,0:T(8,128)(2,1)S(1)}, u32[]{:S(2)}, u32[]{:S(2)}) collective-permute-start(bf16[1056,128]{1,0:T(8,128)(2,1)S(1)} %get-tuple-element.28), channel_id=1, source_target_pairs={{0,19},{1,16},{2,17},{3,18},{16,3},{17,0},{18,1},{19,2},{4,23},{5,... | collective-permute-start | bytes 811016 | tf_op jit(solution)/shard_map/ppermute | solution.py:301
  25.6 18.5 %collective-permute-start.3 = (bf16[1056,128]{1,0:T(8,128)(2,1)S(1)}, bf16[1056,128]{1,0:T(8,128)(2,1)S(1)}, u32[]{:S(2)}, u32[]{:S(2)}) collective-permute-start(bf16[1056,128]{1,0:T(8,128)(2,1)S(1)} %get-tuple-element.23), channel_id=1, source_target_pairs={{0,2},{1,3},{2,0},{3,1},{4,6},{5,7},{6,4},{7,5},{8,10},{9,11},{10,... | collective-permute-start | bytes 811016 | tf_op jit(solution)/shard_map/ppermute | solution.py:298
  25.7 18.4 %collective-permute-start.7 = (bf16[1056,128]{1,0:T(8,128)(2,1)S(1)}, bf16[1056,128]{1,0:T(8,128)(2,1)S(1)}, u32[]{:S(2)}, u32[]{:S(2)}) collective-permute-start(bf16[1056,128]{1,0:T(8,128)(2,1)S(1)} %get-tuple-element.27), channel_id=1, source_target_pairs={{0,18},{1,19},{2,16},{3,17},{16,2},{17,3},{18,0},{19,1},{4,22},{5,... | collective-permute-start | bytes 811016 | tf_op jit(solution)/shard_map/ppermute | solution.py:301
  28.7 18.6 %collective-permute-start.2 = (bf16[1056,128]{1,0:T(8,128)(2,1)S(1)}, bf16[1056,128]{1,0:T(8,128)(2,1)S(1)}, u32[]{:S(2)}, u32[]{:S(2)}) collective-permute-start(bf16[1056,128]{1,0:T(8,128)(2,1)S(1)} %get-tuple-element.22), channel_id=1, source_target_pairs={{0,1},{1,2},{2,3},{3,0},{4,5},{5,6},{6,7},{7,4},{8,9},{9,10},{10,1... | collective-permute-start | bytes 811016 | tf_op jit(solution)/shard_map/ppermute | solution.py:298
  30.6 22.4 %collective-permute-start.6 = (bf16[1056,128]{1,0:T(8,128)(2,1)S(1)}, bf16[1056,128]{1,0:T(8,128)(2,1)S(1)}, u32[]{:S(2)}, u32[]{:S(2)}) collective-permute-start(bf16[1056,128]{1,0:T(8,128)(2,1)S(1)} %get-tuple-element.26), channel_id=1, source_target_pairs={{0,17},{1,18},{2,19},{3,16},{16,1},{17,2},{18,3},{19,0},{4,21},{5,... | collective-permute-start | bytes 811016 | tf_op jit(solution)/shard_map/ppermute | solution.py:301
  44.0 9.0 %collective-permute-start.5 = (bf16[1056,128]{1,0:T(8,128)(2,1)S(1)}, bf16[1056,128]{1,0:T(8,128)(2,1)S(1)}, u32[]{:S(2)}, u32[]{:S(2)}) collective-permute-start(bf16[1056,128]{1,0:T(8,128)(2,1)S(1)} %get-tuple-element.25), channel_id=1, source_target_pairs={{0,16},{1,17},{2,18},{3,19},{16,0},{17,1},{18,2},{19,3},{4,20},{5,... | collective-permute-start | bytes 811016 | tf_op jit(solution)/shard_map/ppermute | solution.py:301
  54.4 10.4 %collective-permute-start.9 = (s16[1056,128]{1,0:T(8,128)(2,1)S(1)}, s16[1056,128]{1,0:T(8,128)(2,1)S(1)}, u32[]{:S(2)}, u32[]{:S(2)}) collective-permute-start(s16[1056,128]{1,0:T(8,128)(2,1)S(1)} %get-tuple-element.30), channel_id=1, source_target_pairs={{0,4},{4,8},{8,12},{1,5},{5,9},{9,13},{2,6},{6,10},{10,14},{3,7},{... | collective-permute-start | bytes 811016 | tf_op jit(solution)/shard_map/ppermute | solution.py:310
  58.1 10.1 %collective-permute-start.10 = (s16[1056,128]{1,0:T(8,128)(2,1)S(1)}, s16[1056,128]{1,0:T(8,128)(2,1)S(1)}, u32[]{:S(2)}, u32[]{:S(2)}) collective-permute-start(s16[1056,128]{1,0:T(8,128)(2,1)S(1)} %get-tuple-element.31), channel_id=1, source_target_pairs={{4,0},{8,4},{12,8},{5,1},{9,5},{13,9},{6,2},{10,6},{14,10},{7,3},{... | collective-permute-start | bytes 811016 | tf_op jit(solution)/shard_map/ppermute | solution.py:311
  68.8 9.0 %collective-permute-start.11 = (s16[528,128]{1,0:T(8,128)(2,1)S(1)}, s16[528,128]{1,0:T(8,128)(2,1)S(1)}, u32[]{:S(2)}, u32[]{:S(2)}) collective-permute-start(s16[528,128]{1,0:T(8,128)(2,1)S(1)} %get-tuple-element.33), channel_id=1, source_target_pairs={{0,32},{32,64},{64,96},{96,128},{128,160},{160,192},{192,224},{224... | collective-permute-start | bytes 405512 | tf_op jit(solution)/shard_map/ppermute | solution.py:317
  70.8 7.4 %collective-permute-start.14 = (s16[528,128]{1,0:T(8,128)(2,1)S(1)}, s16[528,128]{1,0:T(8,128)(2,1)S(1)}, u32[]{:S(2)}, u32[]{:S(2)}) collective-permute-start(s16[528,128]{1,0:T(8,128)(2,1)S(1)} %get-tuple-element.34), channel_id=1, source_target_pairs={{32,0},{64,32},{96,64},{128,96},{160,128},{192,160},{224,192},{0,2... | collective-permute-start | bytes 405512 | tf_op jit(solution)/shard_map/ppermute | solution.py:318
  78.0 8.2 %collective-permute-start.12 = (s16[528,128]{1,0:T(8,128)(2,1)S(1)}, s16[528,128]{1,0:T(8,128)(2,1)S(1)}, u32[]{:S(2)}, u32[]{:S(2)}) collective-permute-start(s16[528,128]{1,0:T(8,128)(2,1)S(1)} %up_2.1), channel_id=1, source_target_pairs={{0,32},{32,64},{64,96},{96,128},{128,160},{160,192},{192,224},{224... | collective-permute-start | bytes 405512 | tf_op jit(solution)/shard_map/ppermute | solution.py:317
  78.4 10.0 %collective-permute-start.15 = (s16[528,128]{1,0:T(8,128)(2,1)S(1)}, s16[528,128]{1,0:T(8,128)(2,1)S(1)}, u32[]{:S(2)}, u32[]{:S(2)}) collective-permute-start(s16[528,128]{1,0:T(8,128)(2,1)S(1)} %down_2.1), channel_id=1, source_target_pairs={{32,0},{64,32},{96,64},{128,96},{160,128},{192,160},{224,192},{0,2... | collective-permute-start | bytes 405512 | tf_op jit(solution)/shard_map/ppermute | solution.py:318
  81.6 11.4 %collective-permute-start.17 = (s16[528,128]{1,0:T(8,128)(2,1)S(1)}, s16[528,128]{1,0:T(8,128)(2,1)S(1)}, u32[]{:S(2)}, u32[]{:S(2)}) collective-permute-start(s16[528,128]{1,0:T(8,128)(2,1)S(1)} %get-tuple-element.35), channel_id=1, source_target_pairs={{0,128},{32,160},{64,192},{96,224},{128,0},{160,32},{192,64},{224,... | collective-permute-start | bytes 405512 | tf_op jit(solution)/shard_map/ppermute | solution.py:315
  86.4 7.0 %collective-permute-start.13 = (s16[528,128]{1,0:T(8,128)(2,1)S(1)}, s16[528,128]{1,0:T(8,128)(2,1)S(1)}, u32[]{:S(2)}, u32[]{:S(2)}) collective-permute-start(s16[528,128]{1,0:T(8,128)(2,1)S(1)} %up_1.1), channel_id=1, source_target_pairs={{0,32},{32,64},{64,96},{96,128},{128,160},{160,192},{192,224},{224... | collective-permute-start | bytes 405512 | tf_op jit(solution)/shard_map/ppermute | solution.py:317
  88.5 7.1 %collective-permute-start.16 = (s16[528,128]{1,0:T(8,128)(2,1)S(1)}, s16[528,128]{1,0:T(8,128)(2,1)S(1)}, u32[]{:S(2)}, u32[]{:S(2)}) collective-permute-start(s16[528,128]{1,0:T(8,128)(2,1)S(1)} %down_1.1), channel_id=1, source_target_pairs={{32,0},{64,32},{96,64},{128,96},{160,128},{192,160},{224,192},{0,2... | collective-permute-start | bytes 405512 | tf_op jit(solution)/shard_map/ppermute | solution.py:318
  (2 other events, 1.3 us)

commit v3 on v2

--- a/solution.py
+++ b/solution.py
@@ -23,15 +23,20 @@
 PIECE = HALF_TILES * TILE + 32
 CELLROW = 4 * TILE + 16
 TOP_CODE = 32000.0
+HOPS = ((1, 3), (2, 0))
+WARP_COST = 0
+CHAIN = 3
+FIRST = (CHAIN, -CHAIN, 4) + tuple(sign * d for d in range(CHAIN + 1, 4) for sign in (1, -1))
 f32 = jnp.float32
 bf16 = jnp.bfloat16
 i16 = jnp.int16
 i32 = jnp.int32
 SMEM = pl.BlockSpec(memory_space=pltpu.SMEM)
 VMEM = pl.BlockSpec(memory_space=pltpu.VMEM)
-
-
-def call(kernel, name, out_shape, in_specs, out_specs, scratch=(), mib=8):
+HBM = pl.BlockSpec(memory_space=pltpu.HBM)
+
+
+def call(kernel, name, out_shape, in_specs, out_specs, scratch=(), mib=8, flops=0):
     return pl.pallas_call(
         kernel,
         out_shape=out_shape,
@@ -39,6 +44,7 @@
         out_specs=out_specs,
         scratch_shapes=scratch,
         compiler_params=pltpu.CompilerParams(vmem_limit_bytes=mib * 2**20),
+        cost_estimate=pl.CostEstimate(flops=flops, transcendentals=0, bytes_accessed=0) if flops else None,
         name=name,
     )
 
@@ -65,28 +71,43 @@
     return total
 
 
-def columns_kernel(taps_ref, patch_ref, cell_ref, img_ref, out_ref, info_ref):
-    over_cols = banded(taps_ref[0].astype(f32)[1:2], (2 * TILE, TILE), 0)
+def columns_kernel(taps_hbm, patch_hbm, cell_hbm, img_hbm, out_ref, info_ref, taps_ref, patch_ref, cell_ref, img_ref, sems):
+    small = [
+        pltpu.make_async_copy(src.at[0], dst, sems.at[n])
+        for n, (src, dst) in enumerate(((taps_hbm, taps_ref), (patch_hbm, patch_ref), (cell_hbm, cell_ref)))
+    ]
+    quarter = COLS // 4
+    parts = []
+    for n in range(4):
+        at = slice(n * quarter, (n + 1) * quarter)
+        parts.append(pltpu.make_async_copy(img_hbm.at[0, :, at], img_ref.at[:, at], sems.at[3 + n]))
+    for copy in small + parts:
+        copy.start()
+    for copy in small:
+        copy.wait()
+    over_cols = banded(taps_ref[...].astype(f32)[1:2], (2 * TILE, TILE), 0)
     lane = lax.broadcasted_iota(i32, (TILE, TILE), 1)
     first = jnp.where(lane >= EDGE, over_cols[TILE:], 0.0).astype(bf16)
     last = jnp.where(lane < EDGE, over_cols[:TILE], 0.0).astype(bf16)
     over_cols = over_cols.astype(bf16)
-    for b in range(BLOCKS):
-        if b == 0:
-            window, weights = img_ref[0, :, :TILE], first
-        elif b == BLOCKS - 1:
-            window, weights = img_ref[0, :, COLS - TILE :], last
-        else:
-            window, weights = img_ref[0, :, (b - 1) * TILE : (b + 1) * TILE], over_cols
-        out_ref[:, b * TILE : (b + 1) * TILE] = jnp.dot(window, weights, preferred_element_type=f32).astype(bf16)
-    owner = patch_ref[0]
-    cell = cell_ref[0]
+    owner = patch_ref[...]
+    cell = cell_ref[...]
     row0 = 2 * (lax.axis_index("y") * 4 + lax.axis_index("x"))
     down = (owner >> 2) * 8 + (cell >> 3) - lax.broadcasted_iota(i32, owner.shape, 0) - row0
     right = (owner & 3) * 8 + (cell & 7) - lax.broadcasted_iota(i32, owner.shape, 1)
     for n, offset in enumerate((down, right)):
         most = jnp.max(jnp.where(owner >= 0, offset.astype(f32), -8.0)).astype(i32)
-        info_ref[n] = jnp.where(most > -8, most, 0)
+        info_ref[n] = jnp.where(most > -8, jnp.clip(most, -2, 2), 0)
+    for b in range(BLOCKS):
+        if b % 8 == 0 and b < BLOCKS - 1:
+            parts[b // 8].wait()
+        if b == 0:
+            window, weights = img_ref[:, :TILE], first
+        elif b == BLOCKS - 1:
+            window, weights = img_ref[:, COLS - TILE :], last
+        else:
+            window, weights = img_ref[:, (b - 1) * TILE : (b + 1) * TILE], over_cols
+        out_ref[:, b * TILE : (b + 1) * TILE] = jnp.dot(window, weights, preferred_element_type=f32).astype(bf16)
 
 
 def rows_kernel(taps_ref, top_ref, bot_ref, passed_ref, out_ref, window_ref, edge_ref):
@@ -139,9 +160,9 @@
             out_ref[r, :, at] = jnp.dot(over_rows[r], window, preferred_element_type=f32).astype(bf16)
 
 
-def warp_kernel(hop, info_ref, patch_ref, class_ref, weight_ref, rows_ref, cols_ref, in_ref, own_ref, sib_ref, half_ref):
+def warp_kernel(hops, info_ref, patch_ref, class_ref, weight_ref, rows_ref, cols_ref, in_ref, *refs):
+    out_refs, half_ref = refs[:-1], refs[-1]
     core = lax.axis_index("core")
-    dest = (lax.axis_index("x") + hop) & 3
     line = lax.broadcasted_iota(i32, (32, TILE), 0)
     weight = jnp.full((32, TILE), weight_ref[0], f32)
     high = weight.astype(bf16).astype(f32)
@@ -150,8 +171,9 @@
     parts = jnp.where(line < 8, high, jnp.where(line < 16, mid, low))
     down = info_ref[0].astype(f32)
     plan = []
-    for side, out_ref in enumerate((own_ref, sib_ref)):
-        half = core if side == 0 else 1 - core
+    for n, out_ref in enumerate(out_refs):
+        dest = (lax.axis_index("x") + hops[n // 2]) & 3
+        half = core if n % 2 == 0 else 1 - core
         marks = jnp.zeros((32, TILE), f32)
         for slot in range(HALF_TILES):
             r, w = divmod(slot, 4)
@@ -231,7 +253,7 @@
     main_ref[...] = rows_ref[2:10]
 
 
-def merge_kernel(in_ref, above_ref, below_ref, main_ref, up_ref, dn_ref, far_ref):
+def merge_kernel(in_ref, above_ref, below_ref, main_ref, *outs):
     main_ref[...] = in_ref[...]
     for r in range(2):
         for ref, at in ((above_ref, r), (below_ref, 6 + r)):
@@ -240,9 +262,8 @@
                 main_ref[at, w * TILE : (w + 1) * TILE, :] = cells[w]
             main_ref[at, 4 * TILE : 4 * TILE + 4, :] = weights
     z = lax.axis_index("z")
-    encode(*held(main_ref, (z + 3) & 7), up_ref, 0)
-    encode(*held(main_ref, (z + 5) & 7), dn_ref, 0)
-    encode(*held(main_ref, (z + 4) & 7), far_ref, 0)
+    for ahead, out_ref in zip(FIRST, outs):
+        encode(*held(main_ref, (z + 8 + ahead) & 7), out_ref, 0)
 
 
 def step_kernel(ahead, main_ref, in_ref, out_ref):
@@ -250,9 +271,10 @@
     encode(*added(held(main_ref, at), decode(in_ref, 0)), out_ref, 0)
 
 
-def finish_kernel(main_ref, up_ref, dn_ref, far_ref, coadd_ref, cover_ref):
+def finish_kernel(main_ref, *refs):
+    ins, (coadd_ref, cover_ref) = refs[:-2], refs[-2:]
     z = lax.axis_index("z")
-    cells, weights = added(held(main_ref, z), decode(up_ref, 0), decode(dn_ref, 0), decode(far_ref, 0))
+    cells, weights = added(held(main_ref, z), *[decode(ref, 0) for ref in ins])
     lane = lax.broadcasted_iota(i32, (1, TILE), 1)
     cover = jnp.zeros((1, TILE), f32)
     for w in range(4):
@@ -271,9 +293,16 @@
         columns_kernel,
         "columns",
         (shape((BAND, BLOCKS * TILE), bf16), shape((2,), i32)),
-        [VMEM] * 4,
+        [HBM] * 4,
         (VMEM, SMEM),
-    )(psf_taps, dest_patch, dest_cell, images)
+        [
+            pltpu.VMEM((2, KTAPS), bf16),
+            pltpu.VMEM((2, COLS // TILE), i32),
+            pltpu.VMEM((2, COLS // TILE), i32),
+            pltpu.VMEM((BAND, COLS), bf16),
+            pltpu.SemaphoreType.DMA((7,)),
+        ],
+    )(*(pltpu.with_memory_space_constraint(a, pltpu.HBM) for a in (psf_taps, dest_patch, dest_cell, images)))
     matched = call(
         rows_kernel,
         "rows",
@@ -285,22 +314,25 @@
     piece = shape((PIECE, TILE), bf16)
     own = [None] * 4
     sib = [None] * 4
-    for hop in (2, 1, 3, 0):
-        stay, leave = call(
-            lambda *refs, hop=hop: warp_kernel(hop, *refs),
-            f"warp_{hop}",
-            (piece, piece),
+    for hops in HOPS:
+        outs = call(
+            lambda *refs, hops=hops: warp_kernel(hops, *refs),
+            "warp_" + "".join(str(h) for h in hops),
+            (piece,) * (2 * len(hops)),
             [SMEM] * 4 + [VMEM] * 3,
-            (VMEM, VMEM),
-            [pltpu.VMEM((2 * HALF_TILES, FRAME, TILE), bf16)],
+            (VMEM,) * (2 * len(hops)),
+            [pltpu.VMEM((2 * HALF_TILES * len(hops), FRAME, TILE), bf16)],
+            flops=WARP_COST,
         )(info, dest_patch, shift_class, exposure_weights, rows, cols, matched)
-        if hop:
-            own[hop] = lax.ppermute(stay, "x", [(i, (i + hop) % 4) for i in range(4)])
-        else:
-            own[hop] = stay
-        sib[hop] = lax.ppermute(
-            leave, ("core", "x"), [(c * 4 + i, (1 - c) * 4 + (i + hop) % 4) for c in range(2) for i in range(4)]
-        )
+        for n, hop in enumerate(hops):
+            own[hop] = outs[2 * n]
+            if hop:
+                own[hop] = lax.ppermute(own[hop], "x", [(i, (i + hop) % 4) for i in range(4)])
+            sib[hop] = lax.ppermute(
+                outs[2 * n + 1],
+                ("core", "x"),
+                [(c * 4 + i, (1 - c) * 4 + (i + hop) % 4) for c in range(2) for i in range(4)],
+            )
     held_rows = shape((8, CELLROW, TILE), f32)
     spill = shape((2 * CELLROW, TILE), i16)
     coded = shape((CELLROW, TILE), i16)
@@ -309,19 +341,27 @@
     )(*own, *sib)
     from_above = lax.ppermute(below, "y", [(i, i + 1) for i in range(3)])
     from_below = lax.ppermute(above, "y", [(i + 1, i) for i in range(3)])
-    main, up, dn, far = call(
-        merge_kernel, "merge", (held_rows, coded, coded, coded), [VMEM] * 3, (VMEM,) * 4
-    )(main, from_above, from_below)
-    far = lax.ppermute(far, "z", [(i, (i + 4) % 8) for i in range(8)])
-    for s in (2, 1, 0):
-        up = lax.ppermute(up, "z", [(i, (i + 1) % 8) for i in range(8)])
-        dn = lax.ppermute(dn, "z", [((i + 1) % 8, i) for i in range(8)])
+    main, *first = call(merge_kernel, "merge", (held_rows,) + (coded,) * len(FIRST), [VMEM] * 3, (VMEM,) * (1 + len(FIRST)))(
+        main, from_above, from_below
+    )
+
+    def along_z(block, hops):
+        return lax.ppermute(block, "z", [(i, (i + hops) % 8) for i in range(8)])
+
+    up, dn = first[:2]
+    for s in range(CHAIN - 1, -1, -1):
+        up, dn = along_z(up, 1), along_z(dn, -1)
         if s:
             up = call(lambda *refs, s=s: step_kernel(s, *refs), f"up_{s}", coded, [VMEM] * 2, VMEM)(main, up)
             dn = call(lambda *refs, s=s: step_kernel(-s, *refs), f"down_{s}", coded, [VMEM] * 2, VMEM)(main, dn)
+    far = [along_z(block, ahead) for ahead, block in zip(FIRST[2:], first[2:])]
     return call(
-        finish_kernel, "finish", (shape((1, 4, TILE, TILE), f32), shape((1, 4), f32)), [VMEM] * 4, (VMEM, VMEM)
-    )(main, up, dn, far)
+        finish_kernel,
+        "finish",
+        (shape((1, 4, TILE, TILE), f32), shape((1, 4), f32)),
+        [VMEM] * (3 + len(far)),
+        (VMEM, VMEM),
+    )(main, up, dn, *far)
 
 
 def solution(mesh):

time: 96.8 us -> 87.9 us (0.908)
  waiting for transfers between devices: 38.3 us -> 31.6 us
  local copies, waits for them, and re-layouts: 4.6 us -> 1.01 us
  starting transfers between devices: 39.8 us -> 41 us
    ppermute x14, waiting for transfers between devices: 29.7 us -> 20.5 us  [the longest x4 13.2 us: local(): lax.ppermute(outs[2 * n + 1], ('core', 'x'), [(c * 4 + i, (1 - c) * 4 + (...]
    unnamed x16 -> x10, local copies, waits for them, and re-layouts: 3.61 us -> 0.02 us
    ppermute x1, waiting for transfers between devices: 0.87 us -> 3.37 us  [local(): top = lax.ppermute(images[0, BAND - HALO:], ('y', 'x'), line)]
    pallas_call x5 -> x3, Pallas kernels: 5.98 us -> 4.48 us  [the longest x2 3.91 us: local(): call(lambda *refs, hops=hops: warp_kernel(hops, *refs), 'warp_' + ''.join...]
    ppermute x14, starting transfers between devices: 27.3 us -> 28.5 us  [the longest x7 18.6 us: along_z(): return lax.ppermute(block, 'z', [(i, (i + hops) % 8) for i in range(8)])]
    pallas_call x1, Pallas kernels: 1.9 us -> 3.01 us  [local(): call(columns_kernel, 'columns', (shape((BAND, BLOCKS * TILE), bf16), shap...]
  transfers between devices with their start and end apart: 18 -> 18, of which waited for: 10 -> 11; matrix products, arithmetic and copies ran while one was open for 0% -> 0% of each run, Pallas kernels for 7% -> 7%
where the time goes in v3:
time: 87.9 us; the launch traced here: 87.1 us
  starting transfers between devices  41 us (47%)
  waiting for transfers between devices  31.6 us (36%)
  Pallas kernels  11.9 us (14%)
  between operations  1.5 us (2%)
  local copies, waits for them, and re-layouts  1.01 us (1%)
    ppermute x7, starting transfers between devices, along_z(): return lax.ppermute(block, 'z', [(i, (i + hops) % 8) for i in range(8)])  18.6 us
    ppermute x4, waiting for transfers between devices, local(): lax.ppermute(outs[2 * n + 1], ('core', 'x'), [(c * 4 + i, (1 - c) * 4 + (...  13.2 us
    ppermute x7, waiting for transfers between devices, along_z(): return lax.ppermute(block, 'z', [(i, (i + hops) % 8) for i in range(8)])  7.24 us
    ppermute x4, starting transfers between devices, local(): lax.ppermute(outs[2 * n + 1], ('core', 'x'), [(c * 4 + i, (1 - c) * 4 + (...  6.67 us
    ppermute x1, starting transfers between devices, local(): bot = lax.ppermute(images[0, :HALO], ('y', 'x'), [(j, i) for i, j in line])  4.55 us
    ppermute x1, waiting for transfers between devices, local(): from_above = lax.ppermute(below, 'y', [(i, i + 1) for i in range(3)])  4.35 us
    pallas_call x2, Pallas kernels, local(): call(lambda *refs, hops=hops: warp_kernel(hops, *refs), 'warp_' + ''.join...  3.91 us
    ppermute x1, starting transfers between devices, local(): from_above = lax.ppermute(below, 'y', [(i, i + 1) for i in range(3)])  3.49 us
  transfers between devices with their start and end apart: 18, of which 11 were waited for; matrix products, arithmetic and copies ran while one was open for 0% of the time, Pallas kernels for 7%

profile of v3, /device:TPU:8, one launch (start us, length us, event | category | flops | bytes accessed | tf_op | source)
XLA Modules:
  0.0 87.1 jit_solution(10163868605517879766)
XLA Ops:
  1.6 4.6 %collective-permute-start.1 = (bf16[16,4096]{1,0:T(8,128)(2,1)S(1)}, bf16[16,4096]{1,0:T(8,128)(2,1)S(1)}, u32[]{:S(2)}, u32[]{:S(2)}) collective-permute-start(bf16[16,4096]{1,0:T(8,128)(2,1)S(1)} %get-tuple-element.36), channel_id=1, source_target_pairs={{1,0},{2,1},{3,2},{4,3},{5,4},{6,5},{7,6},{8,7},{9,8},{10,9},{11,1... | collective-permute-start | bytes 393224 | tf_op jit(solution)/shard_map/ppermute | solution.py:290
  6.2 1.9 %collective-permute-start = (bf16[16,4096]{1,0:T(8,128)(2,1)S(1)}, bf16[16,4096]{1,0:T(8,128)(2,1)S(1)}, u32[]{:S(2)}, u32[]{:S(2)}) collective-permute-start(bf16[16,4096]{1,0:T(8,128)(2,1)S(1)} %get-tuple-element.37), channel_id=1, source_target_pairs={{0,1},{1,2},{2,3},{3,4},{4,5},{5,6},{6,7},{7,8},{8,9},{9,10},{10,1... | collective-permute-start | bytes 393224 | tf_op jit(solution)/shard_map/ppermute | solution.py:289
  8.8 3.0 %columns.1 = (bf16[256,4224]{1,0:T(8,128)(2,1)S(1)}, s32[2]{0:T(128)S(1)}) custom-call(bf16[1,2,13]{2,1,0:T(2,128)(2,1)} %taps_ref.1, s32[1,2,32]{2,1,0:T(2,128)} %refs_1_.3, s32[1,2,32]{2,1,0:T(2,128)} %cell_hbm.1, bf16[1,256,4096]{2,1,0:T(8,128)(2,1)} %img_hbm.1), custom_call_target="tpu_custom_call" | custom-call | tf_op jit(solution)/shard_map/columns/pallas_call | solution.py:292
  11.8 3.4 %collective-permute-done.top_ref = bf16[16,4096]{1,0:T(8,128)(2,1)S(1)} collective-permute-done((bf16[16,4096]{1,0:T(8,128)(2,1)S(1)}, bf16[16,4096]{1,0:T(8,128)(2,1)S(1)}, u32[]{:S(2)}, u32[]{:S(2)}) %collective-permute-start) | collective-permute-done | bytes 131104 | tf_op jit(solution)/shard_map/ppermute | solution.py:289
  15.2 1.4 %rows.1.refs_6_ = bf16[2,144,4224]{2,1,0:T(8,128)(2,1)S(1)} custom-call(bf16[1,2,13]{2,1,0:T(2,128)(2,1)S(1)} %copy-done.4, bf16[16,4096]{1,0:T(8,128)(2,1)S(1)} %collective-permute-done.top_ref, bf16[16,4096]{1,0:T(8,128)(2,1)S(1)} %collective-permute-done.1.bot_ref, bf16[256,4224]{1,0:T(8,128)(2,1)S(1)} %get-tuple-element.20.passed_ref), custom_call_target="tpu_custom_call" | custom-call | tf_op jit(solution)/shard_map/rows/pallas_call | solution.py:306
  16.6 2.0 %warp_13.1 = (bf16[1056,128]{1,0:T(8,128)(2,1)S(1)}, bf16[1056,128]{1,0:T(8,128)(2,1)S(1)}, bf16[1056,128]{1,0:T(8,128)(2,1)S(1)}, bf16[1056,128]{1,0:T(8,128)(2,1)S(1)}) custom-call(s32[2]{0:T(128)S(1)} %get-tuple-element.19.refs_0_, s32[1,2,32]{2,1,0:T(2,128)S(1)} %copy-done.2, s32[1,2,2,32]{3,2,1,0:T(2,128)S(1)} %copy-done.3, f32[1]{0:T(128)S(6)} %copy.10.refs_3_, ...), custom_call_target="tpu_custom_call" | custom-call | tf_op jit(solution)/shard_map/warp_13/pallas_call | solution.py:318
  18.7 3.2 %collective-permute-start.4 = (bf16[1056,128]{1,0:T(8,128)(2,1)S(1)}, bf16[1056,128]{1,0:T(8,128)(2,1)S(1)}, u32[]{:S(2)}, u32[]{:S(2)}) collective-permute-start(bf16[1056,128]{1,0:T(8,128)(2,1)S(1)} %get-tuple-element.24), channel_id=1, source_target_pairs={{0,3},{1,0},{2,1},{3,2},{4,7},{5,4},{6,5},{7,6},{8,11},{9,8},{10,9... | collective-permute-start | bytes 811016 | tf_op jit(solution)/shard_map/ppermute | solution.py:330
  21.9 2.0 %warp_20.1 = (bf16[1056,128]{1,0:T(8,128)(2,1)S(1)}, bf16[1056,128]{1,0:T(8,128)(2,1)S(1)}, bf16[1056,128]{1,0:T(8,128)(2,1)S(1)}, bf16[1056,128]{1,0:T(8,128)(2,1)S(1)}) custom-call(s32[2]{0:T(128)S(1)} %get-tuple-element.19.refs_0_, s32[1,2,32]{2,1,0:T(2,128)S(1)} %copy-done.2, s32[1,2,2,32]{3,2,1,0:T(2,128)S(1)} %copy-done.3, f32[1]{0:T(128)S(6)} %copy.10.refs_3_, ...), custom_call_target="tpu_custom_call" | custom-call | tf_op jit(solution)/shard_map/warp_20/pallas_call | solution.py:318
  24.0 2.9 %collective-permute-start.8 = (bf16[1056,128]{1,0:T(8,128)(2,1)S(1)}, bf16[1056,128]{1,0:T(8,128)(2,1)S(1)}, u32[]{:S(2)}, u32[]{:S(2)}) collective-permute-start(bf16[1056,128]{1,0:T(8,128)(2,1)S(1)} %get-tuple-element.28), channel_id=1, source_target_pairs={{0,19},{1,16},{2,17},{3,18},{16,3},{17,0},{18,1},{19,2},{4,23},{5,... | collective-permute-start | bytes 811016 | tf_op jit(solution)/shard_map/ppermute | solution.py:331
  26.9 3.6 %collective-permute-start.7 = (bf16[1056,128]{1,0:T(8,128)(2,1)S(1)}, bf16[1056,128]{1,0:T(8,128)(2,1)S(1)}, u32[]{:S(2)}, u32[]{:S(2)}) collective-permute-start(bf16[1056,128]{1,0:T(8,128)(2,1)S(1)} %get-tuple-element.27), channel_id=1, source_target_pairs={{0,18},{1,19},{2,16},{3,17},{16,2},{17,3},{18,0},{19,1},{4,22},{5,... | collective-permute-start | bytes 811016 | tf_op jit(solution)/shard_map/ppermute | solution.py:331
  30.6 2.1 %collective-permute-done.6.refs_5_ = bf16[1056,128]{1,0:T(8,128)(2,1)S(1)} collective-permute-done((bf16[1056,128]{1,0:T(8,128)(2,1)S(1)}, bf16[1056,128]{1,0:T(8,128)(2,1)S(1)}, u32[]{:S(2)}, u32[]{:S(2)}) %collective-permute-start.6) | collective-permute-done | bytes 270368 | tf_op jit(solution)/shard_map/ppermute | solution.py:331
  32.7 10.7 %collective-permute-done.8.refs_7_ = bf16[1056,128]{1,0:T(8,128)(2,1)S(1)} collective-permute-done((bf16[1056,128]{1,0:T(8,128)(2,1)S(1)}, bf16[1056,128]{1,0:T(8,128)(2,1)S(1)}, u32[]{:S(2)}, u32[]{:S(2)}) %collective-permute-start.8) | collective-permute-done | bytes 270368 | tf_op jit(solution)/shard_map/ppermute | solution.py:331
  45.2 3.5 %collective-permute-start.9 = (s16[1056,128]{1,0:T(8,128)(2,1)S(1)}, s16[1056,128]{1,0:T(8,128)(2,1)S(1)}, u32[]{:S(2)}, u32[]{:S(2)}) collective-permute-start(s16[1056,128]{1,0:T(8,128)(2,1)S(1)} %get-tuple-element.30), channel_id=1, source_target_pairs={{0,4},{4,8},{8,12},{1,5},{5,9},{9,13},{2,6},{6,10},{10,14},{3,7},{... | collective-permute-start | bytes 811016 | tf_op jit(solution)/shard_map/ppermute | solution.py:342
  48.7 2.5 %collective-permute-start.10 = (s16[1056,128]{1,0:T(8,128)(2,1)S(1)}, s16[1056,128]{1,0:T(8,128)(2,1)S(1)}, u32[]{:S(2)}, u32[]{:S(2)}) collective-permute-start(s16[1056,128]{1,0:T(8,128)(2,1)S(1)} %get-tuple-element.31), channel_id=1, source_target_pairs={{4,0},{8,4},{12,8},{5,1},{9,5},{13,9},{6,2},{10,6},{14,10},{7,3},{... | collective-permute-start | bytes 811016 | tf_op jit(solution)/shard_map/ppermute | solution.py:343
  51.3 4.3 %collective-permute-done.9.above_ref = s16[1056,128]{1,0:T(8,128)(2,1)S(1)} collective-permute-done((s16[1056,128]{1,0:T(8,128)(2,1)S(1)}, s16[1056,128]{1,0:T(8,128)(2,1)S(1)}, u32[]{:S(2)}, u32[]{:S(2)}) %collective-permute-start.9) | collective-permute-done | bytes 270368 | tf_op jit(solution)/shard_map/ppermute | solution.py:342
  55.6 3.4 %collective-permute-done.10.below_ref = s16[1056,128]{1,0:T(8,128)(2,1)S(1)} collective-permute-done((s16[1056,128]{1,0:T(8,128)(2,1)S(1)}, s16[1056,128]{1,0:T(8,128)(2,1)S(1)}, u32[]{:S(2)}, u32[]{:S(2)}) %collective-permute-start.10) | collective-permute-done | bytes 270368 | tf_op jit(solution)/shard_map/ppermute | solution.py:343
  59.6 2.0 %collective-permute-start.11 = (s16[528,128]{1,0:T(8,128)(2,1)S(1)}, s16[528,128]{1,0:T(8,128)(2,1)S(1)}, u32[]{:S(2)}, u32[]{:S(2)}) collective-permute-start(s16[528,128]{1,0:T(8,128)(2,1)S(1)} %get-tuple-element.33), channel_id=1, source_target_pairs={{0,32},{32,64},{64,96},{96,128},{128,160},{160,192},{192,224},{224... | collective-permute-start | bytes 405512 | tf_op jit(solution)/shard_map/ppermute | solution.py:349
  61.7 4.0 %collective-permute-start.14 = (s16[528,128]{1,0:T(8,128)(2,1)S(1)}, s16[528,128]{1,0:T(8,128)(2,1)S(1)}, u32[]{:S(2)}, u32[]{:S(2)}) collective-permute-start(s16[528,128]{1,0:T(8,128)(2,1)S(1)} %get-tuple-element.34), channel_id=1, source_target_pairs={{0,224},{32,0},{64,32},{96,64},{128,96},{160,128},{192,160},{224,1... | collective-permute-start | bytes 405512 | tf_op jit(solution)/shard_map/ppermute | solution.py:349
  65.7 2.9 %collective-permute-done.11.refs_1_ = s16[528,128]{1,0:T(8,128)(2,1)S(1)} collective-permute-done((s16[528,128]{1,0:T(8,128)(2,1)S(1)}, s16[528,128]{1,0:T(8,128)(2,1)S(1)}, u32[]{:S(2)}, u32[]{:S(2)}) %collective-permute-start.11) | collective-permute-done | bytes 135200 | tf_op jit(solution)/shard_map/ppermute | solution.py:349
  69.1 3.3 %collective-permute-start.15 = (s16[528,128]{1,0:T(8,128)(2,1)S(1)}, s16[528,128]{1,0:T(8,128)(2,1)S(1)}, u32[]{:S(2)}, u32[]{:S(2)}) collective-permute-start(s16[528,128]{1,0:T(8,128)(2,1)S(1)} %down_2.1), channel_id=1, source_target_pairs={{0,224},{32,0},{64,32},{96,64},{128,96},{160,128},{192,160},{224,1... | collective-permute-start | bytes 405512 | tf_op jit(solution)/shard_map/ppermute | solution.py:349
  72.4 4.5 %collective-permute-start.17 = (s16[528,128]{1,0:T(8,128)(2,1)S(1)}, s16[528,128]{1,0:T(8,128)(2,1)S(1)}, u32[]{:S(2)}, u32[]{:S(2)}) collective-permute-start(s16[528,128]{1,0:T(8,128)(2,1)S(1)} %get-tuple-element.35), channel_id=1, source_target_pairs={{0,128},{32,160},{64,192},{96,224},{128,0},{160,32},{192,64},{224,... | collective-permute-start | bytes 405512 | tf_op jit(solution)/shard_map/ppermute | solution.py:349
  77.2 1.8 %collective-permute-done.15.refs_1_ = s16[528,128]{1,0:T(8,128)(2,1)S(1)} collective-permute-done((s16[528,128]{1,0:T(8,128)(2,1)S(1)}, s16[528,128]{1,0:T(8,128)(2,1)S(1)}, u32[]{:S(2)}, u32[]{:S(2)}) %collective-permute-start.15) | collective-permute-done | bytes 135200 | tf_op jit(solution)/shard_map/ppermute | solution.py:349
  79.2 4.5 %collective-permute-start.16 = (s16[528,128]{1,0:T(8,128)(2,1)S(1)}, s16[528,128]{1,0:T(8,128)(2,1)S(1)}, u32[]{:S(2)}, u32[]{:S(2)}) collective-permute-start(s16[528,128]{1,0:T(8,128)(2,1)S(1)} %down_1.1), channel_id=1, source_target_pairs={{0,224},{32,0},{64,32},{96,64},{128,96},{160,128},{192,160},{224,1... | collective-permute-start | bytes 405512 | tf_op jit(solution)/shard_map/ppermute | solution.py:349
  84.2 2.1 %collective-permute-done.16.refs_1_ = s16[528,128]{1,0:T(8,128)(2,1)S(1)} collective-permute-done((s16[528,128]{1,0:T(8,128)(2,1)S(1)}, s16[528,128]{1,0:T(8,128)(2,1)S(1)}, u32[]{:S(2)}, u32[]{:S(2)}) %collective-permute-start.16) | collective-permute-done | bytes 135200 | tf_op jit(solution)/shard_map/ppermute | solution.py:349
  (34 shorter events, 5.9 us)
Async XLA Ops:
  0.6 14.5 %copy-start.4 = (bf16[1,2,13]{2,1,0:T(2,128)(2,1)S(1)}, bf16[1,2,13]{2,1,0:T(2,128)(2,1)}, u32[]{:S(2)}) copy-start(bf16[1,2,13]{2,1,0:T(2,128)(2,1)} %taps_ref.1) | copy-start | bytes 160
  1.6 10.2 %collective-permute-start.1 = (bf16[16,4096]{1,0:T(8,128)(2,1)S(1)}, bf16[16,4096]{1,0:T(8,128)(2,1)S(1)}, u32[]{:S(2)}, u32[]{:S(2)}) collective-permute-start(bf16[16,4096]{1,0:T(8,128)(2,1)S(1)} %get-tuple-element.36), channel_id=1, source_target_pairs={{1,0},{2,1},{3,2},{4,3},{5,4},{6,5},{7,6},{8,7},{9,8},{10,9},{11,1... | collective-permute-start | bytes 393224 | tf_op jit(solution)/shard_map/ppermute | solution.py:290
  6.2 9.0 %collective-permute-start = (bf16[16,4096]{1,0:T(8,128)(2,1)S(1)}, bf16[16,4096]{1,0:T(8,128)(2,1)S(1)}, u32[]{:S(2)}, u32[]{:S(2)}) collective-permute-start(bf16[16,4096]{1,0:T(8,128)(2,1)S(1)} %get-tuple-element.37), channel_id=1, source_target_pairs={{0,1},{1,2},{2,3},{3,4},{4,5},{5,6},{6,7},{7,8},{8,9},{9,10},{10,1... | collective-permute-start | bytes 393224 | tf_op jit(solution)/shard_map/ppermute | solution.py:289
  15.2 1.4 %copy-start = (bf16[9,128,144]{2,1,0:T(8,128)(2,1)S(1)}, bf16[9,128,144]{2,1,0:T(8,128)(2,1)}, u32[]{:S(2)}) copy-start(bf16[9,128,144]{2,1,0:T(8,128)(2,1)} %constant.4.clone.refs_4_) | copy-start | bytes 995332
  15.2 1.4 %copy-start.1 = (bf16[8,256,128]{2,1,0:T(8,128)(2,1)S(1)}, bf16[8,256,128]{2,1,0:T(8,128)(2,1)}, u32[]{:S(2)}) copy-start(bf16[8,256,128]{2,1,0:T(8,128)(2,1)} %constant.5.clone.refs_5_) | copy-start | bytes 1572868
  15.2 1.5 %copy-start.2 = (s32[1,2,32]{2,1,0:T(2,128)S(1)}, s32[1,2,32]{2,1,0:T(2,128)}, u32[]{:S(2)}) copy-start(s32[1,2,32]{2,1,0:T(2,128)} %refs_1_.3) | copy-start | bytes 772
  15.2 1.5 %copy-start.3 = (s32[1,2,2,32]{3,2,1,0:T(2,128)S(1)}, s32[1,2,2,32]{3,2,1,0:T(2,128)}, u32[]{:S(2)}) copy-start(s32[1,2,2,32]{3,2,1,0:T(2,128)} %refs_2_.3) | copy-start | bytes 1540
  18.6 8.3 %collective-permute-start.2 = (bf16[1056,128]{1,0:T(8,128)(2,1)S(1)}, bf16[1056,128]{1,0:T(8,128)(2,1)S(1)}, u32[]{:S(2)}, u32[]{:S(2)}) collective-permute-start(bf16[1056,128]{1,0:T(8,128)(2,1)S(1)} %get-tuple-element.22), channel_id=1, source_target_pairs={{0,1},{1,2},{2,3},{3,0},{4,5},{5,6},{6,7},{7,4},{8,9},{9,10},{10,1... | collective-permute-start | bytes 811016 | tf_op jit(solution)/shard_map/ppermute | solution.py:330
  18.7 8.2 %collective-permute-start.4 = (bf16[1056,128]{1,0:T(8,128)(2,1)S(1)}, bf16[1056,128]{1,0:T(8,128)(2,1)S(1)}, u32[]{:S(2)}, u32[]{:S(2)}) collective-permute-start(bf16[1056,128]{1,0:T(8,128)(2,1)S(1)} %get-tuple-element.24), channel_id=1, source_target_pairs={{0,3},{1,0},{2,1},{3,2},{4,7},{5,4},{6,5},{7,6},{8,11},{9,8},{10,9... | collective-permute-start | bytes 811016 | tf_op jit(solution)/shard_map/ppermute | solution.py:330
  23.9 8.8 %collective-permute-start.6 = (bf16[1056,128]{1,0:T(8,128)(2,1)S(1)}, bf16[1056,128]{1,0:T(8,128)(2,1)S(1)}, u32[]{:S(2)}, u32[]{:S(2)}) collective-permute-start(bf16[1056,128]{1,0:T(8,128)(2,1)S(1)} %get-tuple-element.26), channel_id=1, source_target_pairs={{0,17},{1,18},{2,19},{3,16},{16,1},{17,2},{18,3},{19,0},{4,21},{5,... | collective-permute-start | bytes 811016 | tf_op jit(solution)/shard_map/ppermute | solution.py:331
  24.0 19.4 %collective-permute-start.8 = (bf16[1056,128]{1,0:T(8,128)(2,1)S(1)}, bf16[1056,128]{1,0:T(8,128)(2,1)S(1)}, u32[]{:S(2)}, u32[]{:S(2)}) collective-permute-start(bf16[1056,128]{1,0:T(8,128)(2,1)S(1)} %get-tuple-element.28), channel_id=1, source_target_pairs={{0,19},{1,16},{2,17},{3,18},{16,3},{17,0},{18,1},{19,2},{4,23},{5,... | collective-permute-start | bytes 811016 | tf_op jit(solution)/shard_map/ppermute | solution.py:331
  26.9 16.5 %collective-permute-start.3 = (bf16[1056,128]{1,0:T(8,128)(2,1)S(1)}, bf16[1056,128]{1,0:T(8,128)(2,1)S(1)}, u32[]{:S(2)}, u32[]{:S(2)}) collective-permute-start(bf16[1056,128]{1,0:T(8,128)(2,1)S(1)} %get-tuple-element.23), channel_id=1, source_target_pairs={{0,2},{1,3},{2,0},{3,1},{4,6},{5,7},{6,4},{7,5},{8,10},{9,11},{10,... | collective-permute-start | bytes 811016 | tf_op jit(solution)/shard_map/ppermute | solution.py:330
  26.9 16.5 %collective-permute-start.5 = (bf16[1056,128]{1,0:T(8,128)(2,1)S(1)}, bf16[1056,128]{1,0:T(8,128)(2,1)S(1)}, u32[]{:S(2)}, u32[]{:S(2)}) collective-permute-start(bf16[1056,128]{1,0:T(8,128)(2,1)S(1)} %get-tuple-element.25), channel_id=1, source_target_pairs={{0,16},{1,17},{2,18},{3,19},{16,0},{17,1},{18,2},{19,3},{4,20},{5,... | collective-permute-start | bytes 811016 | tf_op jit(solution)/shard_map/ppermute | solution.py:331
  26.9 16.9 %collective-permute-start.7 = (bf16[1056,128]{1,0:T(8,128)(2,1)S(1)}, bf16[1056,128]{1,0:T(8,128)(2,1)S(1)}, u32[]{:S(2)}, u32[]{:S(2)}) collective-permute-start(bf16[1056,128]{1,0:T(8,128)(2,1)S(1)} %get-tuple-element.27), channel_id=1, source_target_pairs={{0,18},{1,19},{2,16},{3,17},{16,2},{17,3},{18,0},{19,1},{4,22},{5,... | collective-permute-start | bytes 811016 | tf_op jit(solution)/shard_map/ppermute | solution.py:331
  45.2 10.4 %collective-permute-start.9 = (s16[1056,128]{1,0:T(8,128)(2,1)S(1)}, s16[1056,128]{1,0:T(8,128)(2,1)S(1)}, u32[]{:S(2)}, u32[]{:S(2)}) collective-permute-start(s16[1056,128]{1,0:T(8,128)(2,1)S(1)} %get-tuple-element.30), channel_id=1, source_target_pairs={{0,4},{4,8},{8,12},{1,5},{5,9},{9,13},{2,6},{6,10},{10,14},{3,7},{... | collective-permute-start | bytes 811016 | tf_op jit(solution)/shard_map/ppermute | solution.py:342
  48.7 10.3 %collective-permute-start.10 = (s16[1056,128]{1,0:T(8,128)(2,1)S(1)}, s16[1056,128]{1,0:T(8,128)(2,1)S(1)}, u32[]{:S(2)}, u32[]{:S(2)}) collective-permute-start(s16[1056,128]{1,0:T(8,128)(2,1)S(1)} %get-tuple-element.31), channel_id=1, source_target_pairs={{4,0},{8,4},{12,8},{5,1},{9,5},{13,9},{6,2},{10,6},{14,10},{7,3},{... | collective-permute-start | bytes 811016 | tf_op jit(solution)/shard_map/ppermute | solution.py:343
  59.6 9.0 %collective-permute-start.11 = (s16[528,128]{1,0:T(8,128)(2,1)S(1)}, s16[528,128]{1,0:T(8,128)(2,1)S(1)}, u32[]{:S(2)}, u32[]{:S(2)}) collective-permute-start(s16[528,128]{1,0:T(8,128)(2,1)S(1)} %get-tuple-element.33), channel_id=1, source_target_pairs={{0,32},{32,64},{64,96},{96,128},{128,160},{160,192},{192,224},{224... | collective-permute-start | bytes 405512 | tf_op jit(solution)/shard_map/ppermute | solution.py:349
  61.7 7.2 %collective-permute-start.14 = (s16[528,128]{1,0:T(8,128)(2,1)S(1)}, s16[528,128]{1,0:T(8,128)(2,1)S(1)}, u32[]{:S(2)}, u32[]{:S(2)}) collective-permute-start(s16[528,128]{1,0:T(8,128)(2,1)S(1)} %get-tuple-element.34), channel_id=1, source_target_pairs={{0,224},{32,0},{64,32},{96,64},{128,96},{160,128},{192,160},{224,1... | collective-permute-start | bytes 405512 | tf_op jit(solution)/shard_map/ppermute | solution.py:349
  68.8 8.1 %collective-permute-start.12 = (s16[528,128]{1,0:T(8,128)(2,1)S(1)}, s16[528,128]{1,0:T(8,128)(2,1)S(1)}, u32[]{:S(2)}, u32[]{:S(2)}) collective-permute-start(s16[528,128]{1,0:T(8,128)(2,1)S(1)} %up_2.1), channel_id=1, source_target_pairs={{0,32},{32,64},{64,96},{96,128},{128,160},{160,192},{192,224},{224... | collective-permute-start | bytes 405512 | tf_op jit(solution)/shard_map/ppermute | solution.py:349
  69.1 9.9 %collective-permute-start.15 = (s16[528,128]{1,0:T(8,128)(2,1)S(1)}, s16[528,128]{1,0:T(8,128)(2,1)S(1)}, u32[]{:S(2)}, u32[]{:S(2)}) collective-permute-start(s16[528,128]{1,0:T(8,128)(2,1)S(1)} %down_2.1), channel_id=1, source_target_pairs={{0,224},{32,0},{64,32},{96,64},{128,96},{160,128},{192,160},{224,1... | collective-permute-start | bytes 405512 | tf_op jit(solution)/shard_map/ppermute | solution.py:349
  72.4 11.4 %collective-permute-start.17 = (s16[528,128]{1,0:T(8,128)(2,1)S(1)}, s16[528,128]{1,0:T(8,128)(2,1)S(1)}, u32[]{:S(2)}, u32[]{:S(2)}) collective-permute-start(s16[528,128]{1,0:T(8,128)(2,1)S(1)} %get-tuple-element.35), channel_id=1, source_target_pairs={{0,128},{32,160},{64,192},{96,224},{128,0},{160,32},{192,64},{224,... | collective-permute-start | bytes 405512 | tf_op jit(solution)/shard_map/ppermute | solution.py:349
  77.1 7.0 %collective-permute-start.13 = (s16[528,128]{1,0:T(8,128)(2,1)S(1)}, s16[528,128]{1,0:T(8,128)(2,1)S(1)}, u32[]{:S(2)}, u32[]{:S(2)}) collective-permute-start(s16[528,128]{1,0:T(8,128)(2,1)S(1)} %up_1.1), channel_id=1, source_target_pairs={{0,32},{32,64},{64,96},{96,128},{128,160},{160,192},{192,224},{224... | collective-permute-start | bytes 405512 | tf_op jit(solution)/shard_map/ppermute | solution.py:349
  79.2 7.1 %collective-permute-start.16 = (s16[528,128]{1,0:T(8,128)(2,1)S(1)}, s16[528,128]{1,0:T(8,128)(2,1)S(1)}, u32[]{:S(2)}, u32[]{:S(2)}) collective-permute-start(s16[528,128]{1,0:T(8,128)(2,1)S(1)} %down_1.1), channel_id=1, source_target_pairs={{0,224},{32,0},{64,32},{96,64},{128,96},{160,128},{192,160},{224,1... | collective-permute-start | bytes 405512 | tf_op jit(solution)/shard_map/ppermute | solution.py:349

commit v4 on v3

--- a/solution.py
+++ b/solution.py
@@ -24,7 +24,6 @@
 CELLROW = 4 * TILE + 16
 TOP_CODE = 32000.0
 HOPS = ((1, 3), (2, 0))
-WARP_COST = 0
 CHAIN = 3
 FIRST = (CHAIN, -CHAIN, 4) + tuple(sign * d for d in range(CHAIN + 1, 4) for sign in (1, -1))
 f32 = jnp.float32
@@ -36,7 +35,7 @@
 HBM = pl.BlockSpec(memory_space=pltpu.HBM)
 
 
-def call(kernel, name, out_shape, in_specs, out_specs, scratch=(), mib=8, flops=0):
+def call(kernel, name, out_shape, in_specs, out_specs, scratch=(), mib=8):
     return pl.pallas_call(
         kernel,
         out_shape=out_shape,
@@ -44,7 +43,7 @@
         out_specs=out_specs,
         scratch_shapes=scratch,
         compiler_params=pltpu.CompilerParams(vmem_limit_bytes=mib * 2**20),
-        cost_estimate=pl.CostEstimate(flops=flops, transcendentals=0, bytes_accessed=0) if flops else None,
+        cost_estimate=pl.CostEstimate(flops=1, transcendentals=0, bytes_accessed=1),
         name=name,
     )
 
@@ -110,22 +109,25 @@
         out_ref[:, b * TILE : (b + 1) * TILE] = jnp.dot(window, weights, preferred_element_type=f32).astype(bf16)
 
 
-def rows_kernel(taps_ref, top_ref, bot_ref, passed_ref, out_ref, window_ref, edge_ref):
+def rows_kernel(taps_ref, outer_ref, inner_ref, passed_ref, out_ref, window_ref, edge_ref):
     patch = lax.axis_index("y") * 4 + lax.axis_index("x")
     taps = taps_ref[0].astype(f32)
     over_cols = banded(taps[1:2], (2 * TILE, TILE), 0).astype(bf16)
     halo = 2 * HALO
-    for b in range(BLOCKS):
-        for side in range(2):
-            k = b - 1 + side
-            at = (slice(b * halo, b * halo + HALO), slice(side * TILE, (side + 1) * TILE))
-            at_bot = (slice(b * halo + HALO, (b + 1) * halo), at[1])
-            if 0 <= k < BLOCKS - 1:
-                window_ref[at] = top_ref[:, k * TILE : (k + 1) * TILE]
-                window_ref[at_bot] = bot_ref[:, k * TILE : (k + 1) * TILE]
-            else:
-                window_ref[at] = jnp.zeros((HALO, TILE), bf16)
-                window_ref[at_bot] = jnp.zeros((HALO, TILE), bf16)
+    for odd, top_ref, bot_ref in ((0, outer_ref, inner_ref), (1, inner_ref, outer_ref)):
+
+        @pl.when((patch & 1) == odd)
+        def _(top_ref=top_ref, bot_ref=bot_ref):
+            for b in range(BLOCKS):
+                for side in range(2):
+                    k = b - 1 + side
+                    for n, ref in enumerate((top_ref, bot_ref)):
+                        rows = jnp.zeros((HALO, TILE), bf16)
+                        if 0 <= k < BLOCKS - 1:
+                            rows = ref[:, k * TILE : (k + 1) * TILE]
+                        first = b * halo + n * HALO
+                        window_ref[first : first + HALO, side * TILE : (side + 1) * TILE] = rows
+
     lane = lax.broadcasted_iota(i32, (halo, TILE), 1)
     for part in range(3):
         each = BLOCKS // 3
@@ -230,37 +232,59 @@
     return cells, sum(p[1] for p in parts[1:]) + parts[0][1]
 
 
-def place_kernel(*refs):
-    pieces = refs[:8]
-    main_ref, above_ref, below_ref, rows_ref = refs[8:]
+def spread(piece, rows_ref, where):
+    notes = piece[HALF_TILES * TILE :, :].astype(f32)
+    weights = notes[0:8] + notes[8:16] + notes[16:24]
+    down = jnp.max(notes[24:32]).astype(i32)
+    for r in range(2):
+        at = where(r, r + down)
+        for w in range(4):
+            slot = r * 4 + w
+            tile = piece[slot * TILE : (slot + 1) * TILE, :].astype(f32)
+            rows_ref[at, w * TILE : (w + 1) * TILE, :] += weights[slot : slot + 1] * tile
+        rows_ref[at, 4 * TILE : 4 * TILE + 4, :] += weights[r * 4 : r * 4 + 4]
+
+
+def spill_kernel(hops, *refs):
+    pieces, out_ref, rows_ref = refs[:4], refs[4], refs[5]
     x = lax.axis_index("x")
     rows_ref[...] = jnp.zeros(rows_ref.shape, f32)
+    for n, hop in enumerate(sorted(set(hops))):
+        mine = [i for i in range(4) if hops[i] == hop]
+        band = (x + 4 - hop) & 3
+
+        def where(r, row, band=band):
+            slot = jnp.where(band == 0, row + 2, row - 2)
+            return jnp.where((slot >= 0) & (slot < 2), slot, 2 + r)
+
+        @pl.when((x == mine[0]) | (x == mine[1]))
+        def _(n=n, where=where):
+            for piece in pieces[2 * n : 2 * n + 2]:
+                spread(piece, rows_ref, where)
+
+    for r in range(2):
+        encode(*held(rows_ref, r), out_ref, r * CELLROW)
+
+
+def place_kernel(*refs):
+    pieces, main_ref, rows_ref = refs[:8], refs[8], refs[9]
+    rows_ref[...] = jnp.zeros(rows_ref.shape, f32)
     for n, piece in enumerate(pieces):
-        band = (x + 4 - n % 4) & 3
-        notes = piece[HALF_TILES * TILE :, :].astype(f32)
-        weights = notes[0:8] + notes[8:16] + notes[16:24]
-        down = jnp.max(notes[24:32]).astype(i32)
+        band = (lax.axis_index("x") + 4 - n % 4) & 3
+        spread(piece, rows_ref, lambda r, row: 2 * band + row + 2)
+    main_ref[...] = rows_ref[2:10]
+
+
+def merge_kernel(in_ref, *refs):
+    spills, main_ref, outs = refs[:2], refs[2], refs[3:]
+    main_ref[...] = in_ref[...]
+    for n, ref in enumerate(spills):
+        first = jnp.where((lax.axis_index("x") & 1) == n, 0, 6)
         for r in range(2):
-            at = 2 * band + r + down + 2
+            cells, weights = added(held(main_ref, first + r), decode(ref, r * CELLROW))
             for w in range(4):
-                slot = r * 4 + w
-                tile = piece[slot * TILE : (slot + 1) * TILE, :].astype(f32)
-                rows_ref[at, w * TILE : (w + 1) * TILE, :] += weights[slot : slot + 1] * tile
-            rows_ref[at, 4 * TILE : 4 * TILE + 4, :] += weights[r * 4 : r * 4 + 4]
-    for r in range(2):
-        encode(*held(rows_ref, r), above_ref, r * CELLROW)
-        encode(*held(rows_ref, 10 + r), below_ref, r * CELLROW)
-    main_ref[...] = rows_ref[2:10]
-
-
-def merge_kernel(in_ref, above_ref, below_ref, main_ref, *outs):
-    main_ref[...] = in_ref[...]
-    for r in range(2):
-        for ref, at in ((above_ref, r), (below_ref, 6 + r)):
-            cells, weights = added(held(in_ref, at), decode(ref, r * CELLROW))
-            for w in range(4):
-                main_ref[at, w * TILE : (w + 1) * TILE, :] = cells[w]
-            main_ref[at, 4 * TILE : 4 * TILE + 4, :] = weights
+                main_ref[first + r, w * TILE : (w + 1) * TILE, :] = cells[w]
+            main_ref[first + r, 4 * TILE : 4 * TILE + 4, :] = weights
     z = lax.axis_index("z")
     for ahead, out_ref in zip(FIRST, outs):
         encode(*held(main_ref, (z + 8 + ahead) & 7), out_ref, 0)
@@ -285,9 +309,11 @@
 
 def local(images, psf_taps, exposure_weights, dest_patch, dest_cell, shift_class):
     shape = jax.ShapeDtypeStruct
-    line = [(i, i + 1) for i in range(15)]
-    top = lax.ppermute(images[0, BAND - HALO :], ("y", "x"), line)
-    bot = lax.ppermute(images[0, :HALO], ("y", "x"), [(j, i) for i, j in line])
+    edge = (BAND - HALO) * (lax.axis_index("x") & 1)
+    outer = lax.dynamic_slice_in_dim(images[0], edge, HALO)
+    inner = lax.dynamic_slice_in_dim(images[0], BAND - HALO - edge, HALO)
+    outer = lax.ppermute(outer, ("y", "x"), [p for i in range(1, 14, 2) for p in ((i, i + 1), (i + 1, i))])
+    inner = lax.ppermute(inner, ("y", "x"), [p for i in range(0, 15, 2) for p in ((i, i + 1), (i + 1, i))])
     rows, cols = (jnp.asarray(t) for t in lanczos_tables())
     passed, info = call(
         columns_kernel,
@@ -310,7 +336,7 @@
         [VMEM] * 4,
         VMEM,
         [pltpu.VMEM((BLOCKS * 2 * HALO, 2 * TILE), bf16), pltpu.VMEM((2 * HALO, BLOCKS * TILE), bf16)],
-    )(psf_taps, top, bot, passed)
+    )(psf_taps, outer, inner, passed)
     piece = shape((PIECE, TILE), bf16)
     own = [None] * 4
     sib = [None] * 4
@@ -322,7 +348,6 @@
             [SMEM] * 4 + [VMEM] * 3,
             (VMEM,) * (2 * len(hops)),
             [pltpu.VMEM((2 * HALF_TILES * len(hops), FRAME, TILE), bf16)],
-            flops=WARP_COST,
         )(info, dest_patch, shift_class, exposure_weights, rows, cols, matched)
         for n, hop in enumerate(hops):
             own[hop] = outs[2 * n]
@@ -336,14 +361,23 @@
     held_rows = shape((8, CELLROW, TILE), f32)
     spill = shape((2 * CELLROW, TILE), i16)
     coded = shape((CELLROW, TILE), i16)
-    main, above, below = call(
-        place_kernel, "place", (held_rows, spill, spill), [VMEM] * 8, (VMEM,) * 3, [pltpu.VMEM((12, CELLROW, TILE), f32)]
-    )(*own, *sib)
-    from_above = lax.ppermute(below, "y", [(i, i + 1) for i in range(3)])
-    from_below = lax.ppermute(above, "y", [(i + 1, i) for i in range(3)])
-    main, *first = call(merge_kernel, "merge", (held_rows,) + (coded,) * len(FIRST), [VMEM] * 3, (VMEM,) * (1 + len(FIRST)))(
-        main, from_above, from_below
-    )
+    spills = []
+    for n, hops in enumerate(((1, 1, 3, 3), (0, 2, 2, 0))):
+        out = call(
+            lambda *refs, hops=hops: spill_kernel(hops, *refs),
+            f"spill_{n}",
+            spill,
+            [VMEM] * 4,
+            VMEM,
+            [pltpu.VMEM((4, CELLROW, TILE), f32)],
+        )(*(piece for hop in sorted(set(hops)) for piece in (own[hop], sib[hop])))
+        lower = [(4 * i + x, 4 * i + 4 + x) for i in range(3) for x in range(4) if x % 2 == n]
+        upper = [(4 * i + 4 + x, 4 * i + x) for i in range(3) for x in range(4) if x % 2 != n]
+        spills.append(lax.ppermute(out, ("y", "x"), lower + upper))
+    main = call(place_kernel, "place", held_rows, [VMEM] * 8, VMEM, [pltpu.VMEM((12, CELLROW, TILE), f32)])(*own, *sib)
+    main, *first = call(
+        merge_kernel, "merge", (held_rows,) + (coded,) * len(FIRST), [VMEM] * 3, (VMEM,) * (1 + len(FIRST))
+    )(main, *spills)
 
     def along_z(block, hops):
         return lax.ppermute(block, "z", [(i, (i + hops) % 8) for i in range(8)])

time: 87.9 us -> 84.1 us (0.957)
  the two profiles are of different devices: /device:TPU:8 before, /device:TPU:96 now
where the time goes in v4:
time: 84.1 us; the launch traced here: 83.9 us
  waiting for transfers between devices  36.2 us (43%)
  starting transfers between devices  32 us (38%)
  Pallas kernels  13.1 us (16%)
  between operations  1.54 us (2%)
  local copies, waits for them, and re-layouts  1.02 us (1%)
    ppermute x7, waiting for transfers between devices, along_z(): return lax.ppermute(block, 'z', [(i, (i + hops) % 8) for i in range(8)])  16.9 us
    ppermute x4, waiting for transfers between devices, local(): lax.ppermute(outs[2 * n + 1], ('core', 'x'), [(c * 4 + i, (1 - c) * 4 + (...  13.3 us
    ppermute x7, starting transfers between devices, along_z(): return lax.ppermute(block, 'z', [(i, (i + hops) % 8) for i in range(8)])  11 us
    ppermute x3, starting transfers between devices, local(): lax.ppermute(own[hop], 'x', [(i, (i + hop) % 4) for i in range(4)])  7.04 us
    ppermute x4, starting transfers between devices, local(): lax.ppermute(outs[2 * n + 1], ('core', 'x'), [(c * 4 + i, (1 - c) * 4 + (...  6.49 us
    ppermute x2, waiting for transfers between devices, local(): spills.append(lax.ppermute(out, ('y', 'x'), lower + upper))  5.98 us
    ppermute x2, starting transfers between devices, local(): spills.append(lax.ppermute(out, ('y', 'x'), lower + upper))  5.29 us
    pallas_call x2, Pallas kernels, local(): call(lambda *refs, hops=hops: warp_kernel(hops, *refs), 'warp_' + ''.join...  3.92 us
  transfers between devices with their start and end apart: 18, of which 10 were waited for; matrix products, arithmetic and copies ran while one was open for 0% of the time, Pallas kernels for 10%

profile of v4, /device:TPU:96, one launch (start us, length us, event | category | flops | bytes accessed | tf_op | source)
XLA Modules:
  0.0 83.9 jit_solution(6897028545200034158)
XLA Ops:
  0.6 1.0 %dynamic-slice_bitcast_fusion = (bf16[16,4096]{1,0:T(8,128)(2,1)S(1)}, bf16[16,4096]{1,0:T(8,128)(2,1)S(1)}) fusion(bf16[1,256,4096]{2,1,0:T(8,128)(2,1)} %img_hbm.1, s32[]{:T(128)S(6)} %select_n.7, s32[]{:T(128)S(6)} %select_n.6), kind=kLoop, calls=%fused_computation | loop fusion | bytes 524296 | tf_op jit(solution)/shard_map/dynamic_slice | solution.py:314
  1.6 1.6 %collective-permute-start.1 = (bf16[16,4096]{1,0:T(8,128)(2,1)S(1)}, bf16[16,4096]{1,0:T(8,128)(2,1)S(1)}, u32[]{:S(2)}, u32[]{:S(2)}) collective-permute-start(bf16[16,4096]{1,0:T(8,128)(2,1)S(1)} %get-tuple-element.30), channel_id=1, source_target_pairs={{0,1},{1,0},{2,3},{3,2},{4,5},{5,4},{6,7},{7,6},{8,9},{9,8},{10,11... | collective-permute-start | bytes 393224 | tf_op jit(solution)/shard_map/ppermute | solution.py:316
  3.9 3.0 %columns.1 = (bf16[256,4224]{1,0:T(8,128)(2,1)S(1)}, s32[2]{0:T(128)S(1)}) custom-call(bf16[1,2,13]{2,1,0:T(2,128)(2,1)} %taps_ref.1, s32[1,2,32]{2,1,0:T(2,128)} %refs_1_.3, s32[1,2,32]{2,1,0:T(2,128)} %cell_hbm.1, bf16[1,256,4096]{2,1,0:T(8,128)(2,1)} %img_hbm.1), custom_call_target="tpu_custom_call" | custom-call | flops 1 | bytes 1 | tf_op jit(solution)/shard_map/columns/pallas_call | solution.py:318
  7.6 1.5 %rows.1.refs_6_ = bf16[2,144,4224]{2,1,0:T(8,128)(2,1)S(1)} custom-call(bf16[1,2,13]{2,1,0:T(2,128)(2,1)S(1)} %copy-done.4, bf16[16,4096]{1,0:T(8,128)(2,1)S(1)} %collective-permute-done.outer_ref, bf16[16,4096]{1,0:T(8,128)(2,1)S(1)} %collective-permute-done.1.inner_ref, bf16[256,4224]{1,0:T(8,128)(2,1)S(1)} %get-tuple-element.17.passed_ref), custom_call_target="tpu_custom_call" | custom-call | flops 1 | bytes 1 | tf_op jit(solution)/shard_map/rows/pallas_call | solution.py:332
  9.2 2.0 %warp_13.1 = (bf16[1056,128]{1,0:T(8,128)(2,1)S(1)}, bf16[1056,128]{1,0:T(8,128)(2,1)S(1)}, bf16[1056,128]{1,0:T(8,128)(2,1)S(1)}, bf16[1056,128]{1,0:T(8,128)(2,1)S(1)}) custom-call(s32[2]{0:T(128)S(1)} %get-tuple-element.16.refs_0_, s32[1,2,32]{2,1,0:T(2,128)S(1)} %copy-done.2, s32[1,2,2,32]{3,2,1,0:T(2,128)S(1)} %copy-done.3, f32[1]{0:T(128)S(6)} %copy.10.refs_3_, ...), custom_call_target="tpu_custom_call" | custom-call | flops 1 | bytes 1 | tf_op jit(solution)/shard_map/warp_13/pallas_call | solution.py:344
  11.1 4.0 %collective-permute-start.2 = (bf16[1056,128]{1,0:T(8,128)(2,1)S(1)}, bf16[1056,128]{1,0:T(8,128)(2,1)S(1)}, u32[]{:S(2)}, u32[]{:S(2)}) collective-permute-start(bf16[1056,128]{1,0:T(8,128)(2,1)S(1)} %get-tuple-element.19), channel_id=1, source_target_pairs={{0,1},{1,2},{2,3},{3,0},{4,5},{5,6},{6,7},{7,4},{8,9},{9,10},{10,1... | collective-permute-start | bytes 811016 | tf_op jit(solution)/shard_map/ppermute | solution.py:355
  15.1 2.8 %collective-permute-start.4 = (bf16[1056,128]{1,0:T(8,128)(2,1)S(1)}, bf16[1056,128]{1,0:T(8,128)(2,1)S(1)}, u32[]{:S(2)}, u32[]{:S(2)}) collective-permute-start(bf16[1056,128]{1,0:T(8,128)(2,1)S(1)} %get-tuple-element.21), channel_id=1, source_target_pairs={{0,3},{1,0},{2,1},{3,2},{4,7},{5,4},{6,5},{7,6},{8,11},{9,8},{10,9... | collective-permute-start | bytes 811016 | tf_op jit(solution)/shard_map/ppermute | solution.py:355
  18.0 2.0 %warp_20.1 = (bf16[1056,128]{1,0:T(8,128)(2,1)S(1)}, bf16[1056,128]{1,0:T(8,128)(2,1)S(1)}, bf16[1056,128]{1,0:T(8,128)(2,1)S(1)}, bf16[1056,128]{1,0:T(8,128)(2,1)S(1)}) custom-call(s32[2]{0:T(128)S(1)} %get-tuple-element.16.refs_0_, s32[1,2,32]{2,1,0:T(2,128)S(1)} %copy-done.2, s32[1,2,2,32]{3,2,1,0:T(2,128)S(1)} %copy-done.3, f32[1]{0:T(128)S(6)} %copy.10.refs_3_, ...), custom_call_target="tpu_custom_call" | custom-call | flops 1 | bytes 1 | tf_op jit(solution)/shard_map/warp_20/pallas_call | solution.py:344
  20.0 2.9 %collective-permute-start.8 = (bf16[1056,128]{1,0:T(8,128)(2,1)S(1)}, bf16[1056,128]{1,0:T(8,128)(2,1)S(1)}, u32[]{:S(2)}, u32[]{:S(2)}) collective-permute-start(bf16[1056,128]{1,0:T(8,128)(2,1)S(1)} %get-tuple-element.25), channel_id=1, source_target_pairs={{0,19},{1,16},{2,17},{3,18},{16,3},{17,0},{18,1},{19,2},{4,23},{5,... | collective-permute-start | bytes 811016 | tf_op jit(solution)/shard_map/ppermute | solution.py:356
  23.3 3.4 %collective-permute-start.7 = (bf16[1056,128]{1,0:T(8,128)(2,1)S(1)}, bf16[1056,128]{1,0:T(8,128)(2,1)S(1)}, u32[]{:S(2)}, u32[]{:S(2)}) collective-permute-start(bf16[1056,128]{1,0:T(8,128)(2,1)S(1)} %get-tuple-element.24), channel_id=1, source_target_pairs={{0,18},{1,19},{2,16},{3,17},{16,2},{17,3},{18,0},{19,1},{4,22},{5,... | collective-permute-start | bytes 811016 | tf_op jit(solution)/shard_map/ppermute | solution.py:356
  26.6 2.6 %collective-permute-done.6.refs_5_.refs_1_ = bf16[1056,128]{1,0:T(8,128)(2,1)S(1)} collective-permute-done((bf16[1056,128]{1,0:T(8,128)(2,1)S(1)}, bf16[1056,128]{1,0:T(8,128)(2,1)S(1)}, u32[]{:S(2)}, u32[]{:S(2)}) %collective-permute-start.6) | collective-permute-done | bytes 270368 | tf_op jit(solution)/shard_map/ppermute | solution.py:356
  29.3 10.7 %collective-permute-done.8.refs_7_.refs_3_ = bf16[1056,128]{1,0:T(8,128)(2,1)S(1)} collective-permute-done((bf16[1056,128]{1,0:T(8,128)(2,1)S(1)}, bf16[1056,128]{1,0:T(8,128)(2,1)S(1)}, u32[]{:S(2)}, u32[]{:S(2)}) %collective-permute-start.8) | collective-permute-done | bytes 270368 | tf_op jit(solution)/shard_map/ppermute | solution.py:356
  40.5 4.0 %collective-permute-start.9 = (s16[1056,128]{1,0:T(8,128)(2,1)S(1)}, s16[1056,128]{1,0:T(8,128)(2,1)S(1)}, u32[]{:S(2)}, u32[]{:S(2)}) collective-permute-start(s16[1056,128]{1,0:T(8,128)(2,1)S(1)} %spill_0.1), channel_id=1, source_target_pairs={{0,4},{2,6},{4,8},{6,10},{8,12},{10,14},{5,1},{7,3},{9,5},{11,7},{... | collective-permute-start | bytes 811016 | tf_op jit(solution)/shard_map/ppermute | solution.py:376
  45.3 1.3 %collective-permute-start.10 = (s16[1056,128]{1,0:T(8,128)(2,1)S(1)}, s16[1056,128]{1,0:T(8,128)(2,1)S(1)}, u32[]{:S(2)}, u32[]{:S(2)}) collective-permute-start(s16[1056,128]{1,0:T(8,128)(2,1)S(1)} %spill_1.1), channel_id=1, source_target_pairs={{1,5},{3,7},{5,9},{7,11},{9,13},{11,15},{4,0},{6,2},{8,4},{10,6},{... | collective-permute-start | bytes 811016 | tf_op jit(solution)/shard_map/ppermute | solution.py:376
  46.6 1.1 %place.1.in_ref = f32[8,528,128]{2,1,0:T(8,128)S(1)} custom-call(bf16[1056,128]{1,0:T(8,128)(2,1)S(1)} %get-tuple-element.18.refs_0_, bf16[1056,128]{1,0:T(8,128)(2,1)S(1)} %collective-permute-done.2.refs_1_.refs_0_, bf16[1056,128]{1,0:T(8,128)(2,1)S(1)} %collective-permute-done.3.refs_2_, bf16[1056,128]{1,0:T(8,128)(2,1)S(1)} %collective-permute-done.4.refs_3_.refs_2_, ...), custom_call_target="tpu_custom_call" | custom-call | flops 1 | bytes 1 | tf_op jit(solution)/shard_map/place/pallas_call | solution.py:377
  48.5 5.2 %collective-permute-done.10.refs_1_ = s16[1056,128]{1,0:T(8,128)(2,1)S(1)} collective-permute-done((s16[1056,128]{1,0:T(8,128)(2,1)S(1)}, s16[1056,128]{1,0:T(8,128)(2,1)S(1)}, u32[]{:S(2)}, u32[]{:S(2)}) %collective-permute-start.10) | collective-permute-done | bytes 270368 | tf_op jit(solution)/shard_map/ppermute | solution.py:376
  54.3 3.2 %collective-permute-start.11 = (s16[528,128]{1,0:T(8,128)(2,1)S(1)}, s16[528,128]{1,0:T(8,128)(2,1)S(1)}, u32[]{:S(2)}, u32[]{:S(2)}) collective-permute-start(s16[528,128]{1,0:T(8,128)(2,1)S(1)} %get-tuple-element.27), channel_id=1, source_target_pairs={{0,32},{32,64},{64,96},{96,128},{128,160},{160,192},{192,224},{224... | collective-permute-start | bytes 405512 | tf_op jit(solution)/shard_map/ppermute | solution.py:383
  57.6 5.4 %collective-permute-done.11.refs_1_ = s16[528,128]{1,0:T(8,128)(2,1)S(1)} collective-permute-done((s16[528,128]{1,0:T(8,128)(2,1)S(1)}, s16[528,128]{1,0:T(8,128)(2,1)S(1)}, u32[]{:S(2)}, u32[]{:S(2)}) %collective-permute-start.11) | collective-permute-done | bytes 135200 | tf_op jit(solution)/shard_map/ppermute | solution.py:383
  63.2 3.7 %collective-permute-start.12 = (s16[528,128]{1,0:T(8,128)(2,1)S(1)}, s16[528,128]{1,0:T(8,128)(2,1)S(1)}, u32[]{:S(2)}, u32[]{:S(2)}) collective-permute-start(s16[528,128]{1,0:T(8,128)(2,1)S(1)} %up_2.1), channel_id=1, source_target_pairs={{0,32},{32,64},{64,96},{96,128},{128,160},{160,192},{192,224},{224... | collective-permute-start | bytes 405512 | tf_op jit(solution)/shard_map/ppermute | solution.py:383
  68.0 3.5 %collective-permute-done.12.refs_1_ = s16[528,128]{1,0:T(8,128)(2,1)S(1)} collective-permute-done((s16[528,128]{1,0:T(8,128)(2,1)S(1)}, s16[528,128]{1,0:T(8,128)(2,1)S(1)}, u32[]{:S(2)}, u32[]{:S(2)}) %collective-permute-start.12) | collective-permute-done | bytes 135200 | tf_op jit(solution)/shard_map/ppermute | solution.py:383
  71.7 3.7 %collective-permute-start.13 = (s16[528,128]{1,0:T(8,128)(2,1)S(1)}, s16[528,128]{1,0:T(8,128)(2,1)S(1)}, u32[]{:S(2)}, u32[]{:S(2)}) collective-permute-start(s16[528,128]{1,0:T(8,128)(2,1)S(1)} %up_1.1), channel_id=1, source_target_pairs={{0,32},{32,64},{64,96},{96,128},{128,160},{160,192},{192,224},{224... | collective-permute-start | bytes 405512 | tf_op jit(solution)/shard_map/ppermute | solution.py:383
  75.4 1.1 %collective-permute-done.15.refs_1_ = s16[528,128]{1,0:T(8,128)(2,1)S(1)} collective-permute-done((s16[528,128]{1,0:T(8,128)(2,1)S(1)}, s16[528,128]{1,0:T(8,128)(2,1)S(1)}, u32[]{:S(2)}, u32[]{:S(2)}) %collective-permute-start.15) | collective-permute-done | bytes 135200 | tf_op jit(solution)/shard_map/ppermute | solution.py:383
  76.8 1.6 %collective-permute-done.17.refs_2_ = s16[528,128]{1,0:T(8,128)(2,1)S(1)} collective-permute-done((s16[528,128]{1,0:T(8,128)(2,1)S(1)}, s16[528,128]{1,0:T(8,128)(2,1)S(1)}, u32[]{:S(2)}, u32[]{:S(2)}) %collective-permute-start.17) | collective-permute-done | bytes 135200 | tf_op jit(solution)/shard_map/ppermute | solution.py:383
  78.4 4.6 %collective-permute-done.16.refs_1_ = s16[528,128]{1,0:T(8,128)(2,1)S(1)} collective-permute-done((s16[528,128]{1,0:T(8,128)(2,1)S(1)}, s16[528,128]{1,0:T(8,128)(2,1)S(1)}, u32[]{:S(2)}, u32[]{:S(2)}) %collective-permute-start.16) | collective-permute-done | bytes 135200 | tf_op jit(solution)/shard_map/ppermute | solution.py:383
  (36 shorter events, 6.4 us)
Async XLA Ops:
  0.6 6.9 %copy-start.4 = (bf16[1,2,13]{2,1,0:T(2,128)(2,1)S(1)}, bf16[1,2,13]{2,1,0:T(2,128)(2,1)}, u32[]{:S(2)}) copy-start(bf16[1,2,13]{2,1,0:T(2,128)(2,1)} %taps_ref.1) | copy-start | bytes 160
  1.6 5.9 %collective-permute-start.1 = (bf16[16,4096]{1,0:T(8,128)(2,1)S(1)}, bf16[16,4096]{1,0:T(8,128)(2,1)S(1)}, u32[]{:S(2)}, u32[]{:S(2)}) collective-permute-start(bf16[16,4096]{1,0:T(8,128)(2,1)S(1)} %get-tuple-element.30), channel_id=1, source_target_pairs={{0,1},{1,0},{2,3},{3,2},{4,5},{5,4},{6,7},{7,6},{8,9},{9,8},{10,11... | collective-permute-start | bytes 393224 | tf_op jit(solution)/shard_map/ppermute | solution.py:316
  3.2 4.3 %collective-permute-start = (bf16[16,4096]{1,0:T(8,128)(2,1)S(1)}, bf16[16,4096]{1,0:T(8,128)(2,1)S(1)}, u32[]{:S(2)}, u32[]{:S(2)}) collective-permute-start(bf16[16,4096]{1,0:T(8,128)(2,1)S(1)} %get-tuple-element.31), channel_id=1, source_target_pairs={{1,2},{2,1},{3,4},{4,3},{5,6},{6,5},{7,8},{8,7},{9,10},{10,9},{11,... | collective-permute-start | bytes 393224 | tf_op jit(solution)/shard_map/ppermute | solution.py:315
  7.6 1.5 %copy-start = (bf16[9,128,144]{2,1,0:T(8,128)(2,1)S(1)}, bf16[9,128,144]{2,1,0:T(8,128)(2,1)}, u32[]{:S(2)}) copy-start(bf16[9,128,144]{2,1,0:T(8,128)(2,1)} %constant.20.clone.refs_4_) | copy-start | bytes 995332
  7.6 1.5 %copy-start.1 = (bf16[8,256,128]{2,1,0:T(8,128)(2,1)S(1)}, bf16[8,256,128]{2,1,0:T(8,128)(2,1)}, u32[]{:S(2)}) copy-start(bf16[8,256,128]{2,1,0:T(8,128)(2,1)} %constant.21.clone.refs_5_) | copy-start | bytes 1572868
  7.6 1.5 %copy-start.2 = (s32[1,2,32]{2,1,0:T(2,128)S(1)}, s32[1,2,32]{2,1,0:T(2,128)}, u32[]{:S(2)}) copy-start(s32[1,2,32]{2,1,0:T(2,128)} %refs_1_.3) | copy-start | bytes 772
  7.6 1.5 %copy-start.3 = (s32[1,2,2,32]{3,2,1,0:T(2,128)S(1)}, s32[1,2,2,32]{3,2,1,0:T(2,128)}, u32[]{:S(2)}) copy-start(s32[1,2,2,32]{3,2,1,0:T(2,128)} %refs_2_.3) | copy-start | bytes 1540
  11.1 12.0 %collective-permute-start.2 = (bf16[1056,128]{1,0:T(8,128)(2,1)S(1)}, bf16[1056,128]{1,0:T(8,128)(2,1)S(1)}, u32[]{:S(2)}, u32[]{:S(2)}) collective-permute-start(bf16[1056,128]{1,0:T(8,128)(2,1)S(1)} %get-tuple-element.19), channel_id=1, source_target_pairs={{0,1},{1,2},{2,3},{3,0},{4,5},{5,6},{6,7},{7,4},{8,9},{9,10},{10,1... | collective-permute-start | bytes 811016 | tf_op jit(solution)/shard_map/ppermute | solution.py:355
  15.1 8.1 %collective-permute-start.4 = (bf16[1056,128]{1,0:T(8,128)(2,1)S(1)}, bf16[1056,128]{1,0:T(8,128)(2,1)S(1)}, u32[]{:S(2)}, u32[]{:S(2)}) collective-permute-start(bf16[1056,128]{1,0:T(8,128)(2,1)S(1)} %get-tuple-element.21), channel_id=1, source_target_pairs={{0,3},{1,0},{2,1},{3,2},{4,7},{5,4},{6,5},{7,6},{8,11},{9,8},{10,9... | collective-permute-start | bytes 811016 | tf_op jit(solution)/shard_map/ppermute | solution.py:355
  19.9 9.3 %collective-permute-start.6 = (bf16[1056,128]{1,0:T(8,128)(2,1)S(1)}, bf16[1056,128]{1,0:T(8,128)(2,1)S(1)}, u32[]{:S(2)}, u32[]{:S(2)}) collective-permute-start(bf16[1056,128]{1,0:T(8,128)(2,1)S(1)} %get-tuple-element.23), channel_id=1, source_target_pairs={{0,17},{1,18},{2,19},{3,16},{16,1},{17,2},{18,3},{19,0},{4,21},{5,... | collective-permute-start | bytes 811016 | tf_op jit(solution)/shard_map/ppermute | solution.py:356
  20.0 19.9 %collective-permute-start.8 = (bf16[1056,128]{1,0:T(8,128)(2,1)S(1)}, bf16[1056,128]{1,0:T(8,128)(2,1)S(1)}, u32[]{:S(2)}, u32[]{:S(2)}) collective-permute-start(bf16[1056,128]{1,0:T(8,128)(2,1)S(1)} %get-tuple-element.25), channel_id=1, source_target_pairs={{0,19},{1,16},{2,17},{3,18},{16,3},{17,0},{18,1},{19,2},{4,23},{5,... | collective-permute-start | bytes 811016 | tf_op jit(solution)/shard_map/ppermute | solution.py:356
  23.0 21.5 %collective-permute-start.3 = (bf16[1056,128]{1,0:T(8,128)(2,1)S(1)}, bf16[1056,128]{1,0:T(8,128)(2,1)S(1)}, u32[]{:S(2)}, u32[]{:S(2)}) collective-permute-start(bf16[1056,128]{1,0:T(8,128)(2,1)S(1)} %get-tuple-element.20), channel_id=1, source_target_pairs={{0,2},{1,3},{2,0},{3,1},{4,6},{5,7},{6,4},{7,5},{8,10},{9,11},{10,... | collective-permute-start | bytes 811016 | tf_op jit(solution)/shard_map/ppermute | solution.py:355
  23.2 21.4 %collective-permute-start.5 = (bf16[1056,128]{1,0:T(8,128)(2,1)S(1)}, bf16[1056,128]{1,0:T(8,128)(2,1)S(1)}, u32[]{:S(2)}, u32[]{:S(2)}) collective-permute-start(bf16[1056,128]{1,0:T(8,128)(2,1)S(1)} %get-tuple-element.22), channel_id=1, source_target_pairs={{0,16},{1,17},{2,18},{3,19},{16,0},{17,1},{18,2},{19,3},{4,20},{5,... | collective-permute-start | bytes 811016 | tf_op jit(solution)/shard_map/ppermute | solution.py:356
  23.3 21.3 %collective-permute-start.7 = (bf16[1056,128]{1,0:T(8,128)(2,1)S(1)}, bf16[1056,128]{1,0:T(8,128)(2,1)S(1)}, u32[]{:S(2)}, u32[]{:S(2)}) collective-permute-start(bf16[1056,128]{1,0:T(8,128)(2,1)S(1)} %get-tuple-element.24), channel_id=1, source_target_pairs={{0,18},{1,19},{2,16},{3,17},{16,2},{17,3},{18,0},{19,1},{4,22},{5,... | collective-permute-start | bytes 811016 | tf_op jit(solution)/shard_map/ppermute | solution.py:356
  40.5 8.0 %collective-permute-start.9 = (s16[1056,128]{1,0:T(8,128)(2,1)S(1)}, s16[1056,128]{1,0:T(8,128)(2,1)S(1)}, u32[]{:S(2)}, u32[]{:S(2)}) collective-permute-start(s16[1056,128]{1,0:T(8,128)(2,1)S(1)} %spill_0.1), channel_id=1, source_target_pairs={{0,4},{2,6},{4,8},{6,10},{8,12},{10,14},{5,1},{7,3},{9,5},{11,7},{... | collective-permute-start | bytes 811016 | tf_op jit(solution)/shard_map/ppermute | solution.py:376
  45.3 8.4 %collective-permute-start.10 = (s16[1056,128]{1,0:T(8,128)(2,1)S(1)}, s16[1056,128]{1,0:T(8,128)(2,1)S(1)}, u32[]{:S(2)}, u32[]{:S(2)}) collective-permute-start(s16[1056,128]{1,0:T(8,128)(2,1)S(1)} %spill_1.1), channel_id=1, source_target_pairs={{1,5},{3,7},{5,9},{7,11},{9,13},{11,15},{4,0},{6,2},{8,4},{10,6},{... | collective-permute-start | bytes 811016 | tf_op jit(solution)/shard_map/ppermute | solution.py:376
  54.3 8.6 %collective-permute-start.11 = (s16[528,128]{1,0:T(8,128)(2,1)S(1)}, s16[528,128]{1,0:T(8,128)(2,1)S(1)}, u32[]{:S(2)}, u32[]{:S(2)}) collective-permute-start(s16[528,128]{1,0:T(8,128)(2,1)S(1)} %get-tuple-element.27), channel_id=1, source_target_pairs={{0,32},{32,64},{64,96},{96,128},{128,160},{160,192},{192,224},{224... | collective-permute-start | bytes 405512 | tf_op jit(solution)/shard_map/ppermute | solution.py:383
  57.6 10.0 %collective-permute-start.14 = (s16[528,128]{1,0:T(8,128)(2,1)S(1)}, s16[528,128]{1,0:T(8,128)(2,1)S(1)}, u32[]{:S(2)}, u32[]{:S(2)}) collective-permute-start(s16[528,128]{1,0:T(8,128)(2,1)S(1)} %get-tuple-element.28), channel_id=1, source_target_pairs={{0,224},{32,0},{64,32},{96,64},{128,96},{160,128},{192,160},{224,1... | collective-permute-start | bytes 405512 | tf_op jit(solution)/shard_map/ppermute | solution.py:383
  63.2 8.3 %collective-permute-start.12 = (s16[528,128]{1,0:T(8,128)(2,1)S(1)}, s16[528,128]{1,0:T(8,128)(2,1)S(1)}, u32[]{:S(2)}, u32[]{:S(2)}) collective-permute-start(s16[528,128]{1,0:T(8,128)(2,1)S(1)} %up_2.1), channel_id=1, source_target_pairs={{0,32},{32,64},{64,96},{96,128},{128,160},{160,192},{192,224},{224... | collective-permute-start | bytes 405512 | tf_op jit(solution)/shard_map/ppermute | solution.py:383
  67.8 8.7 %collective-permute-start.15 = (s16[528,128]{1,0:T(8,128)(2,1)S(1)}, s16[528,128]{1,0:T(8,128)(2,1)S(1)}, u32[]{:S(2)}, u32[]{:S(2)}) collective-permute-start(s16[528,128]{1,0:T(8,128)(2,1)S(1)} %down_2.1), channel_id=1, source_target_pairs={{0,224},{32,0},{64,32},{96,64},{128,96},{160,128},{192,160},{224,1... | collective-permute-start | bytes 405512 | tf_op jit(solution)/shard_map/ppermute | solution.py:383
  67.9 10.6 %collective-permute-start.17 = (s16[528,128]{1,0:T(8,128)(2,1)S(1)}, s16[528,128]{1,0:T(8,128)(2,1)S(1)}, u32[]{:S(2)}, u32[]{:S(2)}) collective-permute-start(s16[528,128]{1,0:T(8,128)(2,1)S(1)} %get-tuple-element.29), channel_id=1, source_target_pairs={{0,128},{32,160},{64,192},{96,224},{128,0},{160,32},{192,64},{224,... | collective-permute-start | bytes 405512 | tf_op jit(solution)/shard_map/ppermute | solution.py:383
  71.7 6.8 %collective-permute-start.13 = (s16[528,128]{1,0:T(8,128)(2,1)S(1)}, s16[528,128]{1,0:T(8,128)(2,1)S(1)}, u32[]{:S(2)}, u32[]{:S(2)}) collective-permute-start(s16[528,128]{1,0:T(8,128)(2,1)S(1)} %up_1.1), channel_id=1, source_target_pairs={{0,32},{32,64},{64,96},{96,128},{128,160},{160,192},{192,224},{224... | collective-permute-start | bytes 405512 | tf_op jit(solution)/shard_map/ppermute | solution.py:383
  76.7 6.3 %collective-permute-start.16 = (s16[528,128]{1,0:T(8,128)(2,1)S(1)}, s16[528,128]{1,0:T(8,128)(2,1)S(1)}, u32[]{:S(2)}, u32[]{:S(2)}) collective-permute-start(s16[528,128]{1,0:T(8,128)(2,1)S(1)} %down_1.1), channel_id=1, source_target_pairs={{0,224},{32,0},{64,32},{96,64},{128,96},{160,128},{192,160},{224,1... | collective-permute-start | bytes 405512 | tf_op jit(solution)/shard_map/ppermute | solution.py:383

commit v5 on v4

--- a/solution.py
+++ b/solution.py
@@ -24,8 +24,8 @@
 CELLROW = 4 * TILE + 16
 TOP_CODE = 32000.0
 HOPS = ((1, 3), (2, 0))
+LATE = 1
 CHAIN = 3
-FIRST = (CHAIN, -CHAIN, 4) + tuple(sign * d for d in range(CHAIN + 1, 4) for sign in (1, -1))
 f32 = jnp.float32
 bf16 = jnp.bfloat16
 i16 = jnp.int16
@@ -286,19 +286,30 @@
                 main_ref[first + r, w * TILE : (w + 1) * TILE, :] = cells[w]
             main_ref[first + r, 4 * TILE : 4 * TILE + 4, :] = weights
     z = lax.axis_index("z")
-    for ahead, out_ref in zip(FIRST, outs):
+    for ahead, out_ref in zip((upward(CHAIN), -upward(CHAIN), 4), outs):
         encode(*held(main_ref, (z + 8 + ahead) & 7), out_ref, 0)
 
 
-def step_kernel(ahead, main_ref, in_ref, out_ref):
-    at = (lax.axis_index("z") + 8 + ahead) & 7
+def upward(by):
+    return by - 2 * by * (lax.axis_index("z") & 1)
+
+
+def step_kernel(ahead, main_ref, in_ref, *refs):
+    out_ref = refs[-1]
+    at = (lax.axis_index("z") + 8 + upward(ahead)) & 7
     encode(*added(held(main_ref, at), decode(in_ref, 0)), out_ref, 0)
 
 
-def finish_kernel(main_ref, *refs):
+def fold_kernel(main_ref, far_ref, out_ref):
+    cells, weights = added(held(main_ref, lax.axis_index("z")), decode(far_ref, 0))
+    for w in range(4):
+        out_ref[0, w * TILE : (w + 1) * TILE, :] = cells[w]
+    out_ref[0, 4 * TILE : 4 * TILE + 4, :] = weights
+
+
+def finish_kernel(own_ref, *refs):
     ins, (coadd_ref, cover_ref) = refs[:-2], refs[-2:]
-    z = lax.axis_index("z")
-    cells, weights = added(held(main_ref, z), *[decode(ref, 0) for ref in ins])
+    cells, weights = added(held(own_ref, 0), *[decode(ref, 0) for ref in ins])
     lane = lax.broadcasted_iota(i32, (1, TILE), 1)
     cover = jnp.zeros((1, TILE), f32)
     for w in range(4):
@@ -375,27 +386,28 @@
         upper = [(4 * i + 4 + x, 4 * i + x) for i in range(3) for x in range(4) if x % 2 != n]
         spills.append(lax.ppermute(out, ("y", "x"), lower + upper))
     main = call(place_kernel, "place", held_rows, [VMEM] * 8, VMEM, [pltpu.VMEM((12, CELLROW, TILE), f32)])(*own, *sib)
-    main, *first = call(
-        merge_kernel, "merge", (held_rows,) + (coded,) * len(FIRST), [VMEM] * 3, (VMEM,) * (1 + len(FIRST))
+    main, one, two, far = call(
+        merge_kernel, "merge", (held_rows,) + (coded,) * 3, [VMEM] * 3, (VMEM,) * 4
     )(main, *spills)
 
-    def along_z(block, hops):
-        return lax.ppermute(block, "z", [(i, (i + hops) % 8) for i in range(8)])
-
-    up, dn = first[:2]
+    pairs = [[p for i in range(n, 8, 2) for p in ((i, (i + 1) % 8), ((i + 1) % 8, i))] for n in range(2)]
+    far = lax.ppermute(far, "z", [(i, (i + 4) % 8) for i in range(8)])
+    mine = call(fold_kernel, "fold", shape((1, CELLROW, TILE), f32), [VMEM] * 2, VMEM)(main, far)
     for s in range(CHAIN - 1, -1, -1):
-        up, dn = along_z(up, 1), along_z(dn, -1)
+        got_one, got_two = lax.ppermute(one, "z", pairs[0]), lax.ppermute(two, "z", pairs[1])
+        one, two = got_two, got_one
         if s:
-            up = call(lambda *refs, s=s: step_kernel(s, *refs), f"up_{s}", coded, [VMEM] * 2, VMEM)(main, up)
-            dn = call(lambda *refs, s=s: step_kernel(-s, *refs), f"down_{s}", coded, [VMEM] * 2, VMEM)(main, dn)
-    far = [along_z(block, ahead) for ahead, block in zip(FIRST[2:], first[2:])]
+            after = (mine,) if s == LATE else ()
+            ins = [VMEM] * (2 + len(after))
+            one = call(lambda *refs, s=s: step_kernel(s, *refs), f"one_{s}", coded, ins, VMEM)(main, got_two, *after)
+            two = call(lambda *refs, s=s: step_kernel(-s, *refs), f"two_{s}", coded, ins, VMEM)(main, got_one, *after)
     return call(
         finish_kernel,
         "finish",
         (shape((1, 4, TILE, TILE), f32), shape((1, 4), f32)),
-        [VMEM] * (3 + len(far)),
+        [VMEM] * 3,
         (VMEM, VMEM),
-    )(main, up, dn, *far)
+    )(mine, one, two)
 
 
 def solution(mesh):

time: 84.1 us -> 81.7 us (0.971)
  the two profiles are of different devices: /device:TPU:96 before, /device:TPU:8 now
where the time goes in v5:
time: 81.7 us; the launch traced here: 81.5 us
  starting transfers between devices  36.4 us (45%)
  waiting for transfers between devices  29.4 us (36%)
  Pallas kernels  13.2 us (16%)
  between operations  1.53 us (2%)
  local copies, waits for them, and re-layouts  1.01 us (1%)
    ppermute x4, waiting for transfers between devices, local(): lax.ppermute(outs[2 * n + 1], ('core', 'x'), [(c * 4 + i, (1 - c) * 4 + (...  12.8 us
    ppermute x3, starting transfers between devices, local(): lax.ppermute(two, 'z', pairs[1])  11.1 us
    ppermute x4, starting transfers between devices, local(): lax.ppermute(outs[2 * n + 1], ('core', 'x'), [(c * 4 + i, (1 - c) * 4 + (...  6.67 us
    ppermute x2, starting transfers between devices, local(): spills.append(lax.ppermute(out, ('y', 'x'), lower + upper))  5.85 us
    ppermute x2, waiting for transfers between devices, local(): spills.append(lax.ppermute(out, ('y', 'x'), lower + upper))  5.35 us
    ppermute x3, waiting for transfers between devices, local(): lax.ppermute(two, 'z', pairs[1])  4.92 us
    pallas_call x2, Pallas kernels, local(): call(lambda *refs, hops=hops: warp_kernel(hops, *refs), 'warp_' + ''.join...  3.91 us
    ppermute x1, starting transfers between devices, local(): lax.ppermute(outer, ('y', 'x'), [p for i in range(1, 14, 2) for p in ((i,...  3.88 us
  transfers between devices with their start and end apart: 18, of which 10 were waited for; matrix products, arithmetic and copies ran while one was open for 0% of the time, Pallas kernels for 10%

profile of v5, /device:TPU:8, one launch (start us, length us, event | category | flops | bytes accessed | tf_op | source)
XLA Modules:
  0.0 81.5 jit_solution(5142215178681695967)
XLA Ops:
  1.6 1.6 %collective-permute-start.1 = (bf16[16,4096]{1,0:T(8,128)(2,1)S(1)}, bf16[16,4096]{1,0:T(8,128)(2,1)S(1)}, u32[]{:S(2)}, u32[]{:S(2)}) collective-permute-start(bf16[16,4096]{1,0:T(8,128)(2,1)S(1)} %get-tuple-element.30), channel_id=1, source_target_pairs={{0,1},{1,0},{2,3},{3,2},{4,5},{5,4},{6,7},{7,6},{8,9},{9,8},{10,11... | collective-permute-start | bytes 393224 | tf_op jit(solution)/shard_map/ppermute | solution.py:327
  3.2 3.9 %collective-permute-start = (bf16[16,4096]{1,0:T(8,128)(2,1)S(1)}, bf16[16,4096]{1,0:T(8,128)(2,1)S(1)}, u32[]{:S(2)}, u32[]{:S(2)}) collective-permute-start(bf16[16,4096]{1,0:T(8,128)(2,1)S(1)} %get-tuple-element.31), channel_id=1, source_target_pairs={{1,2},{2,1},{3,4},{4,3},{5,6},{6,5},{7,8},{8,7},{9,10},{10,9},{11,... | collective-permute-start | bytes 393224 | tf_op jit(solution)/shard_map/ppermute | solution.py:326
  7.1 3.0 %columns.1 = (bf16[256,4224]{1,0:T(8,128)(2,1)S(1)}, s32[2]{0:T(128)S(1)}) custom-call(bf16[1,2,13]{2,1,0:T(2,128)(2,1)} %taps_ref.1, s32[1,2,32]{2,1,0:T(2,128)} %refs_1_.3, s32[1,2,32]{2,1,0:T(2,128)} %cell_hbm.1, bf16[1,256,4096]{2,1,0:T(8,128)(2,1)} %img_hbm.1), custom_call_target="tpu_custom_call" | custom-call | flops 1 | bytes 1 | tf_op jit(solution)/shard_map/columns/pallas_call | solution.py:329
  10.8 1.4 %collective-permute-done.outer_ref = bf16[16,4096]{1,0:T(8,128)(2,1)S(1)} collective-permute-done((bf16[16,4096]{1,0:T(8,128)(2,1)S(1)}, bf16[16,4096]{1,0:T(8,128)(2,1)S(1)}, u32[]{:S(2)}, u32[]{:S(2)}) %collective-permute-start) | collective-permute-done | bytes 131104 | tf_op jit(solution)/shard_map/ppermute | solution.py:326
  12.2 1.5 %rows.1.refs_6_ = bf16[2,144,4224]{2,1,0:T(8,128)(2,1)S(1)} custom-call(bf16[1,2,13]{2,1,0:T(2,128)(2,1)S(1)} %copy-done.4, bf16[16,4096]{1,0:T(8,128)(2,1)S(1)} %collective-permute-done.outer_ref, bf16[16,4096]{1,0:T(8,128)(2,1)S(1)} %collective-permute-done.1.inner_ref, bf16[256,4224]{1,0:T(8,128)(2,1)S(1)} %get-tuple-element.17.passed_ref), custom_call_target="tpu_custom_call" | custom-call | flops 1 | bytes 1 | tf_op jit(solution)/shard_map/rows/pallas_call | solution.py:343
  13.7 2.0 %warp_13.1 = (bf16[1056,128]{1,0:T(8,128)(2,1)S(1)}, bf16[1056,128]{1,0:T(8,128)(2,1)S(1)}, bf16[1056,128]{1,0:T(8,128)(2,1)S(1)}, bf16[1056,128]{1,0:T(8,128)(2,1)S(1)}) custom-call(s32[2]{0:T(128)S(1)} %get-tuple-element.16.refs_0_, s32[1,2,32]{2,1,0:T(2,128)S(1)} %copy-done.2, s32[1,2,2,32]{3,2,1,0:T(2,128)S(1)} %copy-done.3, f32[1]{0:T(128)S(6)} %copy.10.refs_3_, ...), custom_call_target="tpu_custom_call" | custom-call | flops 1 | bytes 1 | tf_op jit(solution)/shard_map/warp_13/pallas_call | solution.py:355
  15.8 3.2 %collective-permute-start.4 = (bf16[1056,128]{1,0:T(8,128)(2,1)S(1)}, bf16[1056,128]{1,0:T(8,128)(2,1)S(1)}, u32[]{:S(2)}, u32[]{:S(2)}) collective-permute-start(bf16[1056,128]{1,0:T(8,128)(2,1)S(1)} %get-tuple-element.21), channel_id=1, source_target_pairs={{0,3},{1,0},{2,1},{3,2},{4,7},{5,4},{6,5},{7,6},{8,11},{9,8},{10,9... | collective-permute-start | bytes 811016 | tf_op jit(solution)/shard_map/ppermute | solution.py:366
  19.0 2.0 %warp_20.1 = (bf16[1056,128]{1,0:T(8,128)(2,1)S(1)}, bf16[1056,128]{1,0:T(8,128)(2,1)S(1)}, bf16[1056,128]{1,0:T(8,128)(2,1)S(1)}, bf16[1056,128]{1,0:T(8,128)(2,1)S(1)}) custom-call(s32[2]{0:T(128)S(1)} %get-tuple-element.16.refs_0_, s32[1,2,32]{2,1,0:T(2,128)S(1)} %copy-done.2, s32[1,2,2,32]{3,2,1,0:T(2,128)S(1)} %copy-done.3, f32[1]{0:T(128)S(6)} %copy.10.refs_3_, ...), custom_call_target="tpu_custom_call" | custom-call | flops 1 | bytes 1 | tf_op jit(solution)/shard_map/warp_20/pallas_call | solution.py:355
  21.1 2.9 %collective-permute-start.8 = (bf16[1056,128]{1,0:T(8,128)(2,1)S(1)}, bf16[1056,128]{1,0:T(8,128)(2,1)S(1)}, u32[]{:S(2)}, u32[]{:S(2)}) collective-permute-start(bf16[1056,128]{1,0:T(8,128)(2,1)S(1)} %get-tuple-element.25), channel_id=1, source_target_pairs={{0,19},{1,16},{2,17},{3,18},{16,3},{17,0},{18,1},{19,2},{4,23},{5,... | collective-permute-start | bytes 811016 | tf_op jit(solution)/shard_map/ppermute | solution.py:367
  24.0 3.6 %collective-permute-start.7 = (bf16[1056,128]{1,0:T(8,128)(2,1)S(1)}, bf16[1056,128]{1,0:T(8,128)(2,1)S(1)}, u32[]{:S(2)}, u32[]{:S(2)}) collective-permute-start(bf16[1056,128]{1,0:T(8,128)(2,1)S(1)} %get-tuple-element.24), channel_id=1, source_target_pairs={{0,18},{1,19},{2,16},{3,17},{16,2},{17,3},{18,0},{19,1},{4,22},{5,... | collective-permute-start | bytes 811016 | tf_op jit(solution)/shard_map/ppermute | solution.py:367
  27.7 1.9 %collective-permute-done.6.refs_5_.refs_1_ = bf16[1056,128]{1,0:T(8,128)(2,1)S(1)} collective-permute-done((bf16[1056,128]{1,0:T(8,128)(2,1)S(1)}, bf16[1056,128]{1,0:T(8,128)(2,1)S(1)}, u32[]{:S(2)}, u32[]{:S(2)}) %collective-permute-start.6) | collective-permute-done | bytes 270368 | tf_op jit(solution)/shard_map/ppermute | solution.py:367
  29.6 10.9 %collective-permute-done.8.refs_7_.refs_3_ = bf16[1056,128]{1,0:T(8,128)(2,1)S(1)} collective-permute-done((bf16[1056,128]{1,0:T(8,128)(2,1)S(1)}, bf16[1056,128]{1,0:T(8,128)(2,1)S(1)}, u32[]{:S(2)}, u32[]{:S(2)}) %collective-permute-start.8) | collective-permute-done | bytes 270368 | tf_op jit(solution)/shard_map/ppermute | solution.py:367
  41.0 3.5 %collective-permute-start.9 = (s16[1056,128]{1,0:T(8,128)(2,1)S(1)}, s16[1056,128]{1,0:T(8,128)(2,1)S(1)}, u32[]{:S(2)}, u32[]{:S(2)}) collective-permute-start(s16[1056,128]{1,0:T(8,128)(2,1)S(1)} %spill_0.1), channel_id=1, source_target_pairs={{0,4},{2,6},{4,8},{6,10},{8,12},{10,14},{5,1},{7,3},{9,5},{11,7},{... | collective-permute-start | bytes 811016 | tf_op jit(solution)/shard_map/ppermute | solution.py:387
  45.3 2.4 %collective-permute-start.10 = (s16[1056,128]{1,0:T(8,128)(2,1)S(1)}, s16[1056,128]{1,0:T(8,128)(2,1)S(1)}, u32[]{:S(2)}, u32[]{:S(2)}) collective-permute-start(s16[1056,128]{1,0:T(8,128)(2,1)S(1)} %spill_1.1), channel_id=1, source_target_pairs={{1,5},{3,7},{5,9},{7,11},{9,13},{11,15},{4,0},{6,2},{8,4},{10,6},{... | collective-permute-start | bytes 811016 | tf_op jit(solution)/shard_map/ppermute | solution.py:387
  49.4 4.8 %collective-permute-done.10.refs_1_ = s16[1056,128]{1,0:T(8,128)(2,1)S(1)} collective-permute-done((s16[1056,128]{1,0:T(8,128)(2,1)S(1)}, s16[1056,128]{1,0:T(8,128)(2,1)S(1)}, u32[]{:S(2)}, u32[]{:S(2)}) %collective-permute-start.10) | collective-permute-done | bytes 270368 | tf_op jit(solution)/shard_map/ppermute | solution.py:387
  54.9 5.9 %collective-permute-start.12 = (s16[528,128]{1,0:T(8,128)(2,1)S(1)}, s16[528,128]{1,0:T(8,128)(2,1)S(1)}, u32[]{:S(2)}, u32[]{:S(2)}) collective-permute-start(s16[528,128]{1,0:T(8,128)(2,1)S(1)} %get-tuple-element.28), channel_id=1, source_target_pairs={{32,64},{64,32},{96,128},{128,96},{160,192},{192,160},{224,0},{0,2... | collective-permute-start | bytes 405512 | tf_op jit(solution)/shard_map/ppermute | solution.py:397
  60.8 3.4 %collective-permute-start.11 = (s16[528,128]{1,0:T(8,128)(2,1)S(1)}, s16[528,128]{1,0:T(8,128)(2,1)S(1)}, u32[]{:S(2)}, u32[]{:S(2)}) collective-permute-start(s16[528,128]{1,0:T(8,128)(2,1)S(1)} %get-tuple-element.27), channel_id=1, source_target_pairs={{0,128},{32,160},{64,192},{96,224},{128,0},{160,32},{192,64},{224,... | collective-permute-start | bytes 405512 | tf_op jit(solution)/shard_map/ppermute | solution.py:394
  64.1 1.8 %collective-permute-done.12.refs_1_ = s16[528,128]{1,0:T(8,128)(2,1)S(1)} collective-permute-done((s16[528,128]{1,0:T(8,128)(2,1)S(1)}, s16[528,128]{1,0:T(8,128)(2,1)S(1)}, u32[]{:S(2)}, u32[]{:S(2)}) %collective-permute-start.12) | collective-permute-done | bytes 135200 | tf_op jit(solution)/shard_map/ppermute | solution.py:397
  66.2 1.9 %collective-permute-done.15.refs_1_ = s16[528,128]{1,0:T(8,128)(2,1)S(1)} collective-permute-done((s16[528,128]{1,0:T(8,128)(2,1)S(1)}, s16[528,128]{1,0:T(8,128)(2,1)S(1)}, u32[]{:S(2)}, u32[]{:S(2)}) %collective-permute-start.15) | collective-permute-done | bytes 135200 | tf_op jit(solution)/shard_map/ppermute | solution.py:397
  68.4 2.7 %collective-permute-start.16 = (s16[528,128]{1,0:T(8,128)(2,1)S(1)}, s16[528,128]{1,0:T(8,128)(2,1)S(1)}, u32[]{:S(2)}, u32[]{:S(2)}) collective-permute-start(s16[528,128]{1,0:T(8,128)(2,1)S(1)} %two_2.1), channel_id=1, source_target_pairs={{32,64},{64,32},{96,128},{128,96},{160,192},{192,160},{224,0},{0,2... | collective-permute-start | bytes 405512 | tf_op jit(solution)/shard_map/ppermute | solution.py:397
  71.1 1.6 %collective-permute-done.11.far_ref = s16[528,128]{1,0:T(8,128)(2,1)S(1)} collective-permute-done((s16[528,128]{1,0:T(8,128)(2,1)S(1)}, s16[528,128]{1,0:T(8,128)(2,1)S(1)}, u32[]{:S(2)}, u32[]{:S(2)}) %collective-permute-start.11) | collective-permute-done | bytes 135200 | tf_op jit(solution)/shard_map/ppermute | solution.py:394
  73.0 2.4 %collective-permute-start.14 = (s16[528,128]{1,0:T(8,128)(2,1)S(1)}, s16[528,128]{1,0:T(8,128)(2,1)S(1)}, u32[]{:S(2)}, u32[]{:S(2)}) collective-permute-start(s16[528,128]{1,0:T(8,128)(2,1)S(1)} %two_1.1), channel_id=1, source_target_pairs={{32,64},{64,32},{96,128},{128,96},{160,192},{192,160},{224,0},{0,2... | collective-permute-start | bytes 405512 | tf_op jit(solution)/shard_map/ppermute | solution.py:397
  76.2 3.1 %collective-permute-done.14.refs_0_ = s16[528,128]{1,0:T(8,128)(2,1)S(1)} collective-permute-done((s16[528,128]{1,0:T(8,128)(2,1)S(1)}, s16[528,128]{1,0:T(8,128)(2,1)S(1)}, u32[]{:S(2)}, u32[]{:S(2)}) %collective-permute-start.14) | collective-permute-done | bytes 135200 | tf_op jit(solution)/shard_map/ppermute | solution.py:397
  79.3 1.4 %collective-permute-done.17.refs_1_ = s16[528,128]{1,0:T(8,128)(2,1)S(1)} collective-permute-done((s16[528,128]{1,0:T(8,128)(2,1)S(1)}, s16[528,128]{1,0:T(8,128)(2,1)S(1)}, u32[]{:S(2)}, u32[]{:S(2)}) %collective-permute-start.17) | collective-permute-done | bytes 135200 | tf_op jit(solution)/shard_map/ppermute | solution.py:397
  (37 shorter events, 7.2 us)
Async XLA Ops:
  0.6 11.6 %copy-start.4 = (bf16[1,2,13]{2,1,0:T(2,128)(2,1)S(1)}, bf16[1,2,13]{2,1,0:T(2,128)(2,1)}, u32[]{:S(2)}) copy-start(bf16[1,2,13]{2,1,0:T(2,128)(2,1)} %taps_ref.1) | copy-start | bytes 160
  1.6 9.1 %collective-permute-start.1 = (bf16[16,4096]{1,0:T(8,128)(2,1)S(1)}, bf16[16,4096]{1,0:T(8,128)(2,1)S(1)}, u32[]{:S(2)}, u32[]{:S(2)}) collective-permute-start(bf16[16,4096]{1,0:T(8,128)(2,1)S(1)} %get-tuple-element.30), channel_id=1, source_target_pairs={{0,1},{1,0},{2,3},{3,2},{4,5},{5,4},{6,7},{7,6},{8,9},{9,8},{10,11... | collective-permute-start | bytes 393224 | tf_op jit(solution)/shard_map/ppermute | solution.py:327
  3.2 9.0 %collective-permute-start = (bf16[16,4096]{1,0:T(8,128)(2,1)S(1)}, bf16[16,4096]{1,0:T(8,128)(2,1)S(1)}, u32[]{:S(2)}, u32[]{:S(2)}) collective-permute-start(bf16[16,4096]{1,0:T(8,128)(2,1)S(1)} %get-tuple-element.31), channel_id=1, source_target_pairs={{1,2},{2,1},{3,4},{4,3},{5,6},{6,5},{7,8},{8,7},{9,10},{10,9},{11,... | collective-permute-start | bytes 393224 | tf_op jit(solution)/shard_map/ppermute | solution.py:326
  12.2 1.5 %copy-start = (bf16[9,128,144]{2,1,0:T(8,128)(2,1)S(1)}, bf16[9,128,144]{2,1,0:T(8,128)(2,1)}, u32[]{:S(2)}) copy-start(bf16[9,128,144]{2,1,0:T(8,128)(2,1)} %constant.20.clone.refs_4_) | copy-start | bytes 995332
  12.2 1.5 %copy-start.1 = (bf16[8,256,128]{2,1,0:T(8,128)(2,1)S(1)}, bf16[8,256,128]{2,1,0:T(8,128)(2,1)}, u32[]{:S(2)}) copy-start(bf16[8,256,128]{2,1,0:T(8,128)(2,1)} %constant.21.clone.refs_5_) | copy-start | bytes 1572868
  12.2 1.5 %copy-start.2 = (s32[1,2,32]{2,1,0:T(2,128)S(1)}, s32[1,2,32]{2,1,0:T(2,128)}, u32[]{:S(2)}) copy-start(s32[1,2,32]{2,1,0:T(2,128)} %refs_1_.3) | copy-start | bytes 772
  12.2 1.5 %copy-start.3 = (s32[1,2,2,32]{3,2,1,0:T(2,128)S(1)}, s32[1,2,2,32]{3,2,1,0:T(2,128)}, u32[]{:S(2)}) copy-start(s32[1,2,2,32]{3,2,1,0:T(2,128)} %refs_2_.3) | copy-start | bytes 1540
  15.7 8.3 %collective-permute-start.2 = (bf16[1056,128]{1,0:T(8,128)(2,1)S(1)}, bf16[1056,128]{1,0:T(8,128)(2,1)S(1)}, u32[]{:S(2)}, u32[]{:S(2)}) collective-permute-start(bf16[1056,128]{1,0:T(8,128)(2,1)S(1)} %get-tuple-element.19), channel_id=1, source_target_pairs={{0,1},{1,2},{2,3},{3,0},{4,5},{5,6},{6,7},{7,4},{8,9},{9,10},{10,1... | collective-permute-start | bytes 811016 | tf_op jit(solution)/shard_map/ppermute | solution.py:366
  15.8 8.2 %collective-permute-start.4 = (bf16[1056,128]{1,0:T(8,128)(2,1)S(1)}, bf16[1056,128]{1,0:T(8,128)(2,1)S(1)}, u32[]{:S(2)}, u32[]{:S(2)}) collective-permute-start(bf16[1056,128]{1,0:T(8,128)(2,1)S(1)} %get-tuple-element.21), channel_id=1, source_target_pairs={{0,3},{1,0},{2,1},{3,2},{4,7},{5,4},{6,5},{7,6},{8,11},{9,8},{10,9... | collective-permute-start | bytes 811016 | tf_op jit(solution)/shard_map/ppermute | solution.py:366
  21.0 8.6 %collective-permute-start.6 = (bf16[1056,128]{1,0:T(8,128)(2,1)S(1)}, bf16[1056,128]{1,0:T(8,128)(2,1)S(1)}, u32[]{:S(2)}, u32[]{:S(2)}) collective-permute-start(bf16[1056,128]{1,0:T(8,128)(2,1)S(1)} %get-tuple-element.23), channel_id=1, source_target_pairs={{0,17},{1,18},{2,19},{3,16},{16,1},{17,2},{18,3},{19,0},{4,21},{5,... | collective-permute-start | bytes 811016 | tf_op jit(solution)/shard_map/ppermute | solution.py:367
  21.1 19.4 %collective-permute-start.8 = (bf16[1056,128]{1,0:T(8,128)(2,1)S(1)}, bf16[1056,128]{1,0:T(8,128)(2,1)S(1)}, u32[]{:S(2)}, u32[]{:S(2)}) collective-permute-start(bf16[1056,128]{1,0:T(8,128)(2,1)S(1)} %get-tuple-element.25), channel_id=1, source_target_pairs={{0,19},{1,16},{2,17},{3,18},{16,3},{17,0},{18,1},{19,2},{4,23},{5,... | collective-permute-start | bytes 811016 | tf_op jit(solution)/shard_map/ppermute | solution.py:367
  24.0 20.5 %collective-permute-start.3 = (bf16[1056,128]{1,0:T(8,128)(2,1)S(1)}, bf16[1056,128]{1,0:T(8,128)(2,1)S(1)}, u32[]{:S(2)}, u32[]{:S(2)}) collective-permute-start(bf16[1056,128]{1,0:T(8,128)(2,1)S(1)} %get-tuple-element.20), channel_id=1, source_target_pairs={{0,2},{1,3},{2,0},{3,1},{4,6},{5,7},{6,4},{7,5},{8,10},{9,11},{10,... | collective-permute-start | bytes 811016 | tf_op jit(solution)/shard_map/ppermute | solution.py:366
  24.0 20.5 %collective-permute-start.5 = (bf16[1056,128]{1,0:T(8,128)(2,1)S(1)}, bf16[1056,128]{1,0:T(8,128)(2,1)S(1)}, u32[]{:S(2)}, u32[]{:S(2)}) collective-permute-start(bf16[1056,128]{1,0:T(8,128)(2,1)S(1)} %get-tuple-element.22), channel_id=1, source_target_pairs={{0,16},{1,17},{2,18},{3,19},{16,0},{17,1},{18,2},{19,3},{4,20},{5,... | collective-permute-start | bytes 811016 | tf_op jit(solution)/shard_map/ppermute | solution.py:367
  24.0 20.5 %collective-permute-start.7 = (bf16[1056,128]{1,0:T(8,128)(2,1)S(1)}, bf16[1056,128]{1,0:T(8,128)(2,1)S(1)}, u32[]{:S(2)}, u32[]{:S(2)}) collective-permute-start(bf16[1056,128]{1,0:T(8,128)(2,1)S(1)} %get-tuple-element.24), channel_id=1, source_target_pairs={{0,18},{1,19},{2,16},{3,17},{16,2},{17,3},{18,0},{19,1},{4,22},{5,... | collective-permute-start | bytes 811016 | tf_op jit(solution)/shard_map/ppermute | solution.py:367
  41.0 8.4 %collective-permute-start.9 = (s16[1056,128]{1,0:T(8,128)(2,1)S(1)}, s16[1056,128]{1,0:T(8,128)(2,1)S(1)}, u32[]{:S(2)}, u32[]{:S(2)}) collective-permute-start(s16[1056,128]{1,0:T(8,128)(2,1)S(1)} %spill_0.1), channel_id=1, source_target_pairs={{0,4},{2,6},{4,8},{6,10},{8,12},{10,14},{5,1},{7,3},{9,5},{11,7},{... | collective-permute-start | bytes 811016 | tf_op jit(solution)/shard_map/ppermute | solution.py:387
  45.3 8.8 %collective-permute-start.10 = (s16[1056,128]{1,0:T(8,128)(2,1)S(1)}, s16[1056,128]{1,0:T(8,128)(2,1)S(1)}, u32[]{:S(2)}, u32[]{:S(2)}) collective-permute-start(s16[1056,128]{1,0:T(8,128)(2,1)S(1)} %spill_1.1), channel_id=1, source_target_pairs={{1,5},{3,7},{5,9},{7,11},{9,13},{11,15},{4,0},{6,2},{8,4},{10,6},{... | collective-permute-start | bytes 811016 | tf_op jit(solution)/shard_map/ppermute | solution.py:387
  54.9 11.1 %collective-permute-start.12 = (s16[528,128]{1,0:T(8,128)(2,1)S(1)}, s16[528,128]{1,0:T(8,128)(2,1)S(1)}, u32[]{:S(2)}, u32[]{:S(2)}) collective-permute-start(s16[528,128]{1,0:T(8,128)(2,1)S(1)} %get-tuple-element.28), channel_id=1, source_target_pairs={{32,64},{64,32},{96,128},{128,96},{160,192},{192,160},{224,0},{0,2... | collective-permute-start | bytes 405512 | tf_op jit(solution)/shard_map/ppermute | solution.py:397
  60.8 7.4 %collective-permute-start.15 = (s16[528,128]{1,0:T(8,128)(2,1)S(1)}, s16[528,128]{1,0:T(8,128)(2,1)S(1)}, u32[]{:S(2)}, u32[]{:S(2)}) collective-permute-start(s16[528,128]{1,0:T(8,128)(2,1)S(1)} %get-tuple-element.29), channel_id=1, source_target_pairs={{0,32},{32,0},{64,96},{96,64},{128,160},{160,128},{192,224},{224,1... | collective-permute-start | bytes 405512 | tf_op jit(solution)/shard_map/ppermute | solution.py:397
  60.8 11.9 %collective-permute-start.11 = (s16[528,128]{1,0:T(8,128)(2,1)S(1)}, s16[528,128]{1,0:T(8,128)(2,1)S(1)}, u32[]{:S(2)}, u32[]{:S(2)}) collective-permute-start(s16[528,128]{1,0:T(8,128)(2,1)S(1)} %get-tuple-element.27), channel_id=1, source_target_pairs={{0,128},{32,160},{64,192},{96,224},{128,0},{160,32},{192,64},{224,... | collective-permute-start | bytes 405512 | tf_op jit(solution)/shard_map/ppermute | solution.py:394
  66.1 6.6 %collective-permute-start.13 = (s16[528,128]{1,0:T(8,128)(2,1)S(1)}, s16[528,128]{1,0:T(8,128)(2,1)S(1)}, u32[]{:S(2)}, u32[]{:S(2)}) collective-permute-start(s16[528,128]{1,0:T(8,128)(2,1)S(1)} %one_2.1), channel_id=1, source_target_pairs={{0,32},{32,0},{64,96},{96,64},{128,160},{160,128},{192,224},{224,1... | collective-permute-start | bytes 405512 | tf_op jit(solution)/shard_map/ppermute | solution.py:397
  68.4 7.0 %collective-permute-start.16 = (s16[528,128]{1,0:T(8,128)(2,1)S(1)}, s16[528,128]{1,0:T(8,128)(2,1)S(1)}, u32[]{:S(2)}, u32[]{:S(2)}) collective-permute-start(s16[528,128]{1,0:T(8,128)(2,1)S(1)} %two_2.1), channel_id=1, source_target_pairs={{32,64},{64,32},{96,128},{128,96},{160,192},{192,160},{224,0},{0,2... | collective-permute-start | bytes 405512 | tf_op jit(solution)/shard_map/ppermute | solution.py:397
  73.0 6.3 %collective-permute-start.14 = (s16[528,128]{1,0:T(8,128)(2,1)S(1)}, s16[528,128]{1,0:T(8,128)(2,1)S(1)}, u32[]{:S(2)}, u32[]{:S(2)}) collective-permute-start(s16[528,128]{1,0:T(8,128)(2,1)S(1)} %two_1.1), channel_id=1, source_target_pairs={{32,64},{64,32},{96,128},{128,96},{160,192},{192,160},{224,0},{0,2... | collective-permute-start | bytes 405512 | tf_op jit(solution)/shard_map/ppermute | solution.py:397
  75.6 5.1 %collective-permute-start.17 = (s16[528,128]{1,0:T(8,128)(2,1)S(1)}, s16[528,128]{1,0:T(8,128)(2,1)S(1)}, u32[]{:S(2)}, u32[]{:S(2)}) collective-permute-start(s16[528,128]{1,0:T(8,128)(2,1)S(1)} %one_1.1), channel_id=1, source_target_pairs={{0,32},{32,0},{64,96},{96,64},{128,160},{160,128},{192,224},{224,1... | collective-permute-start | bytes 405512 | tf_op jit(solution)/shard_map/ppermute | solution.py:397

commit v6 on v5

--- a/solution.py
+++ b/solution.py
@@ -23,7 +23,7 @@
 PIECE = HALF_TILES * TILE + 32
 CELLROW = 4 * TILE + 16
 TOP_CODE = 32000.0
-HOPS = ((1, 3), (2, 0))
+SENDS = (((2, 0), (2, 1)), ((1, 0), (3, 0), (1, 1), (3, 1), (0, 0), (0, 1)))
 LATE = 1
 CHAIN = 3
 f32 = jnp.float32
@@ -162,7 +162,7 @@
             out_ref[r, :, at] = jnp.dot(over_rows[r], window, preferred_element_type=f32).astype(bf16)
 
 
-def warp_kernel(hops, info_ref, patch_ref, class_ref, weight_ref, rows_ref, cols_ref, in_ref, *refs):
+def warp_kernel(sends, info_ref, patch_ref, class_ref, weight_ref, rows_ref, cols_ref, in_ref, *refs):
     out_refs, half_ref = refs[:-1], refs[-1]
     core = lax.axis_index("core")
     line = lax.broadcasted_iota(i32, (32, TILE), 0)
@@ -174,8 +174,8 @@
     down = info_ref[0].astype(f32)
     plan = []
     for n, out_ref in enumerate(out_refs):
-        dest = (lax.axis_index("x") + hops[n // 2]) & 3
-        half = core if n % 2 == 0 else 1 - core
+        dest = (lax.axis_index("x") + sends[n][0]) & 3
+        half = 1 - core if sends[n][1] else core
         marks = jnp.zeros((32, TILE), f32)
         for slot in range(HALF_TILES):
             r, w = divmod(slot, 4)
@@ -351,24 +351,21 @@
     piece = shape((PIECE, TILE), bf16)
     own = [None] * 4
     sib = [None] * 4
-    for hops in HOPS:
+    for sends in SENDS:
         outs = call(
-            lambda *refs, hops=hops: warp_kernel(hops, *refs),
-            "warp_" + "".join(str(h) for h in hops),
-            (piece,) * (2 * len(hops)),
+            lambda *refs, sends=sends: warp_kernel(sends, *refs),
+            f"warp_{len(sends)}",
+            (piece,) * len(sends),
             [SMEM] * 4 + [VMEM] * 3,
-            (VMEM,) * (2 * len(hops)),
-            [pltpu.VMEM((2 * HALF_TILES * len(hops), FRAME, TILE), bf16)],
+            (VMEM,) * len(sends),
+            [pltpu.VMEM((HALF_TILES * len(sends), FRAME, TILE), bf16)],
         )(info, dest_patch, shift_class, exposure_weights, rows, cols, matched)
-        for n, hop in enumerate(hops):
-            own[hop] = outs[2 * n]
-            if hop:
-                own[hop] = lax.ppermute(own[hop], "x", [(i, (i + hop) % 4) for i in range(4)])
-            sib[hop] = lax.ppermute(
-                outs[2 * n + 1],
-                ("core", "x"),
-                [(c * 4 + i, (1 - c) * 4 + (i + hop) % 4) for c in range(2) for i in range(4)],
-            )
+        for (hop, swap), out in zip(sends, outs):
+            if hop or swap:
+                out = lax.ppermute(
+                    out, ("core", "x"), [(c * 4 + i, (c ^ swap) * 4 + (i + hop) % 4) for c in range(2) for i in range(4)]
+                )
+            (sib if swap else own)[hop] = out
     held_rows = shape((8, CELLROW, TILE), f32)
     spill = shape((2 * CELLROW, TILE), i16)
     coded = shape((CELLROW, TILE), i16)

time: 81.7 us -> 79.7 us (0.976)
  waiting for transfers between devices: 29.4 us -> 27.1 us
    ppermute x7, waiting for transfers between devices: 12.8 us -> 6.89 us  [local(): lax.ppermute(out, ('core', 'x'), [(c * 4 + i, (c ^ swap) * 4 + (i + hop)...]
    ppermute x3, starting transfers between devices: 11.1 us -> 7.55 us  [local(): lax.ppermute(two, 'z', pairs[1])]
    ppermute x7, starting transfers between devices: 9.98 us -> 13.4 us  [local(): lax.ppermute(out, ('core', 'x'), [(c * 4 + i, (c ^ swap) * 4 + (i + hop)...]
    ppermute x3, waiting for transfers between devices: 3.32 us -> 5.71 us  [local(): lax.ppermute(one, 'z', pairs[0])]
    ppermute x1, waiting for transfers between devices: 1.6 us -> 3.46 us  [local(): far = lax.ppermute(far, 'z', [(i, (i + 4) % 8) for i in range(8)])]
    ppermute x3, waiting for transfers between devices: 4.92 us -> 3.86 us  [local(): lax.ppermute(two, 'z', pairs[1])]
  transfers between devices with their start and end apart: 18 -> 18, of which waited for: 10 -> 12; matrix products, arithmetic and copies ran while one was open for 0% -> 0% of each run, Pallas kernels for 10% -> 11%
where the time goes in v6:
time: 79.7 us; the launch traced here: 79.5 us
  starting transfers between devices  36.8 us (46%)
  waiting for transfers between devices  27.1 us (34%)
  Pallas kernels  13.1 us (16%)
  between operations  1.48 us (2%)
  local copies, waits for them, and re-layouts  1.01 us (1%)
    ppermute x7, starting transfers between devices, local(): lax.ppermute(out, ('core', 'x'), [(c * 4 + i, (c ^ swap) * 4 + (i + hop)...  13.4 us
    ppermute x3, starting transfers between devices, local(): lax.ppermute(two, 'z', pairs[1])  7.55 us
    ppermute x7, waiting for transfers between devices, local(): lax.ppermute(out, ('core', 'x'), [(c * 4 + i, (c ^ swap) * 4 + (i + hop)...  6.89 us
    ppermute x2, starting transfers between devices, local(): spills.append(lax.ppermute(out, ('y', 'x'), lower + upper))  5.85 us
    ppermute x2, waiting for transfers between devices, local(): spills.append(lax.ppermute(out, ('y', 'x'), lower + upper))  5.77 us
    ppermute x3, waiting for transfers between devices, local(): lax.ppermute(one, 'z', pairs[0])  5.71 us
    pallas_call x2, Pallas kernels, local(): call(lambda *refs, sends=sends: warp_kernel(sends, *refs), f'warp_{len(se...  3.89 us
    ppermute x1, starting transfers between devices, local(): lax.ppermute(outer, ('y', 'x'), [p for i in range(1, 14, 2) for p in ((i,...  3.88 us
  transfers between devices with their start and end apart: 18, of which 12 were waited for; matrix products, arithmetic and copies ran while one was open for 0% of the time, Pallas kernels for 11%

profile of v6, /device:TPU:8, one launch (start us, length us, event | category | flops | bytes accessed | tf_op | source)
XLA Modules:
  0.0 79.5 jit_solution(3739999349434173303)
XLA Ops:
  1.6 1.6 %collective-permute-start.1 = (bf16[16,4096]{1,0:T(8,128)(2,1)S(1)}, bf16[16,4096]{1,0:T(8,128)(2,1)S(1)}, u32[]{:S(2)}, u32[]{:S(2)}) collective-permute-start(bf16[16,4096]{1,0:T(8,128)(2,1)S(1)} %get-tuple-element.30), channel_id=1, source_target_pairs={{0,1},{1,0},{2,3},{3,2},{4,5},{5,4},{6,7},{7,6},{8,9},{9,8},{10,11... | collective-permute-start | bytes 393224 | tf_op jit(solution)/shard_map/ppermute | solution.py:327
  3.2 3.9 %collective-permute-start = (bf16[16,4096]{1,0:T(8,128)(2,1)S(1)}, bf16[16,4096]{1,0:T(8,128)(2,1)S(1)}, u32[]{:S(2)}, u32[]{:S(2)}) collective-permute-start(bf16[16,4096]{1,0:T(8,128)(2,1)S(1)} %get-tuple-element.31), channel_id=1, source_target_pairs={{1,2},{2,1},{3,4},{4,3},{5,6},{6,5},{7,8},{8,7},{9,10},{10,9},{11,... | collective-permute-start | bytes 393224 | tf_op jit(solution)/shard_map/ppermute | solution.py:326
  7.1 3.0 %columns.1 = (bf16[256,4224]{1,0:T(8,128)(2,1)S(1)}, s32[2]{0:T(128)S(1)}) custom-call(bf16[1,2,13]{2,1,0:T(2,128)(2,1)} %taps_ref.1, s32[1,2,32]{2,1,0:T(2,128)} %refs_1_.3, s32[1,2,32]{2,1,0:T(2,128)} %cell_hbm.1, bf16[1,256,4096]{2,1,0:T(8,128)(2,1)} %img_hbm.1), custom_call_target="tpu_custom_call" | custom-call | flops 1 | bytes 1 | tf_op jit(solution)/shard_map/columns/pallas_call | solution.py:329
  10.8 1.4 %collective-permute-done.outer_ref = bf16[16,4096]{1,0:T(8,128)(2,1)S(1)} collective-permute-done((bf16[16,4096]{1,0:T(8,128)(2,1)S(1)}, bf16[16,4096]{1,0:T(8,128)(2,1)S(1)}, u32[]{:S(2)}, u32[]{:S(2)}) %collective-permute-start) | collective-permute-done | bytes 131104 | tf_op jit(solution)/shard_map/ppermute | solution.py:326
  12.2 1.5 %rows.1.refs_6_ = bf16[2,144,4224]{2,1,0:T(8,128)(2,1)S(1)} custom-call(bf16[1,2,13]{2,1,0:T(2,128)(2,1)S(1)} %copy-done.4, bf16[16,4096]{1,0:T(8,128)(2,1)S(1)} %collective-permute-done.outer_ref, bf16[16,4096]{1,0:T(8,128)(2,1)S(1)} %collective-permute-done.1.inner_ref, bf16[256,4224]{1,0:T(8,128)(2,1)S(1)} %get-tuple-element.17.passed_ref), custom_call_target="tpu_custom_call" | custom-call | flops 1 | bytes 1 | tf_op jit(solution)/shard_map/rows/pallas_call | solution.py:343
  13.7 1.4 %warp_2.1 = (bf16[1056,128]{1,0:T(8,128)(2,1)S(1)}, bf16[1056,128]{1,0:T(8,128)(2,1)S(1)}) custom-call(s32[2]{0:T(128)S(1)} %get-tuple-element.16.refs_0_, s32[1,2,32]{2,1,0:T(2,128)S(1)} %copy-done.2, s32[1,2,2,32]{3,2,1,0:T(2,128)S(1)} %copy-done.3, f32[1]{0:T(128)S(6)} %copy.10.refs_3_, bf16[9,128,144]{2,1,0:T(8,128)(2,1)S(1)} %copy-done, ...), custom_call_target="tpu_custom_call" | custom-call | flops 1 | bytes 1 | tf_op jit(solution)/shard_map/warp_2/pallas_call | solution.py:355
  16.4 2.5 %warp_6.1 = (bf16[1056,128]{1,0:T(8,128)(2,1)S(1)}, bf16[1056,128]{1,0:T(8,128)(2,1)S(1)}, bf16[1056,128]{1,0:T(8,128)(2,1)S(1)}, bf16[1056,128]{1,0:T(8,128)(2,...) custom-call(s32[2]{0:T(128)S(1)} %get-tuple-element.16.refs_0_, s32[1,2,32]{2,1,0:T(2,128)S(1)} %copy-done.2, ...), custom_call_target="tpu_custom_call" | custom-call | flops 1 | bytes 1 | tf_op jit(solution)/shard_map/warp_6/pallas_call | solution.py:355
  19.0 1.8 %collective-permute-start.2 = (bf16[1056,128]{1,0:T(8,128)(2,1)S(1)}, bf16[1056,128]{1,0:T(8,128)(2,1)S(1)}, u32[]{:S(2)}, u32[]{:S(2)}) collective-permute-start(bf16[1056,128]{1,0:T(8,128)(2,1)S(1)} %get-tuple-element.19), channel_id=1, source_target_pairs={{0,1},{1,2},{2,3},{3,0},{16,17},{17,18},{18,19},{19,16},{4,5},{5,6... | collective-permute-start | bytes 811016 | tf_op jit(solution)/shard_map/ppermute | solution.py:365
  21.6 2.9 %collective-permute-start.4 = (bf16[1056,128]{1,0:T(8,128)(2,1)S(1)}, bf16[1056,128]{1,0:T(8,128)(2,1)S(1)}, u32[]{:S(2)}, u32[]{:S(2)}) collective-permute-start(bf16[1056,128]{1,0:T(8,128)(2,1)S(1)} %get-tuple-element.21), channel_id=1, source_target_pairs={{0,3},{1,0},{2,1},{3,2},{16,19},{17,16},{18,17},{19,18},{4,7},{5,4... | collective-permute-start | bytes 811016 | tf_op jit(solution)/shard_map/ppermute | solution.py:365
  24.4 1.8 %collective-permute-done.3.refs_2_ = bf16[1056,128]{1,0:T(8,128)(2,1)S(1)} collective-permute-done((bf16[1056,128]{1,0:T(8,128)(2,1)S(1)}, bf16[1056,128]{1,0:T(8,128)(2,1)S(1)}, u32[]{:S(2)}, u32[]{:S(2)}) %collective-permute-start.3) | collective-permute-done | bytes 270368 | tf_op jit(solution)/shard_map/ppermute | solution.py:365
  26.8 6.6 %collective-permute-start.8 = (bf16[1056,128]{1,0:T(8,128)(2,1)S(1)}, bf16[1056,128]{1,0:T(8,128)(2,1)S(1)}, u32[]{:S(2)}, u32[]{:S(2)}) collective-permute-start(bf16[1056,128]{1,0:T(8,128)(2,1)S(1)} %get-tuple-element.25), channel_id=1, source_target_pairs={{0,19},{1,16},{2,17},{3,18},{16,3},{17,0},{18,1},{19,2},{4,23},{5,... | collective-permute-start | bytes 811016 | tf_op jit(solution)/shard_map/ppermute | solution.py:365
  34.0 2.4 %collective-permute-start.10 = (s16[1056,128]{1,0:T(8,128)(2,1)S(1)}, s16[1056,128]{1,0:T(8,128)(2,1)S(1)}, u32[]{:S(2)}, u32[]{:S(2)}) collective-permute-start(s16[1056,128]{1,0:T(8,128)(2,1)S(1)} %spill_1.1), channel_id=1, source_target_pairs={{1,5},{3,7},{5,9},{7,11},{9,13},{11,15},{4,0},{6,2},{8,4},{10,6},{... | collective-permute-start | bytes 811016 | tf_op jit(solution)/shard_map/ppermute | solution.py:384
  37.1 3.7 %collective-permute-done.6.refs_5_.refs_1_ = bf16[1056,128]{1,0:T(8,128)(2,1)S(1)} collective-permute-done((bf16[1056,128]{1,0:T(8,128)(2,1)S(1)}, bf16[1056,128]{1,0:T(8,128)(2,1)S(1)}, u32[]{:S(2)}, u32[]{:S(2)}) %collective-permute-start.6) | collective-permute-done | bytes 270368 | tf_op jit(solution)/shard_map/ppermute | solution.py:365
  41.6 3.5 %collective-permute-start.9 = (s16[1056,128]{1,0:T(8,128)(2,1)S(1)}, s16[1056,128]{1,0:T(8,128)(2,1)S(1)}, u32[]{:S(2)}, u32[]{:S(2)}) collective-permute-start(s16[1056,128]{1,0:T(8,128)(2,1)S(1)} %spill_0.1), channel_id=1, source_target_pairs={{0,4},{2,6},{4,8},{6,10},{8,12},{10,14},{5,1},{7,3},{9,5},{11,7},{... | collective-permute-start | bytes 811016 | tf_op jit(solution)/shard_map/ppermute | solution.py:384
  45.1 1.0 %place.1.in_ref = f32[8,528,128]{2,1,0:T(8,128)S(1)} custom-call(bf16[1056,128]{1,0:T(8,128)(2,1)S(1)} %get-tuple-element.18.refs_0_, bf16[1056,128]{1,0:T(8,128)(2,1)S(1)} %collective-permute-done.2.refs_1_.refs_0_, bf16[1056,128]{1,0:T(8,128)(2,1)S(1)} %collective-permute-done.3.refs_2_, bf16[1056,128]{1,0:T(8,128)(2,1)S(1)} %collective-permute-done.4.refs_3_.refs_2_, ...), custom_call_target="tpu_custom_call" | custom-call | flops 1 | bytes 1 | tf_op jit(solution)/shard_map/place/pallas_call | solution.py:385
  46.1 5.8 %collective-permute-done.9.refs_0_ = s16[1056,128]{1,0:T(8,128)(2,1)S(1)} collective-permute-done((s16[1056,128]{1,0:T(8,128)(2,1)S(1)}, s16[1056,128]{1,0:T(8,128)(2,1)S(1)}, u32[]{:S(2)}, u32[]{:S(2)}) %collective-permute-start.9) | collective-permute-done | bytes 270368 | tf_op jit(solution)/shard_map/ppermute | solution.py:384
  52.6 5.9 %collective-permute-start.12 = (s16[528,128]{1,0:T(8,128)(2,1)S(1)}, s16[528,128]{1,0:T(8,128)(2,1)S(1)}, u32[]{:S(2)}, u32[]{:S(2)}) collective-permute-start(s16[528,128]{1,0:T(8,128)(2,1)S(1)} %get-tuple-element.28), channel_id=1, source_target_pairs={{32,64},{64,32},{96,128},{128,96},{160,192},{192,160},{224,0},{0,2... | collective-permute-start | bytes 405512 | tf_op jit(solution)/shard_map/ppermute | solution.py:394
  58.6 3.4 %collective-permute-start.11 = (s16[528,128]{1,0:T(8,128)(2,1)S(1)}, s16[528,128]{1,0:T(8,128)(2,1)S(1)}, u32[]{:S(2)}, u32[]{:S(2)}) collective-permute-start(s16[528,128]{1,0:T(8,128)(2,1)S(1)} %get-tuple-element.27), channel_id=1, source_target_pairs={{0,128},{32,160},{64,192},{96,224},{128,0},{160,32},{192,64},{224,... | collective-permute-start | bytes 405512 | tf_op jit(solution)/shard_map/ppermute | solution.py:391
  62.6 4.2 %collective-permute-done.15.refs_1_ = s16[528,128]{1,0:T(8,128)(2,1)S(1)} collective-permute-done((s16[528,128]{1,0:T(8,128)(2,1)S(1)}, s16[528,128]{1,0:T(8,128)(2,1)S(1)}, u32[]{:S(2)}, u32[]{:S(2)}) %collective-permute-start.15) | collective-permute-done | bytes 135200 | tf_op jit(solution)/shard_map/ppermute | solution.py:394
  67.1 3.5 %collective-permute-done.11.far_ref = s16[528,128]{1,0:T(8,128)(2,1)S(1)} collective-permute-done((s16[528,128]{1,0:T(8,128)(2,1)S(1)}, s16[528,128]{1,0:T(8,128)(2,1)S(1)}, u32[]{:S(2)}, u32[]{:S(2)}) %collective-permute-start.11) | collective-permute-done | bytes 135200 | tf_op jit(solution)/shard_map/ppermute | solution.py:391
  70.6 1.1 %collective-permute-done.13.refs_1_ = s16[528,128]{1,0:T(8,128)(2,1)S(1)} collective-permute-done((s16[528,128]{1,0:T(8,128)(2,1)S(1)}, s16[528,128]{1,0:T(8,128)(2,1)S(1)}, u32[]{:S(2)}, u32[]{:S(2)}) %collective-permute-start.13) | collective-permute-done | bytes 135200 | tf_op jit(solution)/shard_map/ppermute | solution.py:394
  71.9 1.5 %collective-permute-start.14 = (s16[528,128]{1,0:T(8,128)(2,1)S(1)}, s16[528,128]{1,0:T(8,128)(2,1)S(1)}, u32[]{:S(2)}, u32[]{:S(2)}) collective-permute-start(s16[528,128]{1,0:T(8,128)(2,1)S(1)} %two_1.1), channel_id=1, source_target_pairs={{32,64},{64,32},{96,128},{128,96},{160,192},{192,160},{224,0},{0,2... | collective-permute-start | bytes 405512 | tf_op jit(solution)/shard_map/ppermute | solution.py:394
  73.6 1.1 %collective-permute-start.17 = (s16[528,128]{1,0:T(8,128)(2,1)S(1)}, s16[528,128]{1,0:T(8,128)(2,1)S(1)}, u32[]{:S(2)}, u32[]{:S(2)}) collective-permute-start(s16[528,128]{1,0:T(8,128)(2,1)S(1)} %one_1.1), channel_id=1, source_target_pairs={{0,32},{32,0},{64,96},{96,64},{128,160},{160,128},{192,224},{224,1... | collective-permute-start | bytes 405512 | tf_op jit(solution)/shard_map/ppermute | solution.py:394
  74.7 3.5 %collective-permute-done.14.refs_0_ = s16[528,128]{1,0:T(8,128)(2,1)S(1)} collective-permute-done((s16[528,128]{1,0:T(8,128)(2,1)S(1)}, s16[528,128]{1,0:T(8,128)(2,1)S(1)}, u32[]{:S(2)}, u32[]{:S(2)}) %collective-permute-start.14) | collective-permute-done | bytes 135200 | tf_op jit(solution)/shard_map/ppermute | solution.py:394
  (37 shorter events, 9.2 us)
Async XLA Ops:
  0.6 11.6 %copy-start.4 = (bf16[1,2,13]{2,1,0:T(2,128)(2,1)S(1)}, bf16[1,2,13]{2,1,0:T(2,128)(2,1)}, u32[]{:S(2)}) copy-start(bf16[1,2,13]{2,1,0:T(2,128)(2,1)} %taps_ref.1) | copy-start | bytes 160
  1.6 9.1 %collective-permute-start.1 = (bf16[16,4096]{1,0:T(8,128)(2,1)S(1)}, bf16[16,4096]{1,0:T(8,128)(2,1)S(1)}, u32[]{:S(2)}, u32[]{:S(2)}) collective-permute-start(bf16[16,4096]{1,0:T(8,128)(2,1)S(1)} %get-tuple-element.30), channel_id=1, source_target_pairs={{0,1},{1,0},{2,3},{3,2},{4,5},{5,4},{6,7},{7,6},{8,9},{9,8},{10,11... | collective-permute-start | bytes 393224 | tf_op jit(solution)/shard_map/ppermute | solution.py:327
  3.2 9.0 %collective-permute-start = (bf16[16,4096]{1,0:T(8,128)(2,1)S(1)}, bf16[16,4096]{1,0:T(8,128)(2,1)S(1)}, u32[]{:S(2)}, u32[]{:S(2)}) collective-permute-start(bf16[16,4096]{1,0:T(8,128)(2,1)S(1)} %get-tuple-element.31), channel_id=1, source_target_pairs={{1,2},{2,1},{3,4},{4,3},{5,6},{6,5},{7,8},{8,7},{9,10},{10,9},{11,... | collective-permute-start | bytes 393224 | tf_op jit(solution)/shard_map/ppermute | solution.py:326
  12.2 1.5 %copy-start = (bf16[9,128,144]{2,1,0:T(8,128)(2,1)S(1)}, bf16[9,128,144]{2,1,0:T(8,128)(2,1)}, u32[]{:S(2)}) copy-start(bf16[9,128,144]{2,1,0:T(8,128)(2,1)} %constant.20.clone.refs_4_) | copy-start | bytes 995332
  12.2 1.5 %copy-start.1 = (bf16[8,256,128]{2,1,0:T(8,128)(2,1)S(1)}, bf16[8,256,128]{2,1,0:T(8,128)(2,1)}, u32[]{:S(2)}) copy-start(bf16[8,256,128]{2,1,0:T(8,128)(2,1)} %constant.21.clone.refs_5_) | copy-start | bytes 1572868
  12.2 1.5 %copy-start.2 = (s32[1,2,32]{2,1,0:T(2,128)S(1)}, s32[1,2,32]{2,1,0:T(2,128)}, u32[]{:S(2)}) copy-start(s32[1,2,32]{2,1,0:T(2,128)} %refs_1_.3) | copy-start | bytes 772
  12.2 1.5 %copy-start.3 = (s32[1,2,2,32]{3,2,1,0:T(2,128)S(1)}, s32[1,2,2,32]{3,2,1,0:T(2,128)}, u32[]{:S(2)}) copy-start(s32[1,2,2,32]{3,2,1,0:T(2,128)} %refs_2_.3) | copy-start | bytes 1540
  15.1 11.1 %collective-permute-start.3 = (bf16[1056,128]{1,0:T(8,128)(2,1)S(1)}, bf16[1056,128]{1,0:T(8,128)(2,1)S(1)}, u32[]{:S(2)}, u32[]{:S(2)}) collective-permute-start(bf16[1056,128]{1,0:T(8,128)(2,1)S(1)} %get-tuple-element.20), channel_id=1, source_target_pairs={{0,2},{1,3},{2,0},{3,1},{16,18},{17,19},{18,16},{19,17},{4,6},{5,7... | collective-permute-start | bytes 811016 | tf_op jit(solution)/shard_map/ppermute | solution.py:365
  15.8 11.0 %collective-permute-start.7 = (bf16[1056,128]{1,0:T(8,128)(2,1)S(1)}, bf16[1056,128]{1,0:T(8,128)(2,1)S(1)}, u32[]{:S(2)}, u32[]{:S(2)}) collective-permute-start(bf16[1056,128]{1,0:T(8,128)(2,1)S(1)} %get-tuple-element.24), channel_id=1, source_target_pairs={{0,18},{1,19},{2,16},{3,17},{16,2},{17,3},{18,0},{19,1},{4,22},{5,... | collective-permute-start | bytes 811016 | tf_op jit(solution)/shard_map/ppermute | solution.py:365
  19.0 17.4 %collective-permute-start.2 = (bf16[1056,128]{1,0:T(8,128)(2,1)S(1)}, bf16[1056,128]{1,0:T(8,128)(2,1)S(1)}, u32[]{:S(2)}, u32[]{:S(2)}) collective-permute-start(bf16[1056,128]{1,0:T(8,128)(2,1)S(1)} %get-tuple-element.19), channel_id=1, source_target_pairs={{0,1},{1,2},{2,3},{3,0},{16,17},{17,18},{18,19},{19,16},{4,5},{5,6... | collective-permute-start | bytes 811016 | tf_op jit(solution)/shard_map/ppermute | solution.py:365
  20.8 12.7 %collective-permute-start.5 = (bf16[1056,128]{1,0:T(8,128)(2,1)S(1)}, bf16[1056,128]{1,0:T(8,128)(2,1)S(1)}, u32[]{:S(2)}, u32[]{:S(2)}) collective-permute-start(bf16[1056,128]{1,0:T(8,128)(2,1)S(1)} %get-tuple-element.22), channel_id=1, source_target_pairs={{0,16},{1,17},{2,18},{3,19},{16,0},{17,1},{18,2},{19,3},{4,20},{5,... | collective-permute-start | bytes 811016 | tf_op jit(solution)/shard_map/ppermute | solution.py:365
  21.6 15.6 %collective-permute-start.4 = (bf16[1056,128]{1,0:T(8,128)(2,1)S(1)}, bf16[1056,128]{1,0:T(8,128)(2,1)S(1)}, u32[]{:S(2)}, u32[]{:S(2)}) collective-permute-start(bf16[1056,128]{1,0:T(8,128)(2,1)S(1)} %get-tuple-element.21), channel_id=1, source_target_pairs={{0,3},{1,0},{2,1},{3,2},{16,19},{17,16},{18,17},{19,18},{4,7},{5,4... | collective-permute-start | bytes 811016 | tf_op jit(solution)/shard_map/ppermute | solution.py:365
  26.2 14.7 %collective-permute-start.6 = (bf16[1056,128]{1,0:T(8,128)(2,1)S(1)}, bf16[1056,128]{1,0:T(8,128)(2,1)S(1)}, u32[]{:S(2)}, u32[]{:S(2)}) collective-permute-start(bf16[1056,128]{1,0:T(8,128)(2,1)S(1)} %get-tuple-element.23), channel_id=1, source_target_pairs={{0,17},{1,18},{2,19},{3,16},{16,1},{17,2},{18,3},{19,0},{4,21},{5,... | collective-permute-start | bytes 811016 | tf_op jit(solution)/shard_map/ppermute | solution.py:365
  26.8 14.1 %collective-permute-start.8 = (bf16[1056,128]{1,0:T(8,128)(2,1)S(1)}, bf16[1056,128]{1,0:T(8,128)(2,1)S(1)}, u32[]{:S(2)}, u32[]{:S(2)}) collective-permute-start(bf16[1056,128]{1,0:T(8,128)(2,1)S(1)} %get-tuple-element.25), channel_id=1, source_target_pairs={{0,19},{1,16},{2,17},{3,18},{16,3},{17,0},{18,1},{19,2},{4,23},{5,... | collective-permute-start | bytes 811016 | tf_op jit(solution)/shard_map/ppermute | solution.py:365
  34.0 12.2 %collective-permute-start.10 = (s16[1056,128]{1,0:T(8,128)(2,1)S(1)}, s16[1056,128]{1,0:T(8,128)(2,1)S(1)}, u32[]{:S(2)}, u32[]{:S(2)}) collective-permute-start(s16[1056,128]{1,0:T(8,128)(2,1)S(1)} %spill_1.1), channel_id=1, source_target_pairs={{1,5},{3,7},{5,9},{7,11},{9,13},{11,15},{4,0},{6,2},{8,4},{10,6},{... | collective-permute-start | bytes 811016 | tf_op jit(solution)/shard_map/ppermute | solution.py:384
  41.6 10.3 %collective-permute-start.9 = (s16[1056,128]{1,0:T(8,128)(2,1)S(1)}, s16[1056,128]{1,0:T(8,128)(2,1)S(1)}, u32[]{:S(2)}, u32[]{:S(2)}) collective-permute-start(s16[1056,128]{1,0:T(8,128)(2,1)S(1)} %spill_0.1), channel_id=1, source_target_pairs={{0,4},{2,6},{4,8},{6,10},{8,12},{10,14},{5,1},{7,3},{9,5},{11,7},{... | collective-permute-start | bytes 811016 | tf_op jit(solution)/shard_map/ppermute | solution.py:384
  52.6 9.7 %collective-permute-start.12 = (s16[528,128]{1,0:T(8,128)(2,1)S(1)}, s16[528,128]{1,0:T(8,128)(2,1)S(1)}, u32[]{:S(2)}, u32[]{:S(2)}) collective-permute-start(s16[528,128]{1,0:T(8,128)(2,1)S(1)} %get-tuple-element.28), channel_id=1, source_target_pairs={{32,64},{64,32},{96,128},{128,96},{160,192},{192,160},{224,0},{0,2... | collective-permute-start | bytes 405512 | tf_op jit(solution)/shard_map/ppermute | solution.py:394
  58.6 8.2 %collective-permute-start.15 = (s16[528,128]{1,0:T(8,128)(2,1)S(1)}, s16[528,128]{1,0:T(8,128)(2,1)S(1)}, u32[]{:S(2)}, u32[]{:S(2)}) collective-permute-start(s16[528,128]{1,0:T(8,128)(2,1)S(1)} %get-tuple-element.29), channel_id=1, source_target_pairs={{0,32},{32,0},{64,96},{96,64},{128,160},{160,128},{192,224},{224,1... | collective-permute-start | bytes 405512 | tf_op jit(solution)/shard_map/ppermute | solution.py:394
  58.6 12.0 %collective-permute-start.11 = (s16[528,128]{1,0:T(8,128)(2,1)S(1)}, s16[528,128]{1,0:T(8,128)(2,1)S(1)}, u32[]{:S(2)}, u32[]{:S(2)}) collective-permute-start(s16[528,128]{1,0:T(8,128)(2,1)S(1)} %get-tuple-element.27), channel_id=1, source_target_pairs={{0,128},{32,160},{64,192},{96,224},{128,0},{160,32},{192,64},{224,... | collective-permute-start | bytes 405512 | tf_op jit(solution)/shard_map/ppermute | solution.py:391
  62.5 9.2 %collective-permute-start.13 = (s16[528,128]{1,0:T(8,128)(2,1)S(1)}, s16[528,128]{1,0:T(8,128)(2,1)S(1)}, u32[]{:S(2)}, u32[]{:S(2)}) collective-permute-start(s16[528,128]{1,0:T(8,128)(2,1)S(1)} %one_2.1), channel_id=1, source_target_pairs={{0,32},{32,0},{64,96},{96,64},{128,160},{160,128},{192,224},{224,1... | collective-permute-start | bytes 405512 | tf_op jit(solution)/shard_map/ppermute | solution.py:394
  67.0 6.4 %collective-permute-start.16 = (s16[528,128]{1,0:T(8,128)(2,1)S(1)}, s16[528,128]{1,0:T(8,128)(2,1)S(1)}, u32[]{:S(2)}, u32[]{:S(2)}) collective-permute-start(s16[528,128]{1,0:T(8,128)(2,1)S(1)} %two_2.1), channel_id=1, source_target_pairs={{32,64},{64,32},{96,128},{128,96},{160,192},{192,160},{224,0},{0,2... | collective-permute-start | bytes 405512 | tf_op jit(solution)/shard_map/ppermute | solution.py:394
  71.9 6.3 %collective-permute-start.14 = (s16[528,128]{1,0:T(8,128)(2,1)S(1)}, s16[528,128]{1,0:T(8,128)(2,1)S(1)}, u32[]{:S(2)}, u32[]{:S(2)}) collective-permute-start(s16[528,128]{1,0:T(8,128)(2,1)S(1)} %two_1.1), channel_id=1, source_target_pairs={{32,64},{64,32},{96,128},{128,96},{160,192},{192,160},{224,0},{0,2... | collective-permute-start | bytes 405512 | tf_op jit(solution)/shard_map/ppermute | solution.py:394
  73.6 5.1 %collective-permute-start.17 = (s16[528,128]{1,0:T(8,128)(2,1)S(1)}, s16[528,128]{1,0:T(8,128)(2,1)S(1)}, u32[]{:S(2)}, u32[]{:S(2)}) collective-permute-start(s16[528,128]{1,0:T(8,128)(2,1)S(1)} %one_1.1), channel_id=1, source_target_pairs={{0,32},{32,0},{64,96},{96,64},{128,160},{160,128},{192,224},{224,1... | collective-permute-start | bytes 405512 | tf_op jit(solution)/shard_map/ppermute | solution.py:394

commit v7 on v6

--- a/solution.py
+++ b/solution.py
@@ -109,7 +109,7 @@
         out_ref[:, b * TILE : (b + 1) * TILE] = jnp.dot(window, weights, preferred_element_type=f32).astype(bf16)
 
 
-def rows_kernel(taps_ref, outer_ref, inner_ref, passed_ref, out_ref, window_ref, edge_ref):
+def rows_kernel(taps_ref, inner_ref, outer_ref, passed_ref, out_ref, window_ref, edge_ref):
     patch = lax.axis_index("y") * 4 + lax.axis_index("x")
     taps = taps_ref[0].astype(f32)
     over_cols = banded(taps[1:2], (2 * TILE, TILE), 0).astype(bf16)
@@ -347,7 +347,7 @@
         [VMEM] * 4,
         VMEM,
         [pltpu.VMEM((BLOCKS * 2 * HALO, 2 * TILE), bf16), pltpu.VMEM((2 * HALO, BLOCKS * TILE), bf16)],
-    )(psf_taps, outer, inner, passed)
+    )(psf_taps, inner, outer, passed)
     piece = shape((PIECE, TILE), bf16)
     own = [None] * 4
     sib = [None] * 4

time: 79.7 us -> 79.4 us (level)
  starting transfers between devices: 36.8 us -> 33.7 us
  waiting for transfers between devices: 27.1 us -> 29.7 us
    ppermute x7, waiting for transfers between devices: 6.89 us -> 9.79 us  [local(): lax.ppermute(out, ('core', 'x'), [(c * 4 + i, (c ^ swap) * 4 + (i + hop)...]
    ppermute x7, starting transfers between devices: 13.4 us -> 10.8 us  [local(): lax.ppermute(out, ('core', 'x'), [(c * 4 + i, (c ^ swap) * 4 + (i + hop)...]
    ppermute x1, starting transfers between devices: 1.58 us -> 0.42 us  [local(): lax.ppermute(inner, ('y', 'x'), [p for i in range(0, 15, 2) for p in ((i,...]
    ppermute x1, waiting for transfers between devices: 1.4 us -> 0.6 us  [local(): lax.ppermute(outer, ('y', 'x'), [p for i in range(1, 14, 2) for p in ((i,...]
where the time goes in v7:
time: 79.4 us; the launch traced here: 79.1 us
  starting transfers between devices  33.7 us (42%)
  waiting for transfers between devices  29.7 us (37%)
  Pallas kernels  13.2 us (17%)
  between operations  1.48 us (2%)
  local copies, waits for them, and re-layouts  1.01 us (1%)
    ppermute x7, starting transfers between devices, local(): lax.ppermute(out, ('core', 'x'), [(c * 4 + i, (c ^ swap) * 4 + (i + hop)...  10.8 us
    ppermute x7, waiting for transfers between devices, local(): lax.ppermute(out, ('core', 'x'), [(c * 4 + i, (c ^ swap) * 4 + (i + hop)...  9.79 us
    ppermute x3, starting transfers between devices, local(): lax.ppermute(two, 'z', pairs[1])  7.5 us
    ppermute x3, waiting for transfers between devices, local(): lax.ppermute(one, 'z', pairs[0])  6.4 us
    ppermute x2, starting transfers between devices, local(): spills.append(lax.ppermute(out, ('y', 'x'), lower + upper))  5.84 us
    ppermute x2, waiting for transfers between devices, local(): spills.append(lax.ppermute(out, ('y', 'x'), lower + upper))  5.8 us
    ppermute x1, starting transfers between devices, local(): lax.ppermute(outer, ('y', 'x'), [p for i in range(1, 14, 2) for p in ((i,...  4.55 us
    pallas_call x2, Pallas kernels, local(): call(lambda *refs, sends=sends: warp_kernel(sends, *refs), f'warp_{len(se...  3.89 us
  transfers between devices with their start and end apart: 18, of which 12 were waited for; matrix products, arithmetic and copies ran while one was open for 0% of the time, Pallas kernels for 11%

profile of v7, /device:TPU:8, one launch (start us, length us, event | category | flops | bytes accessed | tf_op | source)
XLA Modules:
  0.0 79.1 jit_solution(4920376006683351541)
XLA Ops:
  1.6 4.6 %collective-permute-start.1 = (bf16[16,4096]{1,0:T(8,128)(2,1)S(1)}, bf16[16,4096]{1,0:T(8,128)(2,1)S(1)}, u32[]{:S(2)}, u32[]{:S(2)}) collective-permute-start(bf16[16,4096]{1,0:T(8,128)(2,1)S(1)} %get-tuple-element.30), channel_id=1, source_target_pairs={{1,2},{2,1},{3,4},{4,3},{5,6},{6,5},{7,8},{8,7},{9,10},{10,9},{11,... | collective-permute-start | bytes 393224 | tf_op jit(solution)/shard_map/ppermute | solution.py:326
  6.6 3.0 %columns.1 = (bf16[256,4224]{1,0:T(8,128)(2,1)S(1)}, s32[2]{0:T(128)S(1)}) custom-call(bf16[1,2,13]{2,1,0:T(2,128)(2,1)} %taps_ref.1, s32[1,2,32]{2,1,0:T(2,128)} %refs_1_.3, s32[1,2,32]{2,1,0:T(2,128)} %cell_hbm.1, bf16[1,256,4096]{2,1,0:T(8,128)(2,1)} %img_hbm.1), custom_call_target="tpu_custom_call" | custom-call | flops 1 | bytes 1 | tf_op jit(solution)/shard_map/columns/pallas_call | solution.py:329
  11.3 1.5 %rows.1.refs_6_ = bf16[2,144,4224]{2,1,0:T(8,128)(2,1)S(1)} custom-call(bf16[1,2,13]{2,1,0:T(2,128)(2,1)S(1)} %copy-done.4, bf16[16,4096]{1,0:T(8,128)(2,1)S(1)} %collective-permute-done.inner_ref, bf16[16,4096]{1,0:T(8,128)(2,1)S(1)} %collective-permute-done.1.outer_ref, bf16[256,4224]{1,0:T(8,128)(2,1)S(1)} %get-tuple-element.17.passed_ref), custom_call_target="tpu_custom_call" | custom-call | flops 1 | bytes 1 | tf_op jit(solution)/shard_map/rows/pallas_call | solution.py:343
  12.8 1.4 %warp_2.1 = (bf16[1056,128]{1,0:T(8,128)(2,1)S(1)}, bf16[1056,128]{1,0:T(8,128)(2,1)S(1)}) custom-call(s32[2]{0:T(128)S(1)} %get-tuple-element.16.refs_0_, s32[1,2,32]{2,1,0:T(2,128)S(1)} %copy-done.2, s32[1,2,2,32]{3,2,1,0:T(2,128)S(1)} %copy-done.3, f32[1]{0:T(128)S(6)} %copy.10.refs_3_, bf16[9,128,144]{2,1,0:T(8,128)(2,1)S(1)} %copy-done, ...), custom_call_target="tpu_custom_call" | custom-call | flops 1 | bytes 1 | tf_op jit(solution)/shard_map/warp_2/pallas_call | solution.py:355
  14.2 1.9 %collective-permute-start.3 = (bf16[1056,128]{1,0:T(8,128)(2,1)S(1)}, bf16[1056,128]{1,0:T(8,128)(2,1)S(1)}, u32[]{:S(2)}, u32[]{:S(2)}) collective-permute-start(bf16[1056,128]{1,0:T(8,128)(2,1)S(1)} %get-tuple-element.20), channel_id=1, source_target_pairs={{0,2},{1,3},{2,0},{3,1},{16,18},{17,19},{18,16},{19,17},{4,6},{5,7... | collective-permute-start | bytes 811016 | tf_op jit(solution)/shard_map/ppermute | solution.py:365
  16.1 2.5 %warp_6.1 = (bf16[1056,128]{1,0:T(8,128)(2,1)S(1)}, bf16[1056,128]{1,0:T(8,128)(2,1)S(1)}, bf16[1056,128]{1,0:T(8,128)(2,1)S(1)}, bf16[1056,128]{1,0:T(8,128)(2,...) custom-call(s32[2]{0:T(128)S(1)} %get-tuple-element.16.refs_0_, s32[1,2,32]{2,1,0:T(2,128)S(1)} %copy-done.2, ...), custom_call_target="tpu_custom_call" | custom-call | flops 1 | bytes 1 | tf_op jit(solution)/shard_map/warp_6/pallas_call | solution.py:355
  18.6 1.5 %collective-permute-start.2 = (bf16[1056,128]{1,0:T(8,128)(2,1)S(1)}, bf16[1056,128]{1,0:T(8,128)(2,1)S(1)}, u32[]{:S(2)}, u32[]{:S(2)}) collective-permute-start(bf16[1056,128]{1,0:T(8,128)(2,1)S(1)} %get-tuple-element.19), channel_id=1, source_target_pairs={{0,1},{1,2},{2,3},{3,0},{16,17},{17,18},{18,19},{19,16},{4,5},{5,6... | collective-permute-start | bytes 811016 | tf_op jit(solution)/shard_map/ppermute | solution.py:365
  21.0 2.5 %collective-permute-start.4 = (bf16[1056,128]{1,0:T(8,128)(2,1)S(1)}, bf16[1056,128]{1,0:T(8,128)(2,1)S(1)}, u32[]{:S(2)}, u32[]{:S(2)}) collective-permute-start(bf16[1056,128]{1,0:T(8,128)(2,1)S(1)} %get-tuple-element.21), channel_id=1, source_target_pairs={{0,3},{1,0},{2,1},{3,2},{16,19},{17,16},{18,17},{19,18},{4,7},{5,4... | collective-permute-start | bytes 811016 | tf_op jit(solution)/shard_map/ppermute | solution.py:365
  23.5 1.7 %collective-permute-done.3.refs_2_ = bf16[1056,128]{1,0:T(8,128)(2,1)S(1)} collective-permute-done((bf16[1056,128]{1,0:T(8,128)(2,1)S(1)}, bf16[1056,128]{1,0:T(8,128)(2,1)S(1)}, u32[]{:S(2)}, u32[]{:S(2)}) %collective-permute-start.3) | collective-permute-done | bytes 270368 | tf_op jit(solution)/shard_map/ppermute | solution.py:365
  25.2 3.6 %collective-permute-done.7.refs_6_.refs_3_ = bf16[1056,128]{1,0:T(8,128)(2,1)S(1)} collective-permute-done((bf16[1056,128]{1,0:T(8,128)(2,1)S(1)}, bf16[1056,128]{1,0:T(8,128)(2,1)S(1)}, u32[]{:S(2)}, u32[]{:S(2)}) %collective-permute-start.7) | collective-permute-done | bytes 270368 | tf_op jit(solution)/shard_map/ppermute | solution.py:365
  28.8 4.0 %collective-permute-start.8 = (bf16[1056,128]{1,0:T(8,128)(2,1)S(1)}, bf16[1056,128]{1,0:T(8,128)(2,1)S(1)}, u32[]{:S(2)}, u32[]{:S(2)}) collective-permute-start(bf16[1056,128]{1,0:T(8,128)(2,1)S(1)} %get-tuple-element.25), channel_id=1, source_target_pairs={{0,19},{1,16},{2,17},{3,18},{16,3},{17,0},{18,1},{19,2},{4,23},{5,... | collective-permute-start | bytes 811016 | tf_op jit(solution)/shard_map/ppermute | solution.py:365
  33.4 2.4 %collective-permute-start.10 = (s16[1056,128]{1,0:T(8,128)(2,1)S(1)}, s16[1056,128]{1,0:T(8,128)(2,1)S(1)}, u32[]{:S(2)}, u32[]{:S(2)}) collective-permute-start(s16[1056,128]{1,0:T(8,128)(2,1)S(1)} %spill_1.1), channel_id=1, source_target_pairs={{1,5},{3,7},{5,9},{7,11},{9,13},{11,15},{4,0},{6,2},{8,4},{10,6},{... | collective-permute-start | bytes 811016 | tf_op jit(solution)/shard_map/ppermute | solution.py:384
  36.4 3.8 %collective-permute-done.6.refs_5_.refs_1_ = bf16[1056,128]{1,0:T(8,128)(2,1)S(1)} collective-permute-done((bf16[1056,128]{1,0:T(8,128)(2,1)S(1)}, bf16[1056,128]{1,0:T(8,128)(2,1)S(1)}, u32[]{:S(2)}, u32[]{:S(2)}) %collective-permute-start.6) | collective-permute-done | bytes 270368 | tf_op jit(solution)/shard_map/ppermute | solution.py:365
  41.0 3.5 %collective-permute-start.9 = (s16[1056,128]{1,0:T(8,128)(2,1)S(1)}, s16[1056,128]{1,0:T(8,128)(2,1)S(1)}, u32[]{:S(2)}, u32[]{:S(2)}) collective-permute-start(s16[1056,128]{1,0:T(8,128)(2,1)S(1)} %spill_0.1), channel_id=1, source_target_pairs={{0,4},{2,6},{4,8},{6,10},{8,12},{10,14},{5,1},{7,3},{9,5},{11,7},{... | collective-permute-start | bytes 811016 | tf_op jit(solution)/shard_map/ppermute | solution.py:384
  44.5 1.1 %place.1.in_ref = f32[8,528,128]{2,1,0:T(8,128)S(1)} custom-call(bf16[1056,128]{1,0:T(8,128)(2,1)S(1)} %get-tuple-element.18.refs_0_, bf16[1056,128]{1,0:T(8,128)(2,1)S(1)} %collective-permute-done.2.refs_1_.refs_0_, bf16[1056,128]{1,0:T(8,128)(2,1)S(1)} %collective-permute-done.3.refs_2_, bf16[1056,128]{1,0:T(8,128)(2,1)S(1)} %collective-permute-done.4.refs_3_.refs_2_, ...), custom_call_target="tpu_custom_call" | custom-call | flops 1 | bytes 1 | tf_op jit(solution)/shard_map/place/pallas_call | solution.py:385
  45.6 5.8 %collective-permute-done.9.refs_0_ = s16[1056,128]{1,0:T(8,128)(2,1)S(1)} collective-permute-done((s16[1056,128]{1,0:T(8,128)(2,1)S(1)}, s16[1056,128]{1,0:T(8,128)(2,1)S(1)}, u32[]{:S(2)}, u32[]{:S(2)}) %collective-permute-start.9) | collective-permute-done | bytes 270368 | tf_op jit(solution)/shard_map/ppermute | solution.py:384
  52.1 5.9 %collective-permute-start.12 = (s16[528,128]{1,0:T(8,128)(2,1)S(1)}, s16[528,128]{1,0:T(8,128)(2,1)S(1)}, u32[]{:S(2)}, u32[]{:S(2)}) collective-permute-start(s16[528,128]{1,0:T(8,128)(2,1)S(1)} %get-tuple-element.28), channel_id=1, source_target_pairs={{32,64},{64,32},{96,128},{128,96},{160,192},{192,160},{224,0},{0,2... | collective-permute-start | bytes 405512 | tf_op jit(solution)/shard_map/ppermute | solution.py:394
  58.1 3.4 %collective-permute-start.11 = (s16[528,128]{1,0:T(8,128)(2,1)S(1)}, s16[528,128]{1,0:T(8,128)(2,1)S(1)}, u32[]{:S(2)}, u32[]{:S(2)}) collective-permute-start(s16[528,128]{1,0:T(8,128)(2,1)S(1)} %get-tuple-element.27), channel_id=1, source_target_pairs={{0,128},{32,160},{64,192},{96,224},{128,0},{160,32},{192,64},{224,... | collective-permute-start | bytes 405512 | tf_op jit(solution)/shard_map/ppermute | solution.py:391
  61.8 4.4 %collective-permute-done.15.refs_1_ = s16[528,128]{1,0:T(8,128)(2,1)S(1)} collective-permute-done((s16[528,128]{1,0:T(8,128)(2,1)S(1)}, s16[528,128]{1,0:T(8,128)(2,1)S(1)}, u32[]{:S(2)}, u32[]{:S(2)}) %collective-permute-start.15) | collective-permute-done | bytes 135200 | tf_op jit(solution)/shard_map/ppermute | solution.py:394
  66.6 3.2 %collective-permute-done.11.far_ref = s16[528,128]{1,0:T(8,128)(2,1)S(1)} collective-permute-done((s16[528,128]{1,0:T(8,128)(2,1)S(1)}, s16[528,128]{1,0:T(8,128)(2,1)S(1)}, u32[]{:S(2)}, u32[]{:S(2)}) %collective-permute-start.11) | collective-permute-done | bytes 135200 | tf_op jit(solution)/shard_map/ppermute | solution.py:391
  69.8 1.5 %collective-permute-done.13.refs_1_ = s16[528,128]{1,0:T(8,128)(2,1)S(1)} collective-permute-done((s16[528,128]{1,0:T(8,128)(2,1)S(1)}, s16[528,128]{1,0:T(8,128)(2,1)S(1)}, u32[]{:S(2)}, u32[]{:S(2)}) %collective-permute-start.13) | collective-permute-done | bytes 135200 | tf_op jit(solution)/shard_map/ppermute | solution.py:394
  71.5 1.5 %collective-permute-start.14 = (s16[528,128]{1,0:T(8,128)(2,1)S(1)}, s16[528,128]{1,0:T(8,128)(2,1)S(1)}, u32[]{:S(2)}, u32[]{:S(2)}) collective-permute-start(s16[528,128]{1,0:T(8,128)(2,1)S(1)} %two_1.1), channel_id=1, source_target_pairs={{32,64},{64,32},{96,128},{128,96},{160,192},{192,160},{224,0},{0,2... | collective-permute-start | bytes 405512 | tf_op jit(solution)/shard_map/ppermute | solution.py:394
  73.2 1.1 %collective-permute-start.17 = (s16[528,128]{1,0:T(8,128)(2,1)S(1)}, s16[528,128]{1,0:T(8,128)(2,1)S(1)}, u32[]{:S(2)}, u32[]{:S(2)}) collective-permute-start(s16[528,128]{1,0:T(8,128)(2,1)S(1)} %one_1.1), channel_id=1, source_target_pairs={{0,32},{32,0},{64,96},{96,64},{128,160},{160,128},{192,224},{224,1... | collective-permute-start | bytes 405512 | tf_op jit(solution)/shard_map/ppermute | solution.py:394
  74.3 3.5 %collective-permute-done.14.refs_0_ = s16[528,128]{1,0:T(8,128)(2,1)S(1)} collective-permute-done((s16[528,128]{1,0:T(8,128)(2,1)S(1)}, s16[528,128]{1,0:T(8,128)(2,1)S(1)}, u32[]{:S(2)}, u32[]{:S(2)}) %collective-permute-start.14) | collective-permute-done | bytes 135200 | tf_op jit(solution)/shard_map/ppermute | solution.py:394
  (37 shorter events, 8.3 us)
Async XLA Ops:
  0.6 10.6 %copy-start.4 = (bf16[1,2,13]{2,1,0:T(2,128)(2,1)S(1)}, bf16[1,2,13]{2,1,0:T(2,128)(2,1)}, u32[]{:S(2)}) copy-start(bf16[1,2,13]{2,1,0:T(2,128)(2,1)} %taps_ref.1) | copy-start | bytes 160
  1.6 9.2 %collective-permute-start.1 = (bf16[16,4096]{1,0:T(8,128)(2,1)S(1)}, bf16[16,4096]{1,0:T(8,128)(2,1)S(1)}, u32[]{:S(2)}, u32[]{:S(2)}) collective-permute-start(bf16[16,4096]{1,0:T(8,128)(2,1)S(1)} %get-tuple-element.30), channel_id=1, source_target_pairs={{1,2},{2,1},{3,4},{4,3},{5,6},{6,5},{7,8},{8,7},{9,10},{10,9},{11,... | collective-permute-start | bytes 393224 | tf_op jit(solution)/shard_map/ppermute | solution.py:326
  6.2 5.1 %collective-permute-start = (bf16[16,4096]{1,0:T(8,128)(2,1)S(1)}, bf16[16,4096]{1,0:T(8,128)(2,1)S(1)}, u32[]{:S(2)}, u32[]{:S(2)}) collective-permute-start(bf16[16,4096]{1,0:T(8,128)(2,1)S(1)} %get-tuple-element.31), channel_id=1, source_target_pairs={{0,1},{1,0},{2,3},{3,2},{4,5},{5,4},{6,7},{7,6},{8,9},{9,8},{10,11... | collective-permute-start | bytes 393224 | tf_op jit(solution)/shard_map/ppermute | solution.py:327
  11.3 1.5 %copy-start = (bf16[9,128,144]{2,1,0:T(8,128)(2,1)S(1)}, bf16[9,128,144]{2,1,0:T(8,128)(2,1)}, u32[]{:S(2)}) copy-start(bf16[9,128,144]{2,1,0:T(8,128)(2,1)} %constant.20.clone.refs_4_) | copy-start | bytes 995332
  11.3 1.5 %copy-start.1 = (bf16[8,256,128]{2,1,0:T(8,128)(2,1)S(1)}, bf16[8,256,128]{2,1,0:T(8,128)(2,1)}, u32[]{:S(2)}) copy-start(bf16[8,256,128]{2,1,0:T(8,128)(2,1)} %constant.21.clone.refs_5_) | copy-start | bytes 1572868
  11.3 1.5 %copy-start.2 = (s32[1,2,32]{2,1,0:T(2,128)S(1)}, s32[1,2,32]{2,1,0:T(2,128)}, u32[]{:S(2)}) copy-start(s32[1,2,32]{2,1,0:T(2,128)} %refs_1_.3) | copy-start | bytes 772
  11.3 1.5 %copy-start.3 = (s32[1,2,2,32]{3,2,1,0:T(2,128)S(1)}, s32[1,2,2,32]{3,2,1,0:T(2,128)}, u32[]{:S(2)}) copy-start(s32[1,2,2,32]{3,2,1,0:T(2,128)} %refs_2_.3) | copy-start | bytes 1540
  14.2 11.1 %collective-permute-start.3 = (bf16[1056,128]{1,0:T(8,128)(2,1)S(1)}, bf16[1056,128]{1,0:T(8,128)(2,1)S(1)}, u32[]{:S(2)}, u32[]{:S(2)}) collective-permute-start(bf16[1056,128]{1,0:T(8,128)(2,1)S(1)} %get-tuple-element.20), channel_id=1, source_target_pairs={{0,2},{1,3},{2,0},{3,1},{16,18},{17,19},{18,16},{19,17},{4,6},{5,7... | collective-permute-start | bytes 811016 | tf_op jit(solution)/shard_map/ppermute | solution.py:365
  16.1 12.8 %collective-permute-start.7 = (bf16[1056,128]{1,0:T(8,128)(2,1)S(1)}, bf16[1056,128]{1,0:T(8,128)(2,1)S(1)}, u32[]{:S(2)}, u32[]{:S(2)}) collective-permute-start(bf16[1056,128]{1,0:T(8,128)(2,1)S(1)} %get-tuple-element.24), channel_id=1, source_target_pairs={{0,18},{1,19},{2,16},{3,17},{16,2},{17,3},{18,0},{19,1},{4,22},{5,... | collective-permute-start | bytes 811016 | tf_op jit(solution)/shard_map/ppermute | solution.py:365
  18.6 17.2 %collective-permute-start.2 = (bf16[1056,128]{1,0:T(8,128)(2,1)S(1)}, bf16[1056,128]{1,0:T(8,128)(2,1)S(1)}, u32[]{:S(2)}, u32[]{:S(2)}) collective-permute-start(bf16[1056,128]{1,0:T(8,128)(2,1)S(1)} %get-tuple-element.19), channel_id=1, source_target_pairs={{0,1},{1,2},{2,3},{3,0},{16,17},{17,18},{18,19},{19,16},{4,5},{5,6... | collective-permute-start | bytes 811016 | tf_op jit(solution)/shard_map/ppermute | solution.py:365
  20.2 12.7 %collective-permute-start.5 = (bf16[1056,128]{1,0:T(8,128)(2,1)S(1)}, bf16[1056,128]{1,0:T(8,128)(2,1)S(1)}, u32[]{:S(2)}, u32[]{:S(2)}) collective-permute-start(bf16[1056,128]{1,0:T(8,128)(2,1)S(1)} %get-tuple-element.22), channel_id=1, source_target_pairs={{0,16},{1,17},{2,18},{3,19},{16,0},{17,1},{18,2},{19,3},{4,20},{5,... | collective-permute-start | bytes 811016 | tf_op jit(solution)/shard_map/ppermute | solution.py:365
  21.0 15.4 %collective-permute-start.4 = (bf16[1056,128]{1,0:T(8,128)(2,1)S(1)}, bf16[1056,128]{1,0:T(8,128)(2,1)S(1)}, u32[]{:S(2)}, u32[]{:S(2)}) collective-permute-start(bf16[1056,128]{1,0:T(8,128)(2,1)S(1)} %get-tuple-element.21), channel_id=1, source_target_pairs={{0,3},{1,0},{2,1},{3,2},{16,19},{17,16},{18,17},{19,18},{4,7},{5,4... | collective-permute-start | bytes 811016 | tf_op jit(solution)/shard_map/ppermute | solution.py:365
  25.2 15.0 %collective-permute-start.6 = (bf16[1056,128]{1,0:T(8,128)(2,1)S(1)}, bf16[1056,128]{1,0:T(8,128)(2,1)S(1)}, u32[]{:S(2)}, u32[]{:S(2)}) collective-permute-start(bf16[1056,128]{1,0:T(8,128)(2,1)S(1)} %get-tuple-element.23), channel_id=1, source_target_pairs={{0,17},{1,18},{2,19},{3,16},{16,1},{17,2},{18,3},{19,0},{4,21},{5,... | collective-permute-start | bytes 811016 | tf_op jit(solution)/shard_map/ppermute | solution.py:365
  28.8 11.4 %collective-permute-start.8 = (bf16[1056,128]{1,0:T(8,128)(2,1)S(1)}, bf16[1056,128]{1,0:T(8,128)(2,1)S(1)}, u32[]{:S(2)}, u32[]{:S(2)}) collective-permute-start(bf16[1056,128]{1,0:T(8,128)(2,1)S(1)} %get-tuple-element.25), channel_id=1, source_target_pairs={{0,19},{1,16},{2,17},{3,18},{16,3},{17,0},{18,1},{19,2},{4,23},{5,... | collective-permute-start | bytes 811016 | tf_op jit(solution)/shard_map/ppermute | solution.py:365
  33.4 12.2 %collective-permute-start.10 = (s16[1056,128]{1,0:T(8,128)(2,1)S(1)}, s16[1056,128]{1,0:T(8,128)(2,1)S(1)}, u32[]{:S(2)}, u32[]{:S(2)}) collective-permute-start(s16[1056,128]{1,0:T(8,128)(2,1)S(1)} %spill_1.1), channel_id=1, source_target_pairs={{1,5},{3,7},{5,9},{7,11},{9,13},{11,15},{4,0},{6,2},{8,4},{10,6},{... | collective-permute-start | bytes 811016 | tf_op jit(solution)/shard_map/ppermute | solution.py:384
  41.0 10.4 %collective-permute-start.9 = (s16[1056,128]{1,0:T(8,128)(2,1)S(1)}, s16[1056,128]{1,0:T(8,128)(2,1)S(1)}, u32[]{:S(2)}, u32[]{:S(2)}) collective-permute-start(s16[1056,128]{1,0:T(8,128)(2,1)S(1)} %spill_0.1), channel_id=1, source_target_pairs={{0,4},{2,6},{4,8},{6,10},{8,12},{10,14},{5,1},{7,3},{9,5},{11,7},{... | collective-permute-start | bytes 811016 | tf_op jit(solution)/shard_map/ppermute | solution.py:384
  52.1 9.3 %collective-permute-start.12 = (s16[528,128]{1,0:T(8,128)(2,1)S(1)}, s16[528,128]{1,0:T(8,128)(2,1)S(1)}, u32[]{:S(2)}, u32[]{:S(2)}) collective-permute-start(s16[528,128]{1,0:T(8,128)(2,1)S(1)} %get-tuple-element.28), channel_id=1, source_target_pairs={{32,64},{64,32},{96,128},{128,96},{160,192},{192,160},{224,0},{0,2... | collective-permute-start | bytes 405512 | tf_op jit(solution)/shard_map/ppermute | solution.py:394
  58.1 8.2 %collective-permute-start.15 = (s16[528,128]{1,0:T(8,128)(2,1)S(1)}, s16[528,128]{1,0:T(8,128)(2,1)S(1)}, u32[]{:S(2)}, u32[]{:S(2)}) collective-permute-start(s16[528,128]{1,0:T(8,128)(2,1)S(1)} %get-tuple-element.29), channel_id=1, source_target_pairs={{0,32},{32,0},{64,96},{96,64},{128,160},{160,128},{192,224},{224,1... | collective-permute-start | bytes 405512 | tf_op jit(solution)/shard_map/ppermute | solution.py:394
  58.1 11.7 %collective-permute-start.11 = (s16[528,128]{1,0:T(8,128)(2,1)S(1)}, s16[528,128]{1,0:T(8,128)(2,1)S(1)}, u32[]{:S(2)}, u32[]{:S(2)}) collective-permute-start(s16[528,128]{1,0:T(8,128)(2,1)S(1)} %get-tuple-element.27), channel_id=1, source_target_pairs={{0,128},{32,160},{64,192},{96,224},{128,0},{160,32},{192,64},{224,... | collective-permute-start | bytes 405512 | tf_op jit(solution)/shard_map/ppermute | solution.py:391
  61.7 9.6 %collective-permute-start.13 = (s16[528,128]{1,0:T(8,128)(2,1)S(1)}, s16[528,128]{1,0:T(8,128)(2,1)S(1)}, u32[]{:S(2)}, u32[]{:S(2)}) collective-permute-start(s16[528,128]{1,0:T(8,128)(2,1)S(1)} %one_2.1), channel_id=1, source_target_pairs={{0,32},{32,0},{64,96},{96,64},{128,160},{160,128},{192,224},{224,1... | collective-permute-start | bytes 405512 | tf_op jit(solution)/shard_map/ppermute | solution.py:394
  66.5 6.5 %collective-permute-start.16 = (s16[528,128]{1,0:T(8,128)(2,1)S(1)}, s16[528,128]{1,0:T(8,128)(2,1)S(1)}, u32[]{:S(2)}, u32[]{:S(2)}) collective-permute-start(s16[528,128]{1,0:T(8,128)(2,1)S(1)} %two_2.1), channel_id=1, source_target_pairs={{32,64},{64,32},{96,128},{128,96},{160,192},{192,160},{224,0},{0,2... | collective-permute-start | bytes 405512 | tf_op jit(solution)/shard_map/ppermute | solution.py:394
  71.5 6.3 %collective-permute-start.14 = (s16[528,128]{1,0:T(8,128)(2,1)S(1)}, s16[528,128]{1,0:T(8,128)(2,1)S(1)}, u32[]{:S(2)}, u32[]{:S(2)}) collective-permute-start(s16[528,128]{1,0:T(8,128)(2,1)S(1)} %two_1.1), channel_id=1, source_target_pairs={{32,64},{64,32},{96,128},{128,96},{160,192},{192,160},{224,0},{0,2... | collective-permute-start | bytes 405512 | tf_op jit(solution)/shard_map/ppermute | solution.py:394
  73.2 5.1 %collective-permute-start.17 = (s16[528,128]{1,0:T(8,128)(2,1)S(1)}, s16[528,128]{1,0:T(8,128)(2,1)S(1)}, u32[]{:S(2)}, u32[]{:S(2)}) collective-permute-start(s16[528,128]{1,0:T(8,128)(2,1)S(1)} %one_1.1), channel_id=1, source_target_pairs={{0,32},{32,0},{64,96},{96,64},{128,160},{160,128},{192,224},{224,1... | collective-permute-start | bytes 405512 | tf_op jit(solution)/shard_map/ppermute | solution.py:394

commit v8 on v7

--- a/solution.py
+++ b/solution.py
@@ -70,7 +70,7 @@
     return total
 
 
-def columns_kernel(taps_hbm, patch_hbm, cell_hbm, img_hbm, out_ref, info_ref, taps_ref, patch_ref, cell_ref, img_ref, sems):
+def columns_kernel(taps_hbm, patch_hbm, cell_hbm, img_hbm, out_ref, info_ref, cols_out, rows_out, taps_ref, patch_ref, cell_ref, img_ref, sems):
     small = [
         pltpu.make_async_copy(src.at[0], dst, sems.at[n])
         for n, (src, dst) in enumerate(((taps_hbm, taps_ref), (patch_hbm, patch_ref), (cell_hbm, cell_ref)))
@@ -89,6 +89,19 @@
     first = jnp.where(lane >= EDGE, over_cols[TILE:], 0.0).astype(bf16)
     last = jnp.where(lane < EDGE, over_cols[:TILE], 0.0).astype(bf16)
     over_cols = over_cols.astype(bf16)
+    cols_out[...] = over_cols
+    patch = lax.axis_index("y") * 4 + lax.axis_index("x")
+    taps = taps_ref[...].astype(f32)
+    shape = (FRAME, WINDOW)
+    row = lax.broadcasted_iota(i32, shape, 0)
+    base = jnp.zeros(shape, f32)
+    step = lax.broadcasted_iota(i32, shape, 1) - row - 7
+    for k in range(KTAPS):
+        base = jnp.where(step == k, taps[0:1, k : k + 1], base)
+    low = jnp.where(patch == 0, 3, 0)
+    high = jnp.where(patch == 15, 130, 133)
+    rows_out[0] = jnp.where((row >= low) & (row <= 133), base, 0.0).astype(bf16)
+    rows_out[1] = jnp.where(row <= high, base, 0.0).astype(bf16)
     owner = patch_ref[...]
     cell = cell_ref[...]
     row0 = 2 * (lax.axis_index("y") * 4 + lax.axis_index("x"))
@@ -109,10 +122,9 @@
         out_ref[:, b * TILE : (b + 1) * TILE] = jnp.dot(window, weights, preferred_element_type=f32).astype(bf16)
 
 
-def rows_kernel(taps_ref, inner_ref, outer_ref, passed_ref, out_ref, window_ref, edge_ref):
+def rows_kernel(cols_ref, rows_ref, inner_ref, outer_ref, passed_ref, out_ref, window_ref, edge_ref):
     patch = lax.axis_index("y") * 4 + lax.axis_index("x")
-    taps = taps_ref[0].astype(f32)
-    over_cols = banded(taps[1:2], (2 * TILE, TILE), 0).astype(bf16)
+    over_cols = cols_ref[...]
     halo = 2 * HALO
     for odd, top_ref, bot_ref in ((0, outer_ref, inner_ref), (1, inner_ref, outer_ref)):
 
@@ -142,24 +154,12 @@
             if b == BLOCKS - 1:
                 rows = jnp.where(lane < EDGE, rows, 0.0)
             edge_ref[:, b * TILE : (b + 1) * TILE] = rows.astype(bf16)
-    shape = (FRAME, WINDOW)
-    row = lax.broadcasted_iota(i32, shape, 0)
-    base = jnp.zeros(shape, f32)
-    step = lax.broadcasted_iota(i32, shape, 1) - row - 7
-    for k in range(KTAPS):
-        base = jnp.where(step == k, taps[0:1, k : k + 1], base)
-    low = jnp.where(patch == 0, 3, 0)
-    high = jnp.where(patch == 15, 130, 133)
-    over_rows = (
-        jnp.where((row >= low) & (row <= 133), base, 0.0).astype(bf16),
-        jnp.where(row <= high, base, 0.0).astype(bf16),
-    )
     for n in range(BLOCKS // 3):
         at = slice(n * 3 * TILE, (n + 1) * 3 * TILE)
         upper = jnp.concatenate([edge_ref[:HALO, at], passed_ref[:FRAME, at]], axis=0)
         lower = jnp.concatenate([passed_ref[BAND - FRAME :, at], edge_ref[HALO:, at]], axis=0)
         for r, window in enumerate((upper, lower)):
-            out_ref[r, :, at] = jnp.dot(over_rows[r], window, preferred_element_type=f32).astype(bf16)
+            out_ref[r, :, at] = jnp.dot(rows_ref[r], window, preferred_element_type=f32).astype(bf16)
 
 
 def warp_kernel(sends, info_ref, patch_ref, class_ref, weight_ref, rows_ref, cols_ref, in_ref, *refs):
@@ -277,11 +277,11 @@
 
 def merge_kernel(in_ref, *refs):
     spills, main_ref, outs = refs[:2], refs[2], refs[3:]
-    main_ref[...] = in_ref[...]
+    main_ref[2:6] = in_ref[2:6]
     for n, ref in enumerate(spills):
         first = jnp.where((lax.axis_index("x") & 1) == n, 0, 6)
         for r in range(2):
-            cells, weights = added(held(main_ref, first + r), decode(ref, r * CELLROW))
+            cells, weights = added(held(in_ref, first + r), decode(ref, r * CELLROW))
             for w in range(4):
                 main_ref[first + r, w * TILE : (w + 1) * TILE, :] = cells[w]
             main_ref[first + r, 4 * TILE : 4 * TILE + 4, :] = weights
@@ -326,12 +326,17 @@
     outer = lax.ppermute(outer, ("y", "x"), [p for i in range(1, 14, 2) for p in ((i, i + 1), (i + 1, i))])
     inner = lax.ppermute(inner, ("y", "x"), [p for i in range(0, 15, 2) for p in ((i, i + 1), (i + 1, i))])
     rows, cols = (jnp.asarray(t) for t in lanczos_tables())
-    passed, info = call(
+    passed, info, over_cols, over_rows = call(
         columns_kernel,
         "columns",
-        (shape((BAND, BLOCKS * TILE), bf16), shape((2,), i32)),
+        (
+            shape((BAND, BLOCKS * TILE), bf16),
+            shape((2,), i32),
+            shape((2 * TILE, TILE), bf16),
+            shape((2, FRAME, WINDOW), bf16),
+        ),
         [HBM] * 4,
-        (VMEM, SMEM),
+        (VMEM, SMEM, VMEM, VMEM),
         [
             pltpu.VMEM((2, KTAPS), bf16),
             pltpu.VMEM((2, COLS // TILE), i32),
@@ -344,10 +349,10 @@
         rows_kernel,
         "rows",
         shape((2, FRAME, BLOCKS * TILE), bf16),
-        [VMEM] * 4,
+        [VMEM] * 5,
         VMEM,
         [pltpu.VMEM((BLOCKS * 2 * HALO, 2 * TILE), bf16), pltpu.VMEM((2 * HALO, BLOCKS * TILE), bf16)],
-    )(psf_taps, inner, outer, passed)
+    )(over_cols, over_rows, inner, outer, passed)
     piece = shape((PIECE, TILE), bf16)
     own = [None] * 4
     sib = [None] * 4

time: 79.4 us -> 79 us (level)
  no operation moved by 1% of the time
where the time goes in v8:
time: 79 us; the launch traced here: 78.8 us
  starting transfers between devices  33.7 us (43%)
  waiting for transfers between devices  29.7 us (38%)
  Pallas kernels  12.8 us (16%)
  between operations  1.46 us (2%)
  local copies, waits for them, and re-layouts  1.01 us (1%)
    ppermute x7, starting transfers between devices, local(): lax.ppermute(out, ('core', 'x'), [(c * 4 + i, (c ^ swap) * 4 + (i + hop)...  10.8 us
    ppermute x7, waiting for transfers between devices, local(): lax.ppermute(out, ('core', 'x'), [(c * 4 + i, (c ^ swap) * 4 + (i + hop)...  9.82 us
    ppermute x3, starting transfers between devices, local(): lax.ppermute(two, 'z', pairs[1])  7.52 us
    ppermute x3, waiting for transfers between devices, local(): lax.ppermute(one, 'z', pairs[0])  6.46 us
    ppermute x2, starting transfers between devices, local(): spills.append(lax.ppermute(out, ('y', 'x'), lower + upper))  5.84 us
    ppermute x2, waiting for transfers between devices, local(): spills.append(lax.ppermute(out, ('y', 'x'), lower + upper))  5.79 us
    ppermute x1, starting transfers between devices, local(): lax.ppermute(outer, ('y', 'x'), [p for i in range(1, 14, 2) for p in ((i,...  4.55 us
    pallas_call x2, Pallas kernels, local(): call(lambda *refs, sends=sends: warp_kernel(sends, *refs), f'warp_{len(se...  3.89 us
  transfers between devices with their start and end apart: 18, of which 12 were waited for; matrix products, arithmetic and copies ran while one was open for 0% of the time, Pallas kernels for 11%

profile of v8, /device:TPU:8, one launch (start us, length us, event | category | flops | bytes accessed | tf_op | source)
XLA Modules:
  0.0 78.8 jit_solution(820513487363570906)
XLA Ops:
  1.6 4.6 %collective-permute-start.1 = (bf16[16,4096]{1,0:T(8,128)(2,1)S(1)}, bf16[16,4096]{1,0:T(8,128)(2,1)S(1)}, u32[]{:S(2)}, u32[]{:S(2)}) collective-permute-start(bf16[16,4096]{1,0:T(8,128)(2,1)S(1)} %get-tuple-element.34), channel_id=1, source_target_pairs={{1,2},{2,1},{3,4},{4,3},{5,6},{6,5},{7,8},{8,7},{9,10},{10,9},{11,... | collective-permute-start | bytes 393224 | tf_op jit(solution)/shard_map/ppermute | solution.py:326
  6.6 3.0 %columns.1 = (bf16[256,4224]{1,0:T(8,128)(2,1)S(1)}, s32[2]{0:T(128)S(1)}, bf16[256,128]{1,0:T(8,128)(2,1)S(1)}, bf16[2,144,160]{2,1,0:T(8,128)(2,1)S(1)}) custom-call(bf16[1,2,13]{2,1,0:T(2,128)(2,1)} %taps_hbm.1, s32[1,2,32]{2,1,0:T(2,128)} %refs_1_.3, s32[1,2,32]{2,1,0:T(2,128)} %cell_hbm.1, bf16[1,256,4096]{2,1,0:T(8,128)(2,1)} %img_hbm.1), custom_call_target="tpu_custom_call" | custom-call | flops 1 | bytes 1 | tf_op jit(solution)/shard_map/columns/pallas_call | solution.py:329
  11.3 1.3 %rows.1.refs_6_ = bf16[2,144,4224]{2,1,0:T(8,128)(2,1)S(1)} custom-call(bf16[256,128]{1,0:T(8,128)(2,1)S(1)} %get-tuple-element.19.cols_ref, bf16[2,144,160]{2,1,0:T(8,128)(2,1)S(1)} %get-tuple-element.20.rows_ref, bf16[16,4096]{1,0:T(8,128)(2,1)S(1)} %collective-permute-done.inner_ref, bf16[16,4096]{1,0:T(8,128)(2,1)S(1)} %collective-permute-done.1.outer_ref, ...), custom_call_target="tpu_custom_call" | custom-call | flops 1 | bytes 1 | tf_op jit(solution)/shard_map/rows/pallas_call | solution.py:348
  12.6 1.4 %warp_2.1 = (bf16[1056,128]{1,0:T(8,128)(2,1)S(1)}, bf16[1056,128]{1,0:T(8,128)(2,1)S(1)}) custom-call(s32[2]{0:T(128)S(1)} %get-tuple-element.18.refs_0_, s32[1,2,32]{2,1,0:T(2,128)S(1)} %copy-done.2, s32[1,2,2,32]{3,2,1,0:T(2,128)S(1)} %copy-done.3, f32[1]{0:T(128)S(6)} %copy.10.refs_3_, bf16[9,128,144]{2,1,0:T(8,128)(2,1)S(1)} %copy-done, ...), custom_call_target="tpu_custom_call" | custom-call | flops 1 | bytes 1 | tf_op jit(solution)/shard_map/warp_2/pallas_call | solution.py:360
  14.0 1.9 %collective-permute-start.3 = (bf16[1056,128]{1,0:T(8,128)(2,1)S(1)}, bf16[1056,128]{1,0:T(8,128)(2,1)S(1)}, u32[]{:S(2)}, u32[]{:S(2)}) collective-permute-start(bf16[1056,128]{1,0:T(8,128)(2,1)S(1)} %get-tuple-element.24), channel_id=1, source_target_pairs={{0,2},{1,3},{2,0},{3,1},{16,18},{17,19},{18,16},{19,17},{4,6},{5,7... | collective-permute-start | bytes 811016 | tf_op jit(solution)/shard_map/ppermute | solution.py:370
  15.9 2.5 %warp_6.1 = (bf16[1056,128]{1,0:T(8,128)(2,1)S(1)}, bf16[1056,128]{1,0:T(8,128)(2,1)S(1)}, bf16[1056,128]{1,0:T(8,128)(2,1)S(1)}, bf16[1056,128]{1,0:T(8,128)(2,...) custom-call(s32[2]{0:T(128)S(1)} %get-tuple-element.18.refs_0_, s32[1,2,32]{2,1,0:T(2,128)S(1)} %copy-done.2, ...), custom_call_target="tpu_custom_call" | custom-call | flops 1 | bytes 1 | tf_op jit(solution)/shard_map/warp_6/pallas_call | solution.py:360
  18.4 1.5 %collective-permute-start.2 = (bf16[1056,128]{1,0:T(8,128)(2,1)S(1)}, bf16[1056,128]{1,0:T(8,128)(2,1)S(1)}, u32[]{:S(2)}, u32[]{:S(2)}) collective-permute-start(bf16[1056,128]{1,0:T(8,128)(2,1)S(1)} %get-tuple-element.23), channel_id=1, source_target_pairs={{0,1},{1,2},{2,3},{3,0},{16,17},{17,18},{18,19},{19,16},{4,5},{5,6... | collective-permute-start | bytes 811016 | tf_op jit(solution)/shard_map/ppermute | solution.py:370
  20.8 2.5 %collective-permute-start.4 = (bf16[1056,128]{1,0:T(8,128)(2,1)S(1)}, bf16[1056,128]{1,0:T(8,128)(2,1)S(1)}, u32[]{:S(2)}, u32[]{:S(2)}) collective-permute-start(bf16[1056,128]{1,0:T(8,128)(2,1)S(1)} %get-tuple-element.25), channel_id=1, source_target_pairs={{0,3},{1,0},{2,1},{3,2},{16,19},{17,16},{18,17},{19,18},{4,7},{5,4... | collective-permute-start | bytes 811016 | tf_op jit(solution)/shard_map/ppermute | solution.py:370
  23.3 1.7 %collective-permute-done.3.refs_2_ = bf16[1056,128]{1,0:T(8,128)(2,1)S(1)} collective-permute-done((bf16[1056,128]{1,0:T(8,128)(2,1)S(1)}, bf16[1056,128]{1,0:T(8,128)(2,1)S(1)}, u32[]{:S(2)}, u32[]{:S(2)}) %collective-permute-start.3) | collective-permute-done | bytes 270368 | tf_op jit(solution)/shard_map/ppermute | solution.py:370
  25.0 3.6 %collective-permute-done.7.refs_6_.refs_3_ = bf16[1056,128]{1,0:T(8,128)(2,1)S(1)} collective-permute-done((bf16[1056,128]{1,0:T(8,128)(2,1)S(1)}, bf16[1056,128]{1,0:T(8,128)(2,1)S(1)}, u32[]{:S(2)}, u32[]{:S(2)}) %collective-permute-start.7) | collective-permute-done | bytes 270368 | tf_op jit(solution)/shard_map/ppermute | solution.py:370
  28.7 4.0 %collective-permute-start.8 = (bf16[1056,128]{1,0:T(8,128)(2,1)S(1)}, bf16[1056,128]{1,0:T(8,128)(2,1)S(1)}, u32[]{:S(2)}, u32[]{:S(2)}) collective-permute-start(bf16[1056,128]{1,0:T(8,128)(2,1)S(1)} %get-tuple-element.29), channel_id=1, source_target_pairs={{0,19},{1,16},{2,17},{3,18},{16,3},{17,0},{18,1},{19,2},{4,23},{5,... | collective-permute-start | bytes 811016 | tf_op jit(solution)/shard_map/ppermute | solution.py:370
  33.2 2.4 %collective-permute-start.10 = (s16[1056,128]{1,0:T(8,128)(2,1)S(1)}, s16[1056,128]{1,0:T(8,128)(2,1)S(1)}, u32[]{:S(2)}, u32[]{:S(2)}) collective-permute-start(s16[1056,128]{1,0:T(8,128)(2,1)S(1)} %spill_1.1), channel_id=1, source_target_pairs={{1,5},{3,7},{5,9},{7,11},{9,13},{11,15},{4,0},{6,2},{8,4},{10,6},{... | collective-permute-start | bytes 811016 | tf_op jit(solution)/shard_map/ppermute | solution.py:389
  36.2 3.8 %collective-permute-done.6.refs_5_.refs_1_ = bf16[1056,128]{1,0:T(8,128)(2,1)S(1)} collective-permute-done((bf16[1056,128]{1,0:T(8,128)(2,1)S(1)}, bf16[1056,128]{1,0:T(8,128)(2,1)S(1)}, u32[]{:S(2)}, u32[]{:S(2)}) %collective-permute-start.6) | collective-permute-done | bytes 270368 | tf_op jit(solution)/shard_map/ppermute | solution.py:370
  40.8 3.5 %collective-permute-start.9 = (s16[1056,128]{1,0:T(8,128)(2,1)S(1)}, s16[1056,128]{1,0:T(8,128)(2,1)S(1)}, u32[]{:S(2)}, u32[]{:S(2)}) collective-permute-start(s16[1056,128]{1,0:T(8,128)(2,1)S(1)} %spill_0.1), channel_id=1, source_target_pairs={{0,4},{2,6},{4,8},{6,10},{8,12},{10,14},{5,1},{7,3},{9,5},{11,7},{... | collective-permute-start | bytes 811016 | tf_op jit(solution)/shard_map/ppermute | solution.py:389
  44.3 1.1 %place.1.in_ref = f32[8,528,128]{2,1,0:T(8,128)S(1)} custom-call(bf16[1056,128]{1,0:T(8,128)(2,1)S(1)} %get-tuple-element.22.refs_0_, bf16[1056,128]{1,0:T(8,128)(2,1)S(1)} %collective-permute-done.2.refs_1_.refs_0_, bf16[1056,128]{1,0:T(8,128)(2,1)S(1)} %collective-permute-done.3.refs_2_, bf16[1056,128]{1,0:T(8,128)(2,1)S(1)} %collective-permute-done.4.refs_3_.refs_2_, ...), custom_call_target="tpu_custom_call" | custom-call | flops 1 | bytes 1 | tf_op jit(solution)/shard_map/place/pallas_call | solution.py:390
  45.4 5.8 %collective-permute-done.9.refs_0_ = s16[1056,128]{1,0:T(8,128)(2,1)S(1)} collective-permute-done((s16[1056,128]{1,0:T(8,128)(2,1)S(1)}, s16[1056,128]{1,0:T(8,128)(2,1)S(1)}, u32[]{:S(2)}, u32[]{:S(2)}) %collective-permute-start.9) | collective-permute-done | bytes 270368 | tf_op jit(solution)/shard_map/ppermute | solution.py:389
  51.8 6.0 %collective-permute-start.12 = (s16[528,128]{1,0:T(8,128)(2,1)S(1)}, s16[528,128]{1,0:T(8,128)(2,1)S(1)}, u32[]{:S(2)}, u32[]{:S(2)}) collective-permute-start(s16[528,128]{1,0:T(8,128)(2,1)S(1)} %get-tuple-element.32), channel_id=1, source_target_pairs={{32,64},{64,32},{96,128},{128,96},{160,192},{192,160},{224,0},{0,2... | collective-permute-start | bytes 405512 | tf_op jit(solution)/shard_map/ppermute | solution.py:399
  57.7 3.4 %collective-permute-start.11 = (s16[528,128]{1,0:T(8,128)(2,1)S(1)}, s16[528,128]{1,0:T(8,128)(2,1)S(1)}, u32[]{:S(2)}, u32[]{:S(2)}) collective-permute-start(s16[528,128]{1,0:T(8,128)(2,1)S(1)} %get-tuple-element.31), channel_id=1, source_target_pairs={{0,128},{32,160},{64,192},{96,224},{128,0},{160,32},{192,64},{224,... | collective-permute-start | bytes 405512 | tf_op jit(solution)/shard_map/ppermute | solution.py:396
  61.5 4.4 %collective-permute-done.15.refs_1_ = s16[528,128]{1,0:T(8,128)(2,1)S(1)} collective-permute-done((s16[528,128]{1,0:T(8,128)(2,1)S(1)}, s16[528,128]{1,0:T(8,128)(2,1)S(1)}, u32[]{:S(2)}, u32[]{:S(2)}) %collective-permute-start.15) | collective-permute-done | bytes 135200 | tf_op jit(solution)/shard_map/ppermute | solution.py:399
  66.2 3.1 %collective-permute-done.11.far_ref = s16[528,128]{1,0:T(8,128)(2,1)S(1)} collective-permute-done((s16[528,128]{1,0:T(8,128)(2,1)S(1)}, s16[528,128]{1,0:T(8,128)(2,1)S(1)}, u32[]{:S(2)}, u32[]{:S(2)}) %collective-permute-start.11) | collective-permute-done | bytes 135200 | tf_op jit(solution)/shard_map/ppermute | solution.py:396
  69.4 1.5 %collective-permute-done.13.refs_1_ = s16[528,128]{1,0:T(8,128)(2,1)S(1)} collective-permute-done((s16[528,128]{1,0:T(8,128)(2,1)S(1)}, s16[528,128]{1,0:T(8,128)(2,1)S(1)}, u32[]{:S(2)}, u32[]{:S(2)}) %collective-permute-start.13) | collective-permute-done | bytes 135200 | tf_op jit(solution)/shard_map/ppermute | solution.py:399
  71.2 1.5 %collective-permute-start.14 = (s16[528,128]{1,0:T(8,128)(2,1)S(1)}, s16[528,128]{1,0:T(8,128)(2,1)S(1)}, u32[]{:S(2)}, u32[]{:S(2)}) collective-permute-start(s16[528,128]{1,0:T(8,128)(2,1)S(1)} %two_1.1), channel_id=1, source_target_pairs={{32,64},{64,32},{96,128},{128,96},{160,192},{192,160},{224,0},{0,2... | collective-permute-start | bytes 405512 | tf_op jit(solution)/shard_map/ppermute | solution.py:399
  72.9 1.1 %collective-permute-start.17 = (s16[528,128]{1,0:T(8,128)(2,1)S(1)}, s16[528,128]{1,0:T(8,128)(2,1)S(1)}, u32[]{:S(2)}, u32[]{:S(2)}) collective-permute-start(s16[528,128]{1,0:T(8,128)(2,1)S(1)} %one_1.1), channel_id=1, source_target_pairs={{0,32},{32,0},{64,96},{96,64},{128,160},{160,128},{192,224},{224,1... | collective-permute-start | bytes 405512 | tf_op jit(solution)/shard_map/ppermute | solution.py:399
  73.9 3.5 %collective-permute-done.14.refs_0_ = s16[528,128]{1,0:T(8,128)(2,1)S(1)} collective-permute-done((s16[528,128]{1,0:T(8,128)(2,1)S(1)}, s16[528,128]{1,0:T(8,128)(2,1)S(1)}, u32[]{:S(2)}, u32[]{:S(2)}) %collective-permute-start.14) | collective-permute-done | bytes 135200 | tf_op jit(solution)/shard_map/ppermute | solution.py:399
  (35 shorter events, 8.2 us)
Async XLA Ops:
  1.6 9.2 %collective-permute-start.1 = (bf16[16,4096]{1,0:T(8,128)(2,1)S(1)}, bf16[16,4096]{1,0:T(8,128)(2,1)S(1)}, u32[]{:S(2)}, u32[]{:S(2)}) collective-permute-start(bf16[16,4096]{1,0:T(8,128)(2,1)S(1)} %get-tuple-element.34), channel_id=1, source_target_pairs={{1,2},{2,1},{3,4},{4,3},{5,6},{6,5},{7,8},{8,7},{9,10},{10,9},{11,... | collective-permute-start | bytes 393224 | tf_op jit(solution)/shard_map/ppermute | solution.py:326
  6.2 5.1 %collective-permute-start = (bf16[16,4096]{1,0:T(8,128)(2,1)S(1)}, bf16[16,4096]{1,0:T(8,128)(2,1)S(1)}, u32[]{:S(2)}, u32[]{:S(2)}) collective-permute-start(bf16[16,4096]{1,0:T(8,128)(2,1)S(1)} %get-tuple-element.35), channel_id=1, source_target_pairs={{0,1},{1,0},{2,3},{3,2},{4,5},{5,4},{6,7},{7,6},{8,9},{9,8},{10,11... | collective-permute-start | bytes 393224 | tf_op jit(solution)/shard_map/ppermute | solution.py:327
  11.2 1.3 %copy-start = (bf16[9,128,144]{2,1,0:T(8,128)(2,1)S(1)}, bf16[9,128,144]{2,1,0:T(8,128)(2,1)}, u32[]{:S(2)}) copy-start(bf16[9,128,144]{2,1,0:T(8,128)(2,1)} %constant.20.clone.refs_4_) | copy-start | bytes 995332
  11.2 1.3 %copy-start.1 = (bf16[8,256,128]{2,1,0:T(8,128)(2,1)S(1)}, bf16[8,256,128]{2,1,0:T(8,128)(2,1)}, u32[]{:S(2)}) copy-start(bf16[8,256,128]{2,1,0:T(8,128)(2,1)} %constant.21.clone.refs_5_) | copy-start | bytes 1572868
  11.2 1.3 %copy-start.2 = (s32[1,2,32]{2,1,0:T(2,128)S(1)}, s32[1,2,32]{2,1,0:T(2,128)}, u32[]{:S(2)}) copy-start(s32[1,2,32]{2,1,0:T(2,128)} %refs_1_.3) | copy-start | bytes 772
  11.3 1.4 %copy-start.3 = (s32[1,2,2,32]{3,2,1,0:T(2,128)S(1)}, s32[1,2,2,32]{3,2,1,0:T(2,128)}, u32[]{:S(2)}) copy-start(s32[1,2,2,32]{3,2,1,0:T(2,128)} %refs_2_.3) | copy-start | bytes 1540
  14.0 11.0 %collective-permute-start.3 = (bf16[1056,128]{1,0:T(8,128)(2,1)S(1)}, bf16[1056,128]{1,0:T(8,128)(2,1)S(1)}, u32[]{:S(2)}, u32[]{:S(2)}) collective-permute-start(bf16[1056,128]{1,0:T(8,128)(2,1)S(1)} %get-tuple-element.24), channel_id=1, source_target_pairs={{0,2},{1,3},{2,0},{3,1},{16,18},{17,19},{18,16},{19,17},{4,6},{5,7... | collective-permute-start | bytes 811016 | tf_op jit(solution)/shard_map/ppermute | solution.py:370
  15.9 12.8 %collective-permute-start.7 = (bf16[1056,128]{1,0:T(8,128)(2,1)S(1)}, bf16[1056,128]{1,0:T(8,128)(2,1)S(1)}, u32[]{:S(2)}, u32[]{:S(2)}) collective-permute-start(bf16[1056,128]{1,0:T(8,128)(2,1)S(1)} %get-tuple-element.28), channel_id=1, source_target_pairs={{0,18},{1,19},{2,16},{3,17},{16,2},{17,3},{18,0},{19,1},{4,22},{5,... | collective-permute-start | bytes 811016 | tf_op jit(solution)/shard_map/ppermute | solution.py:370
  18.4 17.2 %collective-permute-start.2 = (bf16[1056,128]{1,0:T(8,128)(2,1)S(1)}, bf16[1056,128]{1,0:T(8,128)(2,1)S(1)}, u32[]{:S(2)}, u32[]{:S(2)}) collective-permute-start(bf16[1056,128]{1,0:T(8,128)(2,1)S(1)} %get-tuple-element.23), channel_id=1, source_target_pairs={{0,1},{1,2},{2,3},{3,0},{16,17},{17,18},{18,19},{19,16},{4,5},{5,6... | collective-permute-start | bytes 811016 | tf_op jit(solution)/shard_map/ppermute | solution.py:370
  19.9 12.7 %collective-permute-start.5 = (bf16[1056,128]{1,0:T(8,128)(2,1)S(1)}, bf16[1056,128]{1,0:T(8,128)(2,1)S(1)}, u32[]{:S(2)}, u32[]{:S(2)}) collective-permute-start(bf16[1056,128]{1,0:T(8,128)(2,1)S(1)} %get-tuple-element.26), channel_id=1, source_target_pairs={{0,16},{1,17},{2,18},{3,19},{16,0},{17,1},{18,2},{19,3},{4,20},{5,... | collective-permute-start | bytes 811016 | tf_op jit(solution)/shard_map/ppermute | solution.py:370
  20.8 15.4 %collective-permute-start.4 = (bf16[1056,128]{1,0:T(8,128)(2,1)S(1)}, bf16[1056,128]{1,0:T(8,128)(2,1)S(1)}, u32[]{:S(2)}, u32[]{:S(2)}) collective-permute-start(bf16[1056,128]{1,0:T(8,128)(2,1)S(1)} %get-tuple-element.25), channel_id=1, source_target_pairs={{0,3},{1,0},{2,1},{3,2},{16,19},{17,16},{18,17},{19,18},{4,7},{5,4... | collective-permute-start | bytes 811016 | tf_op jit(solution)/shard_map/ppermute | solution.py:370
  25.0 15.0 %collective-permute-start.6 = (bf16[1056,128]{1,0:T(8,128)(2,1)S(1)}, bf16[1056,128]{1,0:T(8,128)(2,1)S(1)}, u32[]{:S(2)}, u32[]{:S(2)}) collective-permute-start(bf16[1056,128]{1,0:T(8,128)(2,1)S(1)} %get-tuple-element.27), channel_id=1, source_target_pairs={{0,17},{1,18},{2,19},{3,16},{16,1},{17,2},{18,3},{19,0},{4,21},{5,... | collective-permute-start | bytes 811016 | tf_op jit(solution)/shard_map/ppermute | solution.py:370
  28.7 11.4 %collective-permute-start.8 = (bf16[1056,128]{1,0:T(8,128)(2,1)S(1)}, bf16[1056,128]{1,0:T(8,128)(2,1)S(1)}, u32[]{:S(2)}, u32[]{:S(2)}) collective-permute-start(bf16[1056,128]{1,0:T(8,128)(2,1)S(1)} %get-tuple-element.29), channel_id=1, source_target_pairs={{0,19},{1,16},{2,17},{3,18},{16,3},{17,0},{18,1},{19,2},{4,23},{5,... | collective-permute-start | bytes 811016 | tf_op jit(solution)/shard_map/ppermute | solution.py:370
  33.2 12.2 %collective-permute-start.10 = (s16[1056,128]{1,0:T(8,128)(2,1)S(1)}, s16[1056,128]{1,0:T(8,128)(2,1)S(1)}, u32[]{:S(2)}, u32[]{:S(2)}) collective-permute-start(s16[1056,128]{1,0:T(8,128)(2,1)S(1)} %spill_1.1), channel_id=1, source_target_pairs={{1,5},{3,7},{5,9},{7,11},{9,13},{11,15},{4,0},{6,2},{8,4},{10,6},{... | collective-permute-start | bytes 811016 | tf_op jit(solution)/shard_map/ppermute | solution.py:389
  40.8 10.4 %collective-permute-start.9 = (s16[1056,128]{1,0:T(8,128)(2,1)S(1)}, s16[1056,128]{1,0:T(8,128)(2,1)S(1)}, u32[]{:S(2)}, u32[]{:S(2)}) collective-permute-start(s16[1056,128]{1,0:T(8,128)(2,1)S(1)} %spill_0.1), channel_id=1, source_target_pairs={{0,4},{2,6},{4,8},{6,10},{8,12},{10,14},{5,1},{7,3},{9,5},{11,7},{... | collective-permute-start | bytes 811016 | tf_op jit(solution)/shard_map/ppermute | solution.py:389
  51.8 9.3 %collective-permute-start.12 = (s16[528,128]{1,0:T(8,128)(2,1)S(1)}, s16[528,128]{1,0:T(8,128)(2,1)S(1)}, u32[]{:S(2)}, u32[]{:S(2)}) collective-permute-start(s16[528,128]{1,0:T(8,128)(2,1)S(1)} %get-tuple-element.32), channel_id=1, source_target_pairs={{32,64},{64,32},{96,128},{128,96},{160,192},{192,160},{224,0},{0,2... | collective-permute-start | bytes 405512 | tf_op jit(solution)/shard_map/ppermute | solution.py:399
  57.7 8.2 %collective-permute-start.15 = (s16[528,128]{1,0:T(8,128)(2,1)S(1)}, s16[528,128]{1,0:T(8,128)(2,1)S(1)}, u32[]{:S(2)}, u32[]{:S(2)}) collective-permute-start(s16[528,128]{1,0:T(8,128)(2,1)S(1)} %get-tuple-element.33), channel_id=1, source_target_pairs={{0,32},{32,0},{64,96},{96,64},{128,160},{160,128},{192,224},{224,1... | collective-permute-start | bytes 405512 | tf_op jit(solution)/shard_map/ppermute | solution.py:399
  57.7 11.6 %collective-permute-start.11 = (s16[528,128]{1,0:T(8,128)(2,1)S(1)}, s16[528,128]{1,0:T(8,128)(2,1)S(1)}, u32[]{:S(2)}, u32[]{:S(2)}) collective-permute-start(s16[528,128]{1,0:T(8,128)(2,1)S(1)} %get-tuple-element.31), channel_id=1, source_target_pairs={{0,128},{32,160},{64,192},{96,224},{128,0},{160,32},{192,64},{224,... | collective-permute-start | bytes 405512 | tf_op jit(solution)/shard_map/ppermute | solution.py:396
  61.3 9.6 %collective-permute-start.13 = (s16[528,128]{1,0:T(8,128)(2,1)S(1)}, s16[528,128]{1,0:T(8,128)(2,1)S(1)}, u32[]{:S(2)}, u32[]{:S(2)}) collective-permute-start(s16[528,128]{1,0:T(8,128)(2,1)S(1)} %one_2.1), channel_id=1, source_target_pairs={{0,32},{32,0},{64,96},{96,64},{128,160},{160,128},{192,224},{224,1... | collective-permute-start | bytes 405512 | tf_op jit(solution)/shard_map/ppermute | solution.py:399
  66.1 6.5 %collective-permute-start.16 = (s16[528,128]{1,0:T(8,128)(2,1)S(1)}, s16[528,128]{1,0:T(8,128)(2,1)S(1)}, u32[]{:S(2)}, u32[]{:S(2)}) collective-permute-start(s16[528,128]{1,0:T(8,128)(2,1)S(1)} %two_2.1), channel_id=1, source_target_pairs={{32,64},{64,32},{96,128},{128,96},{160,192},{192,160},{224,0},{0,2... | collective-permute-start | bytes 405512 | tf_op jit(solution)/shard_map/ppermute | solution.py:399
  71.2 6.3 %collective-permute-start.14 = (s16[528,128]{1,0:T(8,128)(2,1)S(1)}, s16[528,128]{1,0:T(8,128)(2,1)S(1)}, u32[]{:S(2)}, u32[]{:S(2)}) collective-permute-start(s16[528,128]{1,0:T(8,128)(2,1)S(1)} %two_1.1), channel_id=1, source_target_pairs={{32,64},{64,32},{96,128},{128,96},{160,192},{192,160},{224,0},{0,2... | collective-permute-start | bytes 405512 | tf_op jit(solution)/shard_map/ppermute | solution.py:399
  72.9 5.1 %collective-permute-start.17 = (s16[528,128]{1,0:T(8,128)(2,1)S(1)}, s16[528,128]{1,0:T(8,128)(2,1)S(1)}, u32[]{:S(2)}, u32[]{:S(2)}) collective-permute-start(s16[528,128]{1,0:T(8,128)(2,1)S(1)} %one_1.1), channel_id=1, source_target_pairs={{0,32},{32,0},{64,96},{96,64},{128,160},{160,128},{192,224},{224,1... | collective-permute-start | bytes 405512 | tf_op jit(solution)/shard_map/ppermute | solution.py:399

commit v9 on v8

--- a/solution.py
+++ b/solution.py
@@ -259,7 +259,7 @@
 
         @pl.when((x == mine[0]) | (x == mine[1]))
         def _(n=n, where=where):
-            for piece in pieces[2 * n : 2 * n + 2]:
+            for piece in pieces[n::2]:
                 spread(piece, rows_ref, where)
 
     for r in range(2):
@@ -383,7 +383,7 @@
             [VMEM] * 4,
             VMEM,
             [pltpu.VMEM((4, CELLROW, TILE), f32)],
-        )(*(piece for hop in sorted(set(hops)) for piece in (own[hop], sib[hop])))
+        )(*(piece for side in (sib, own) for piece in (side[hop] for hop in sorted(set(hops)))))
         lower = [(4 * i + x, 4 * i + 4 + x) for i in range(3) for x in range(4) if x % 2 == n]
         upper = [(4 * i + 4 + x, 4 * i + x) for i in range(3) for x in range(4) if x % 2 != n]
         spills.append(lax.ppermute(out, ("y", "x"), lower + upper))

time: 79 us -> 79 us (level)
  no operation moved by 1% of the time
where the time goes in v9:
time: 79 us; the launch traced here: 78.7 us
  starting transfers between devices  33.7 us (43%)
  waiting for transfers between devices  29.8 us (38%)
  Pallas kernels  12.7 us (16%)
  between operations  1.46 us (2%)
  local copies, waits for them, and re-layouts  1.01 us (1%)
    ppermute x7, starting transfers between devices, local(): lax.ppermute(out, ('core', 'x'), [(c * 4 + i, (c ^ swap) * 4 + (i + hop)...  10.8 us
    ppermute x7, waiting for transfers between devices, local(): lax.ppermute(out, ('core', 'x'), [(c * 4 + i, (c ^ swap) * 4 + (i + hop)...  9.82 us
    ppermute x3, starting transfers between devices, local(): lax.ppermute(two, 'z', pairs[1])  7.52 us
    ppermute x3, waiting for transfers between devices, local(): lax.ppermute(one, 'z', pairs[0])  6.36 us
    ppermute x2, waiting for transfers between devices, local(): spills.append(lax.ppermute(out, ('y', 'x'), lower + upper))  5.89 us
    ppermute x2, starting transfers between devices, local(): spills.append(lax.ppermute(out, ('y', 'x'), lower + upper))  5.84 us
    ppermute x1, starting transfers between devices, local(): lax.ppermute(outer, ('y', 'x'), [p for i in range(1, 14, 2) for p in ((i,...  4.55 us
    pallas_call x2, Pallas kernels, local(): call(lambda *refs, sends=sends: warp_kernel(sends, *refs), f'warp_{len(se...  3.9 us
  transfers between devices with their start and end apart: 18, of which 12 were waited for; matrix products, arithmetic and copies ran while one was open for 0% of the time, Pallas kernels for 11%

profile of v9, /device:TPU:8, one launch (start us, length us, event | category | flops | bytes accessed | tf_op | source)
XLA Modules:
  0.0 78.7 jit_solution(17269682065443135589)
XLA Ops:
  1.6 4.6 %collective-permute-start.1 = (bf16[16,4096]{1,0:T(8,128)(2,1)S(1)}, bf16[16,4096]{1,0:T(8,128)(2,1)S(1)}, u32[]{:S(2)}, u32[]{:S(2)}) collective-permute-start(bf16[16,4096]{1,0:T(8,128)(2,1)S(1)} %get-tuple-element.34), channel_id=1, source_target_pairs={{1,2},{2,1},{3,4},{4,3},{5,6},{6,5},{7,8},{8,7},{9,10},{10,9},{11,... | collective-permute-start | bytes 393224 | tf_op jit(solution)/shard_map/ppermute | solution.py:326
  6.6 3.0 %columns.1 = (bf16[256,4224]{1,0:T(8,128)(2,1)S(1)}, s32[2]{0:T(128)S(1)}, bf16[256,128]{1,0:T(8,128)(2,1)S(1)}, bf16[2,144,160]{2,1,0:T(8,128)(2,1)S(1)}) custom-call(bf16[1,2,13]{2,1,0:T(2,128)(2,1)} %taps_hbm.1, s32[1,2,32]{2,1,0:T(2,128)} %refs_1_.3, s32[1,2,32]{2,1,0:T(2,128)} %cell_hbm.1, bf16[1,256,4096]{2,1,0:T(8,128)(2,1)} %img_hbm.1), custom_call_target="tpu_custom_call" | custom-call | flops 1 | bytes 1 | tf_op jit(solution)/shard_map/columns/pallas_call | solution.py:329
  11.3 1.3 %rows.1.refs_6_ = bf16[2,144,4224]{2,1,0:T(8,128)(2,1)S(1)} custom-call(bf16[256,128]{1,0:T(8,128)(2,1)S(1)} %get-tuple-element.19.cols_ref, bf16[2,144,160]{2,1,0:T(8,128)(2,1)S(1)} %get-tuple-element.20.rows_ref, bf16[16,4096]{1,0:T(8,128)(2,1)S(1)} %collective-permute-done.inner_ref, bf16[16,4096]{1,0:T(8,128)(2,1)S(1)} %collective-permute-done.1.outer_ref, ...), custom_call_target="tpu_custom_call" | custom-call | flops 1 | bytes 1 | tf_op jit(solution)/shard_map/rows/pallas_call | solution.py:348
  12.6 1.4 %warp_2.1 = (bf16[1056,128]{1,0:T(8,128)(2,1)S(1)}, bf16[1056,128]{1,0:T(8,128)(2,1)S(1)}) custom-call(s32[2]{0:T(128)S(1)} %get-tuple-element.18.refs_0_, s32[1,2,32]{2,1,0:T(2,128)S(1)} %copy-done.2, s32[1,2,2,32]{3,2,1,0:T(2,128)S(1)} %copy-done.3, f32[1]{0:T(128)S(6)} %copy.10.refs_3_, bf16[9,128,144]{2,1,0:T(8,128)(2,1)S(1)} %copy-done, ...), custom_call_target="tpu_custom_call" | custom-call | flops 1 | bytes 1 | tf_op jit(solution)/shard_map/warp_2/pallas_call | solution.py:360
  14.0 1.9 %collective-permute-start.3 = (bf16[1056,128]{1,0:T(8,128)(2,1)S(1)}, bf16[1056,128]{1,0:T(8,128)(2,1)S(1)}, u32[]{:S(2)}, u32[]{:S(2)}) collective-permute-start(bf16[1056,128]{1,0:T(8,128)(2,1)S(1)} %get-tuple-element.24), channel_id=1, source_target_pairs={{0,2},{1,3},{2,0},{3,1},{16,18},{17,19},{18,16},{19,17},{4,6},{5,7... | collective-permute-start | bytes 811016 | tf_op jit(solution)/shard_map/ppermute | solution.py:370
  15.9 2.5 %warp_6.1 = (bf16[1056,128]{1,0:T(8,128)(2,1)S(1)}, bf16[1056,128]{1,0:T(8,128)(2,1)S(1)}, bf16[1056,128]{1,0:T(8,128)(2,1)S(1)}, bf16[1056,128]{1,0:T(8,128)(2,...) custom-call(s32[2]{0:T(128)S(1)} %get-tuple-element.18.refs_0_, s32[1,2,32]{2,1,0:T(2,128)S(1)} %copy-done.2, ...), custom_call_target="tpu_custom_call" | custom-call | flops 1 | bytes 1 | tf_op jit(solution)/shard_map/warp_6/pallas_call | solution.py:360
  18.4 1.5 %collective-permute-start.2 = (bf16[1056,128]{1,0:T(8,128)(2,1)S(1)}, bf16[1056,128]{1,0:T(8,128)(2,1)S(1)}, u32[]{:S(2)}, u32[]{:S(2)}) collective-permute-start(bf16[1056,128]{1,0:T(8,128)(2,1)S(1)} %get-tuple-element.23), channel_id=1, source_target_pairs={{0,1},{1,2},{2,3},{3,0},{16,17},{17,18},{18,19},{19,16},{4,5},{5,6... | collective-permute-start | bytes 811016 | tf_op jit(solution)/shard_map/ppermute | solution.py:370
  20.8 2.5 %collective-permute-start.4 = (bf16[1056,128]{1,0:T(8,128)(2,1)S(1)}, bf16[1056,128]{1,0:T(8,128)(2,1)S(1)}, u32[]{:S(2)}, u32[]{:S(2)}) collective-permute-start(bf16[1056,128]{1,0:T(8,128)(2,1)S(1)} %get-tuple-element.25), channel_id=1, source_target_pairs={{0,3},{1,0},{2,1},{3,2},{16,19},{17,16},{18,17},{19,18},{4,7},{5,4... | collective-permute-start | bytes 811016 | tf_op jit(solution)/shard_map/ppermute | solution.py:370
  23.3 1.7 %collective-permute-done.3.refs_2_.refs_3_ = bf16[1056,128]{1,0:T(8,128)(2,1)S(1)} collective-permute-done((bf16[1056,128]{1,0:T(8,128)(2,1)S(1)}, bf16[1056,128]{1,0:T(8,128)(2,1)S(1)}, u32[]{:S(2)}, u32[]{:S(2)}) %collective-permute-start.3) | collective-permute-done | bytes 270368 | tf_op jit(solution)/shard_map/ppermute | solution.py:370
  25.0 3.7 %collective-permute-done.7.refs_6_.refs_1_ = bf16[1056,128]{1,0:T(8,128)(2,1)S(1)} collective-permute-done((bf16[1056,128]{1,0:T(8,128)(2,1)S(1)}, bf16[1056,128]{1,0:T(8,128)(2,1)S(1)}, u32[]{:S(2)}, u32[]{:S(2)}) %collective-permute-start.7) | collective-permute-done | bytes 270368 | tf_op jit(solution)/shard_map/ppermute | solution.py:370
  28.7 4.0 %collective-permute-start.8 = (bf16[1056,128]{1,0:T(8,128)(2,1)S(1)}, bf16[1056,128]{1,0:T(8,128)(2,1)S(1)}, u32[]{:S(2)}, u32[]{:S(2)}) collective-permute-start(bf16[1056,128]{1,0:T(8,128)(2,1)S(1)} %get-tuple-element.29), channel_id=1, source_target_pairs={{0,19},{1,16},{2,17},{3,18},{16,3},{17,0},{18,1},{19,2},{4,23},{5,... | collective-permute-start | bytes 811016 | tf_op jit(solution)/shard_map/ppermute | solution.py:370
  33.2 2.4 %collective-permute-start.10 = (s16[1056,128]{1,0:T(8,128)(2,1)S(1)}, s16[1056,128]{1,0:T(8,128)(2,1)S(1)}, u32[]{:S(2)}, u32[]{:S(2)}) collective-permute-start(s16[1056,128]{1,0:T(8,128)(2,1)S(1)} %spill_1.1), channel_id=1, source_target_pairs={{1,5},{3,7},{5,9},{7,11},{9,13},{11,15},{4,0},{6,2},{8,4},{10,6},{... | collective-permute-start | bytes 811016 | tf_op jit(solution)/shard_map/ppermute | solution.py:389
  36.2 3.8 %collective-permute-done.6.refs_5_.refs_0_ = bf16[1056,128]{1,0:T(8,128)(2,1)S(1)} collective-permute-done((bf16[1056,128]{1,0:T(8,128)(2,1)S(1)}, bf16[1056,128]{1,0:T(8,128)(2,1)S(1)}, u32[]{:S(2)}, u32[]{:S(2)}) %collective-permute-start.6) | collective-permute-done | bytes 270368 | tf_op jit(solution)/shard_map/ppermute | solution.py:370
  40.8 3.5 %collective-permute-start.9 = (s16[1056,128]{1,0:T(8,128)(2,1)S(1)}, s16[1056,128]{1,0:T(8,128)(2,1)S(1)}, u32[]{:S(2)}, u32[]{:S(2)}) collective-permute-start(s16[1056,128]{1,0:T(8,128)(2,1)S(1)} %spill_0.1), channel_id=1, source_target_pairs={{0,4},{2,6},{4,8},{6,10},{8,12},{10,14},{5,1},{7,3},{9,5},{11,7},{... | collective-permute-start | bytes 811016 | tf_op jit(solution)/shard_map/ppermute | solution.py:389
  44.3 1.0 %place.1.in_ref = f32[8,528,128]{2,1,0:T(8,128)S(1)} custom-call(bf16[1056,128]{1,0:T(8,128)(2,1)S(1)} %get-tuple-element.22.refs_0_.refs_2_, bf16[1056,128]{1,0:T(8,128)(2,1)S(1)} %collective-permute-done.2.refs_1_.refs_2_, bf16[1056,128]{1,0:T(8,128)(2,1)S(1)} %collective-permute-done.3.refs_2_.refs_3_, ...), custom_call_target="tpu_custom_call" | custom-call | flops 1 | bytes 1 | tf_op jit(solution)/shard_map/place/pallas_call | solution.py:390
  45.3 5.9 %collective-permute-done.9.refs_0_ = s16[1056,128]{1,0:T(8,128)(2,1)S(1)} collective-permute-done((s16[1056,128]{1,0:T(8,128)(2,1)S(1)}, s16[1056,128]{1,0:T(8,128)(2,1)S(1)}, u32[]{:S(2)}, u32[]{:S(2)}) %collective-permute-start.9) | collective-permute-done | bytes 270368 | tf_op jit(solution)/shard_map/ppermute | solution.py:389
  51.8 5.9 %collective-permute-start.12 = (s16[528,128]{1,0:T(8,128)(2,1)S(1)}, s16[528,128]{1,0:T(8,128)(2,1)S(1)}, u32[]{:S(2)}, u32[]{:S(2)}) collective-permute-start(s16[528,128]{1,0:T(8,128)(2,1)S(1)} %get-tuple-element.32), channel_id=1, source_target_pairs={{32,64},{64,32},{96,128},{128,96},{160,192},{192,160},{224,0},{0,2... | collective-permute-start | bytes 405512 | tf_op jit(solution)/shard_map/ppermute | solution.py:399
  57.7 3.4 %collective-permute-start.11 = (s16[528,128]{1,0:T(8,128)(2,1)S(1)}, s16[528,128]{1,0:T(8,128)(2,1)S(1)}, u32[]{:S(2)}, u32[]{:S(2)}) collective-permute-start(s16[528,128]{1,0:T(8,128)(2,1)S(1)} %get-tuple-element.31), channel_id=1, source_target_pairs={{0,128},{32,160},{64,192},{96,224},{128,0},{160,32},{192,64},{224,... | collective-permute-start | bytes 405512 | tf_op jit(solution)/shard_map/ppermute | solution.py:396
  61.5 4.4 %collective-permute-done.15.refs_1_ = s16[528,128]{1,0:T(8,128)(2,1)S(1)} collective-permute-done((s16[528,128]{1,0:T(8,128)(2,1)S(1)}, s16[528,128]{1,0:T(8,128)(2,1)S(1)}, u32[]{:S(2)}, u32[]{:S(2)}) %collective-permute-start.15) | collective-permute-done | bytes 135200 | tf_op jit(solution)/shard_map/ppermute | solution.py:399
  66.2 3.2 %collective-permute-done.11.far_ref = s16[528,128]{1,0:T(8,128)(2,1)S(1)} collective-permute-done((s16[528,128]{1,0:T(8,128)(2,1)S(1)}, s16[528,128]{1,0:T(8,128)(2,1)S(1)}, u32[]{:S(2)}, u32[]{:S(2)}) %collective-permute-start.11) | collective-permute-done | bytes 135200 | tf_op jit(solution)/shard_map/ppermute | solution.py:396
  69.5 1.5 %collective-permute-done.13.refs_1_ = s16[528,128]{1,0:T(8,128)(2,1)S(1)} collective-permute-done((s16[528,128]{1,0:T(8,128)(2,1)S(1)}, s16[528,128]{1,0:T(8,128)(2,1)S(1)}, u32[]{:S(2)}, u32[]{:S(2)}) %collective-permute-start.13) | collective-permute-done | bytes 135200 | tf_op jit(solution)/shard_map/ppermute | solution.py:399
  71.1 1.5 %collective-permute-start.14 = (s16[528,128]{1,0:T(8,128)(2,1)S(1)}, s16[528,128]{1,0:T(8,128)(2,1)S(1)}, u32[]{:S(2)}, u32[]{:S(2)}) collective-permute-start(s16[528,128]{1,0:T(8,128)(2,1)S(1)} %two_1.1), channel_id=1, source_target_pairs={{32,64},{64,32},{96,128},{128,96},{160,192},{192,160},{224,0},{0,2... | collective-permute-start | bytes 405512 | tf_op jit(solution)/shard_map/ppermute | solution.py:399
  72.8 1.1 %collective-permute-start.17 = (s16[528,128]{1,0:T(8,128)(2,1)S(1)}, s16[528,128]{1,0:T(8,128)(2,1)S(1)}, u32[]{:S(2)}, u32[]{:S(2)}) collective-permute-start(s16[528,128]{1,0:T(8,128)(2,1)S(1)} %one_1.1), channel_id=1, source_target_pairs={{0,32},{32,0},{64,96},{96,64},{128,160},{160,128},{192,224},{224,1... | collective-permute-start | bytes 405512 | tf_op jit(solution)/shard_map/ppermute | solution.py:399
  73.9 3.5 %collective-permute-done.14.refs_0_ = s16[528,128]{1,0:T(8,128)(2,1)S(1)} collective-permute-done((s16[528,128]{1,0:T(8,128)(2,1)S(1)}, s16[528,128]{1,0:T(8,128)(2,1)S(1)}, u32[]{:S(2)}, u32[]{:S(2)}) %collective-permute-start.14) | collective-permute-done | bytes 135200 | tf_op jit(solution)/shard_map/ppermute | solution.py:399
  (35 shorter events, 8.2 us)
Async XLA Ops:
  1.6 9.2 %collective-permute-start.1 = (bf16[16,4096]{1,0:T(8,128)(2,1)S(1)}, bf16[16,4096]{1,0:T(8,128)(2,1)S(1)}, u32[]{:S(2)}, u32[]{:S(2)}) collective-permute-start(bf16[16,4096]{1,0:T(8,128)(2,1)S(1)} %get-tuple-element.34), channel_id=1, source_target_pairs={{1,2},{2,1},{3,4},{4,3},{5,6},{6,5},{7,8},{8,7},{9,10},{10,9},{11,... | collective-permute-start | bytes 393224 | tf_op jit(solution)/shard_map/ppermute | solution.py:326
  6.2 5.1 %collective-permute-start = (bf16[16,4096]{1,0:T(8,128)(2,1)S(1)}, bf16[16,4096]{1,0:T(8,128)(2,1)S(1)}, u32[]{:S(2)}, u32[]{:S(2)}) collective-permute-start(bf16[16,4096]{1,0:T(8,128)(2,1)S(1)} %get-tuple-element.35), channel_id=1, source_target_pairs={{0,1},{1,0},{2,3},{3,2},{4,5},{5,4},{6,7},{7,6},{8,9},{9,8},{10,11... | collective-permute-start | bytes 393224 | tf_op jit(solution)/shard_map/ppermute | solution.py:327
  11.2 1.3 %copy-start = (bf16[9,128,144]{2,1,0:T(8,128)(2,1)S(1)}, bf16[9,128,144]{2,1,0:T(8,128)(2,1)}, u32[]{:S(2)}) copy-start(bf16[9,128,144]{2,1,0:T(8,128)(2,1)} %constant.20.clone.refs_4_) | copy-start | bytes 995332
  11.2 1.3 %copy-start.1 = (bf16[8,256,128]{2,1,0:T(8,128)(2,1)S(1)}, bf16[8,256,128]{2,1,0:T(8,128)(2,1)}, u32[]{:S(2)}) copy-start(bf16[8,256,128]{2,1,0:T(8,128)(2,1)} %constant.21.clone.refs_5_) | copy-start | bytes 1572868
  11.2 1.3 %copy-start.2 = (s32[1,2,32]{2,1,0:T(2,128)S(1)}, s32[1,2,32]{2,1,0:T(2,128)}, u32[]{:S(2)}) copy-start(s32[1,2,32]{2,1,0:T(2,128)} %refs_1_.3) | copy-start | bytes 772
  11.3 1.4 %copy-start.3 = (s32[1,2,2,32]{3,2,1,0:T(2,128)S(1)}, s32[1,2,2,32]{3,2,1,0:T(2,128)}, u32[]{:S(2)}) copy-start(s32[1,2,2,32]{3,2,1,0:T(2,128)} %refs_2_.3) | copy-start | bytes 1540
  14.0 11.0 %collective-permute-start.3 = (bf16[1056,128]{1,0:T(8,128)(2,1)S(1)}, bf16[1056,128]{1,0:T(8,128)(2,1)S(1)}, u32[]{:S(2)}, u32[]{:S(2)}) collective-permute-start(bf16[1056,128]{1,0:T(8,128)(2,1)S(1)} %get-tuple-element.24), channel_id=1, source_target_pairs={{0,2},{1,3},{2,0},{3,1},{16,18},{17,19},{18,16},{19,17},{4,6},{5,7... | collective-permute-start | bytes 811016 | tf_op jit(solution)/shard_map/ppermute | solution.py:370
  15.9 12.8 %collective-permute-start.7 = (bf16[1056,128]{1,0:T(8,128)(2,1)S(1)}, bf16[1056,128]{1,0:T(8,128)(2,1)S(1)}, u32[]{:S(2)}, u32[]{:S(2)}) collective-permute-start(bf16[1056,128]{1,0:T(8,128)(2,1)S(1)} %get-tuple-element.28), channel_id=1, source_target_pairs={{0,18},{1,19},{2,16},{3,17},{16,2},{17,3},{18,0},{19,1},{4,22},{5,... | collective-permute-start | bytes 811016 | tf_op jit(solution)/shard_map/ppermute | solution.py:370
  18.4 17.1 %collective-permute-start.2 = (bf16[1056,128]{1,0:T(8,128)(2,1)S(1)}, bf16[1056,128]{1,0:T(8,128)(2,1)S(1)}, u32[]{:S(2)}, u32[]{:S(2)}) collective-permute-start(bf16[1056,128]{1,0:T(8,128)(2,1)S(1)} %get-tuple-element.23), channel_id=1, source_target_pairs={{0,1},{1,2},{2,3},{3,0},{16,17},{17,18},{18,19},{19,16},{4,5},{5,6... | collective-permute-start | bytes 811016 | tf_op jit(solution)/shard_map/ppermute | solution.py:370
  19.9 12.7 %collective-permute-start.5 = (bf16[1056,128]{1,0:T(8,128)(2,1)S(1)}, bf16[1056,128]{1,0:T(8,128)(2,1)S(1)}, u32[]{:S(2)}, u32[]{:S(2)}) collective-permute-start(bf16[1056,128]{1,0:T(8,128)(2,1)S(1)} %get-tuple-element.26), channel_id=1, source_target_pairs={{0,16},{1,17},{2,18},{3,19},{16,0},{17,1},{18,2},{19,3},{4,20},{5,... | collective-permute-start | bytes 811016 | tf_op jit(solution)/shard_map/ppermute | solution.py:370
  20.8 15.4 %collective-permute-start.4 = (bf16[1056,128]{1,0:T(8,128)(2,1)S(1)}, bf16[1056,128]{1,0:T(8,128)(2,1)S(1)}, u32[]{:S(2)}, u32[]{:S(2)}) collective-permute-start(bf16[1056,128]{1,0:T(8,128)(2,1)S(1)} %get-tuple-element.25), channel_id=1, source_target_pairs={{0,3},{1,0},{2,1},{3,2},{16,19},{17,16},{18,17},{19,18},{4,7},{5,4... | collective-permute-start | bytes 811016 | tf_op jit(solution)/shard_map/ppermute | solution.py:370
  25.0 15.0 %collective-permute-start.6 = (bf16[1056,128]{1,0:T(8,128)(2,1)S(1)}, bf16[1056,128]{1,0:T(8,128)(2,1)S(1)}, u32[]{:S(2)}, u32[]{:S(2)}) collective-permute-start(bf16[1056,128]{1,0:T(8,128)(2,1)S(1)} %get-tuple-element.27), channel_id=1, source_target_pairs={{0,17},{1,18},{2,19},{3,16},{16,1},{17,2},{18,3},{19,0},{4,21},{5,... | collective-permute-start | bytes 811016 | tf_op jit(solution)/shard_map/ppermute | solution.py:370
  28.7 11.4 %collective-permute-start.8 = (bf16[1056,128]{1,0:T(8,128)(2,1)S(1)}, bf16[1056,128]{1,0:T(8,128)(2,1)S(1)}, u32[]{:S(2)}, u32[]{:S(2)}) collective-permute-start(bf16[1056,128]{1,0:T(8,128)(2,1)S(1)} %get-tuple-element.29), channel_id=1, source_target_pairs={{0,19},{1,16},{2,17},{3,18},{16,3},{17,0},{18,1},{19,2},{4,23},{5,... | collective-permute-start | bytes 811016 | tf_op jit(solution)/shard_map/ppermute | solution.py:370
  33.2 12.1 %collective-permute-start.10 = (s16[1056,128]{1,0:T(8,128)(2,1)S(1)}, s16[1056,128]{1,0:T(8,128)(2,1)S(1)}, u32[]{:S(2)}, u32[]{:S(2)}) collective-permute-start(s16[1056,128]{1,0:T(8,128)(2,1)S(1)} %spill_1.1), channel_id=1, source_target_pairs={{1,5},{3,7},{5,9},{7,11},{9,13},{11,15},{4,0},{6,2},{8,4},{10,6},{... | collective-permute-start | bytes 811016 | tf_op jit(solution)/shard_map/ppermute | solution.py:389
  40.8 10.4 %collective-permute-start.9 = (s16[1056,128]{1,0:T(8,128)(2,1)S(1)}, s16[1056,128]{1,0:T(8,128)(2,1)S(1)}, u32[]{:S(2)}, u32[]{:S(2)}) collective-permute-start(s16[1056,128]{1,0:T(8,128)(2,1)S(1)} %spill_0.1), channel_id=1, source_target_pairs={{0,4},{2,6},{4,8},{6,10},{8,12},{10,14},{5,1},{7,3},{9,5},{11,7},{... | collective-permute-start | bytes 811016 | tf_op jit(solution)/shard_map/ppermute | solution.py:389
  51.8 9.4 %collective-permute-start.12 = (s16[528,128]{1,0:T(8,128)(2,1)S(1)}, s16[528,128]{1,0:T(8,128)(2,1)S(1)}, u32[]{:S(2)}, u32[]{:S(2)}) collective-permute-start(s16[528,128]{1,0:T(8,128)(2,1)S(1)} %get-tuple-element.32), channel_id=1, source_target_pairs={{32,64},{64,32},{96,128},{128,96},{160,192},{192,160},{224,0},{0,2... | collective-permute-start | bytes 405512 | tf_op jit(solution)/shard_map/ppermute | solution.py:399
  57.7 8.2 %collective-permute-start.15 = (s16[528,128]{1,0:T(8,128)(2,1)S(1)}, s16[528,128]{1,0:T(8,128)(2,1)S(1)}, u32[]{:S(2)}, u32[]{:S(2)}) collective-permute-start(s16[528,128]{1,0:T(8,128)(2,1)S(1)} %get-tuple-element.33), channel_id=1, source_target_pairs={{0,32},{32,0},{64,96},{96,64},{128,160},{160,128},{192,224},{224,1... | collective-permute-start | bytes 405512 | tf_op jit(solution)/shard_map/ppermute | solution.py:399
  57.7 11.7 %collective-permute-start.11 = (s16[528,128]{1,0:T(8,128)(2,1)S(1)}, s16[528,128]{1,0:T(8,128)(2,1)S(1)}, u32[]{:S(2)}, u32[]{:S(2)}) collective-permute-start(s16[528,128]{1,0:T(8,128)(2,1)S(1)} %get-tuple-element.31), channel_id=1, source_target_pairs={{0,128},{32,160},{64,192},{96,224},{128,0},{160,32},{192,64},{224,... | collective-permute-start | bytes 405512 | tf_op jit(solution)/shard_map/ppermute | solution.py:396
  61.3 9.6 %collective-permute-start.13 = (s16[528,128]{1,0:T(8,128)(2,1)S(1)}, s16[528,128]{1,0:T(8,128)(2,1)S(1)}, u32[]{:S(2)}, u32[]{:S(2)}) collective-permute-start(s16[528,128]{1,0:T(8,128)(2,1)S(1)} %one_2.1), channel_id=1, source_target_pairs={{0,32},{32,0},{64,96},{96,64},{128,160},{160,128},{192,224},{224,1... | collective-permute-start | bytes 405512 | tf_op jit(solution)/shard_map/ppermute | solution.py:399
  66.1 6.5 %collective-permute-start.16 = (s16[528,128]{1,0:T(8,128)(2,1)S(1)}, s16[528,128]{1,0:T(8,128)(2,1)S(1)}, u32[]{:S(2)}, u32[]{:S(2)}) collective-permute-start(s16[528,128]{1,0:T(8,128)(2,1)S(1)} %two_2.1), channel_id=1, source_target_pairs={{32,64},{64,32},{96,128},{128,96},{160,192},{192,160},{224,0},{0,2... | collective-permute-start | bytes 405512 | tf_op jit(solution)/shard_map/ppermute | solution.py:399
  71.1 6.3 %collective-permute-start.14 = (s16[528,128]{1,0:T(8,128)(2,1)S(1)}, s16[528,128]{1,0:T(8,128)(2,1)S(1)}, u32[]{:S(2)}, u32[]{:S(2)}) collective-permute-start(s16[528,128]{1,0:T(8,128)(2,1)S(1)} %two_1.1), channel_id=1, source_target_pairs={{32,64},{64,32},{96,128},{128,96},{160,192},{192,160},{224,0},{0,2... | collective-permute-start | bytes 405512 | tf_op jit(solution)/shard_map/ppermute | solution.py:399
  72.8 5.1 %collective-permute-start.17 = (s16[528,128]{1,0:T(8,128)(2,1)S(1)}, s16[528,128]{1,0:T(8,128)(2,1)S(1)}, u32[]{:S(2)}, u32[]{:S(2)}) collective-permute-start(s16[528,128]{1,0:T(8,128)(2,1)S(1)} %one_1.1), channel_id=1, source_target_pairs={{0,32},{32,0},{64,96},{96,64},{128,160},{160,128},{192,224},{224,1... | collective-permute-start | bytes 405512 | tf_op jit(solution)/shard_map/ppermute | solution.py:399
